TPU v7x, 32 devices: a whole 2x2x4 slice. The times are simulated.
32 devices in a mesh: aa: 4 (over x, core), ba: 8 (over z, y).
Axes of the slice: x: 2, y: 2, z: 4, core: 2. Of those that a mesh axis runs over, the one named last changes fastest.
Arguments:
- hidden: bfloat16 [512, 3072], P('aa'), may hold values from -24 to 24
- head_weight: bfloat16 [3072, 8, 4, 2048], P(None, 'ba'), as said below
- teacher: bfloat16 [512, 4, 8, 2048], P('ba', 'aa'), may hold values from -60 to 250
Outputs:
- divergence: float32 [], replicated
- grad_hidden: bfloat16 [512, 3072], P('aa')
- grad_head: bfloat16 [3072, 8, 4, 2048], P('aa', 'ba')
Inputs may be any that keep to these rules, and one draw needn't show every extreme that they name: `head_weight`: entries of order one over the square root of 3072.
All inputs are finite; a program needn't handle non-finite values.
Results may differ from a plain program's by a relative error of at most 0.0049.
Values may be sent and summed in bfloat16 or wider, within the bound.
No kernel may reach another device: no remote copies, remote signals or barrier semaphores. Data moves between devices by JAX's collectives and lax.ppermute only.
A program may use at most 192 MiB of HBM per device.

v0:
```python
import jax
import jax.numpy as jnp
from jax import lax
from jax.sharding import PartitionSpec as P

grad_scale = 256.0


def on_device(hidden, head_weight, teacher):
    token_rows = hidden.shape[0]
    model_width = hidden.shape[1]
    vocab_local = head_weight.shape[2] * head_weight.shape[3]
    weight_flat = head_weight.reshape(model_width, vocab_local)
    arrived = lax.all_to_all(
        lax.all_to_all(teacher, "ba", split_axis=2, concat_axis=0, tiled=True),
        "aa",
        split_axis=0,
        concat_axis=1,
        tiled=True,
    )
    target = arrived.reshape(token_rows, vocab_local).astype(jnp.float32)
    student = jnp.dot(hidden, weight_flat, preferred_element_type=jnp.float32)
    student_peak = jnp.max(student, axis=1)
    target_peak = jnp.max(target, axis=1)
    student_peak, target_peak = lax.pmax((student_peak, target_peak), "ba")
    student_total, target_total = lax.psum(
        (
            jnp.sum(jnp.exp(student - student_peak[:, None]), axis=1),
            jnp.sum(jnp.exp(target - target_peak[:, None]), axis=1),
        ),
        "ba",
    )
    log_student = student - student_peak[:, None] - jnp.log(student_total)[:, None]
    log_target = target - target_peak[:, None] - jnp.log(target_total)[:, None]
    student_prob = jnp.exp(log_student)
    target_prob = jnp.exp(log_target)
    summed = lax.psum(jnp.sum(target_prob * (log_target - log_student)), ("aa", "ba"))
    divergence = summed / (token_rows * lax.axis_size("aa"))
    gradient = (grad_scale * (student_prob - target_prob)).astype(jnp.bfloat16)
    partial_hidden = lax.dot_general(
        gradient, weight_flat, (((1,), (1,)), ((), ())), preferred_element_type=jnp.float32
    )
    grad_hidden = lax.psum(partial_hidden, "ba").astype(jnp.bfloat16)
    share_rows = model_width // lax.axis_size("aa")
    column_part = lax.all_to_all(hidden, "aa", split_axis=1, concat_axis=0, tiled=True)
    grad_flat = lax.dot_general(
        column_part,
        lax.all_gather(gradient, "aa", axis=0, tiled=True),
        (((0,), (0,)), ((), ())),
        preferred_element_type=jnp.float32,
    )
    grad_head = grad_flat.astype(jnp.bfloat16).reshape(
        share_rows, 1, head_weight.shape[2], head_weight.shape[3]
    )
    return (divergence, grad_hidden, grad_head)


def solution(mesh):
    placed = (P("aa", None), P(None, "ba", None, None), P("ba", "aa", None, None))
    return jax.shard_map(
        on_device,
        mesh=mesh,
        in_specs=placed,
        out_specs=(P(), P("aa", None), P("aa", "ba", None, None)),
        check_vma=False,
    )
```

profile of v0, /device:TPU:0, one launch (start us, length us, event | category | flops | bytes accessed | tf_op | source)
XLA Modules:
  0.0 389.4 jit_solution(4361720211098920409)
XLA Ops:
  7.2 4.1 %copy.22 = bf16[64,1,8,2048]{3,0,1,2:T(8,128)(2,1)} copy(bf16[64,1,8,2048]{3,2,1,0:T(8,128)(2,1)} %param.5) | data formatting | bytes 4194304 | tf_op args[2]
  11.2 7.3 %all-to-all-start = ((bf16[64,1,8,2048]{3,0,1,2:T(8,128)(2,1)}), bf16[64,1,8,2048]{3,0,1,2:T(8,128)(2,1)S(1)}, u32[]{:S(2)}, u32[]{:S(2)}) async-start(bf16[64,1,8,2048]{3,0,1,2:T(8,128)(2,1)} %copy.22), calls=%async_computation | async-start | bytes 4194304 | tf_op jit(solution)/shard_map/all_to_all | solution.py:15
  18.5 43.6 %copy.30 = bf16[384,8,4,2048]{3,1,2,0:T(8,128)(2,1)} copy(bf16[384,8,4,2048]{3,2,1,0:T(4,128)(2,1)} %bitcast.33) | data formatting | bytes 100663296
  62.1 4.6 %all-to-all-done = bf16[64,1,8,2048]{3,0,1,2:T(8,128)(2,1)S(1)} async-done(((bf16[64,1,8,2048]{3,0,1,2:T(8,128)(2,1)}), bf16[64,1,8,2048]{3,0,1,2:T(8,128)(2,1)S(1)}, u32[]{:S(2)}, u32[]{:S(2)}) %all-to-all-start) | async-done | bytes 2097184 | tf_op jit(solution)/shard_map/all_to_all | solution.py:15
  67.3 2.9 reduce.7
  70.2 4.6 %reshape.37 = bf16[4,2,131072]{2,1,0:T(2,128)(2,1)} reshape(bf16[512,2048]{1,0:T(8,128)(2,1)} %reduce.7) | data formatting | bytes 4194304
  74.8 3.6 all-to-all-start.1
  78.4 20.9 %fusion.2 = (f32[128]{0:T(128)S(1)}, f32[128,8192]{1,0:T(8,128)}) fusion(bf16[128,3072]{1,0:T(8,128)(2,1)S(1)} %copy-done.1, bf16[3072,8192]{1,0:T(8,128)(2,1)} %bitcast.31), kind=kOutput, calls=%fused_computation.10 | convolution fusion | flops 6443499520 | bytes 55312896 | tf_op jit(solution)/shard_map/dot_general | solution.py:22
  99.3 4.7 %all-to-all-done.1 = bf16[4,2,131072]{2,1,0:T(2,128)(2,1)S(1)} async-done(((bf16[4,2,131072]{2,1,0:T(2,128)(2,1)}), bf16[4,2,131072]{2,1,0:T(2,128)(2,1)S(1)}, u32[]{:S(2)}, u32[]{:S(2)}) %all-to-all-start.1) | async-done | bytes 2097184 | tf_op jit(solution)/shard_map/all_to_all | solution.py:14
  104.0 3.3 reshape.38
  107.3 6.3 %convert_bitcast_fusion = (f32[128,4,1,1,2048]{4,0,1,3,2:T(8,128)}, bf16[512,1,1,2048]{3,0,2,1:T(8,128)(2,1)S(1)}) fusion(bf16[512,1,1,2048]{3,2,1,0:T(2,128)(2,1)} %reshape.38), kind=kLoop, calls=%fused_computation.2 | loop fusion | flops 1048576 | bytes 8388608 | tf_op jit(solution)/shard_map/convert_element_type | solution.py:21
  113.6 6.0 %reduce_max.30 = bf16[512]{0:T(512)(128)(2,1)S(1)} reduce(bf16[512,1,1,2048]{3,2,1,0:T(2,128)(2,1)} %reshape.38, bf16[]{:T(256)} %constant.2.clone.1), dimensions={1,2,3}, to_apply=%region_0.0 | reduce | flops 1048064 | bytes 2098178 | tf_op jit(solution)/shard_map/reduce_max | solution.py:24
  119.6 4.9 %copy.25 = f32[128,4,1,1,2048]{4,1,0,3,2:T(4,128)S(1)} copy(f32[128,4,1,1,2048]{4,0,1,3,2:T(8,128)} %get-tuple-element.22) | data formatting | bytes 8388608 | tf_op jit(solution)/shard_map/convert_element_type | solution.py:21
  124.5 5.5 %copy.29 = f32[16,8,4,2048]{3,1,2,0:T(8,128)} copy(f32[16,8,4,2048]{3,2,1,0:T(4,128)S(1)} %bitcast.35) | data formatting | bytes 8388608
  130.0 19.7 %all-reduce.1 = (f32[128]{0:T(128)S(1)}, f32[128]{0:T(128)S(1)}) all-reduce(f32[128]{0:T(128)S(1)} %get-tuple-element.26, bf16[128]{0:T(256)(128)(2,1)S(1)} %bitcast_reduce_fusion), channel_id=1, replica_groups=mesh['aa'=4,'ba'=8] {'ba'}, use_global_device_ids=true, to_apply=%region_6.0 | all-reduce | flops 256 | bytes 1792 | tf_op jit(solution)/shard_map/pmax | solution.py:25
  150.6 2.9 exponential_reduce_fusion
  153.5 17.1 %all-reduce = (f32[128]{0:T(128)S(1)}, f32[128]{0:T(128)S(1)}) all-reduce(f32[128]{0:T(128)S(1)} %exponential_reduce_fusion, f32[128]{0:T(128)S(1)} %fusion.1), channel_id=1, replica_groups=mesh['aa'=4,'ba'=8] {'ba'}, use_global_device_ids=true, to_apply=%region_8.0 | all-reduce | flops 256 | bytes 2048 | tf_op jit(solution)/shard_map/psum | solution.py:26
  170.6 6.2 %multiply_convert_fusion = (bf16[128,8192]{1,0:T(8,128)(2,1)}, f32[]{:T(128)}) fusion(f32[128,8192]{1,0:T(8,128)} %bitcast.34, f32[128,8192]{1,0:T(8,128)} %get-tuple-element.27, f32[128]{0:T(128)S(1)} %log.7, f32[128]{0:T(128)S(1)} %get-tuple-element.20, f32[128]{0:T(128)S(1)} %log.6, f32[128]{0:T(128)S(1)} %get-tuple-element.21), kind=kLoop, calls=%fused_computation.5 | loop fusion | flops 10485759 | bytes 10487812 | tf_op jit(solution)/shard_map/convert_element_type | solution.py:39
  178.0 22.4 %all_to_all.46 = bf16[128,4,768]{0,2,1:T(8,128)(2,1)S(1)} all-to-all(bf16[128,4,768]{0,2,1:T(8,128)(2,1)} %bitcast.40), channel_id=1, replica_groups=mesh['aa'=4,'ba'=8] {'aa'}, dimensions={1} | all-to-all | bytes 1572864 | tf_op jit(solution)/shard_map/all_to_all | solution.py:45
  201.6 38.2 %psum.30 = f32[]{:T(128)} all-reduce(f32[]{:T(128)} %get-tuple-element.25), channel_id=1, replica_groups=mesh['aa'=4,'ba'=8] {'aa','ba'}, use_global_device_ids=true, to_apply=%region_10.0 | all-reduce | flops 1 | bytes 8 | tf_op jit(solution)/shard_map/psum | solution.py:37
  239.8 23.3 %fusion.3 = f32[128,3072]{1,0:T(8,128)} fusion(bf16[128,8192]{1,0:T(8,128)(2,1)S(1)} %copy-done, bf16[3072,8192]{1,0:T(8,128)(2,1)} %bitcast.32), kind=kOutput, calls=%fused_computation.11 | convolution fusion | flops 6442450944 | bytes 54001664 | tf_op jit(solution)/shard_map/dot_general | solution.py:40
  263.8 83.1 %all-reduce.3 = bf16[128,3072]{1,0:T(8,128)(2,1)} all-reduce(f32[128,3072]{1,0:T(8,128)} %fusion.3), channel_id=1, replica_groups=mesh['aa'=4,'ba'=8] {'ba'}, use_global_device_ids=true, to_apply=%region_11.12 | all-reduce | flops 393216 | bytes 2359296 | tf_op jit(solution)/shard_map/psum | solution.py:43
  346.9 12.9 %convolution_convert_fusion = bf16[8192,768]{1,0:T(8,128)(2,1)} fusion(bf16[512,8192]{1,0:T(8,128)(2,1)} %all-gather.2.cloned.1.call-done, bf16[512,768]{1,0:T(8,128)(2,1)S(1)} %bitcast.41), kind=kOutput, calls=%fused_computation | convolution fusion | flops 6448742400 | bytes 21757952 | tf_op jit(solution)/shard_map/dot_general | solution.py:46
  359.8 21.6 %copy.28 = bf16[768,1,4,2048]{3,2,1,0:T(4,128)(2,1)} copy(bf16[768,1,4,2048]{0,3,2,1:T(8,128)(2,1)} %bitcast.36) | data formatting | bytes 25165824
  (16 shorter events, 3.8 us)
Async XLA Ops:
  11.2 55.5 %all-to-all-start = ((bf16[64,1,8,2048]{3,0,1,2:T(8,128)(2,1)}), bf16[64,1,8,2048]{3,0,1,2:T(8,128)(2,1)S(1)}, u32[]{:S(2)}, u32[]{:S(2)}) async-start(bf16[64,1,8,2048]{3,0,1,2:T(8,128)(2,1)} %copy.22), calls=%async_computation | async-start | bytes 4194304 | tf_op jit(solution)/shard_map/all_to_all | solution.py:15
  70.2 8.2 %copy-start.1 = (bf16[128,3072]{1,0:T(8,128)(2,1)S(1)}, bf16[128,3072]{1,0:T(8,128)(2,1)}, u32[]{:S(2)}) copy-start(bf16[128,3072]{1,0:T(8,128)(2,1)} %param.3) | copy-start | bytes 2359300
  74.8 29.3 %all-to-all-start.1 = ((bf16[4,2,131072]{2,1,0:T(2,128)(2,1)}), bf16[4,2,131072]{2,1,0:T(2,128)(2,1)S(1)}, u32[]{:S(2)}, u32[]{:S(2)}) async-start(bf16[4,2,131072]{2,1,0:T(2,128)(2,1)} %reshape.37), calls=%async_computation.1 | async-start | bytes 4194304 | tf_op jit(solution)/shard_map/all_to_all | solution.py:14
  78.4 268.5 %all-gather.2.cloned.1.call-start = ((), (), s32[]{:S(2)}) async-start(), calls=%async_computation.3 | async-start | bytes 10485760 | tf_op jit(solution)/shard_map/all_gather | solution.py:48
  176.8 63.0 %copy-start = (bf16[128,8192]{1,0:T(8,128)(2,1)S(1)}, bf16[128,8192]{1,0:T(8,128)(2,1)}, u32[]{:S(2)}) copy-start(bf16[128,8192]{1,0:T(8,128)(2,1)} %get-tuple-element.24) | copy-start | bytes 6291460
  239.8 107.1 %copy-start.2 = (bf16[4,128,768]{2,1,0:T(8,128)(2,1)S(1)}, bf16[4,128,768]{2,1,0:T(8,128)(2,1)}, u32[]{:S(2)}) copy-start(bf16[4,128,768]{2,1,0:T(8,128)(2,1)} %copy.27) | copy-start | bytes 2359300
Sparse Core Ops, SparseCore 0:
  177.0 64.2 all-gather.1
where the time goes:
time: 391 us; the launch traced here: 389 us
  blocking collectives  181 us (46%)
  local copies, waits for them, and re-layouts  90.4 us (23%)
  matrix products  57.1 us (15%)
  other arithmetic  25.2 us (6%)
  between operations  15.9 us (4%)
  starting transfers between devices  10.9 us (3%)
  waiting for transfers between devices  9.35 us (2%)
    unnamed x13, local copies, waits for them, and re-layouts  83.8 us
    psum x1, blocking collectives, on_device(): grad_hidden = lax.psum(partial_hidden, 'ba').astype(jnp.bfloat16)  83.1 us
    psum x1, blocking collectives, on_device(): lax.psum(jnp.sum(target_prob * (log_target - log_student)), ('aa', 'ba'))  38.2 us
    dot_general x1, matrix products, on_device(): lax.dot_general(gradient, weight_flat, (((1,), (1,)), ((), ())), preferre...  23.3 us
    all_to_all x1, blocking collectives, on_device(): lax.all_to_all(hidden, 'aa', split_axis=1, concat_axis=0, tiled=True)  22.4 us
    dot_general x1, matrix products, on_device(): student = jnp.dot(hidden, weight_flat, preferred_element_type=jnp.float32)  20.9 us
    pmax x1, blocking collectives, on_device(): student_peak, target_peak = lax.pmax((student_peak, target_peak), 'ba')  19.7 us
    psum x1, blocking collectives, on_device(): lax.psum((jnp.sum(jnp.exp(student - student_peak[:, None]), axis=1), jnp....  17.1 us
  transfers between devices with their start and end apart: 3, of which 2 were waited for; matrix products, arithmetic and copies ran while one was open for 23% of the time, Pallas kernels for 0%

commit v1 on v0

v1 whole, which is shorter than its diff:
```python
import functools

import jax
import jax.numpy as jnp
from jax import lax
from jax.experimental import pallas as pl
from jax.experimental.pallas import tpu as pltpu
from jax.sharding import PartitionSpec as P

grad_scale = 256.0
lanes = 128
f32 = jnp.float32
bf16 = jnp.bfloat16
anywhere = pl.BlockSpec(memory_space=pl.ANY)
whole_vmem = pl.BlockSpec(memory_space=pltpu.VMEM)


def limits(mib):
    return pltpu.CompilerParams(vmem_limit_bytes=mib << 20)


def largest_tile(size, most, step):
    tile = min(size, most)
    while size % tile or tile % step:
        tile -= step
    return tile


def exchange(value, axis, mask):
    count = lax.axis_size(axis)
    return lax.ppermute(value, axis, [(i, i ^ mask) for i in range(count)])


def across(column, rows):
    del rows
    return jnp.transpose(jnp.broadcast_to(column, (lanes, column.shape[1])))


def split_teacher(teacher):
    tokens, _, owners, piece = teacher.shape
    cols = largest_tile(piece, 512, lanes)

    def kernel(in_ref, *refs):
        outs, stat_ref, peak_ref, total_ref = refs[:owners], refs[owners], refs[-2], refs[-1]
        step = pl.program_id(0)
        me = lax.axis_index("ba")
        flat = in_ref[:, 0].reshape(tokens * owners, cols)
        row = lax.broadcasted_iota(jnp.int32, (tokens * owners, tokens * owners), 0)
        col = lax.broadcasted_iota(jnp.int32, (tokens * owners, tokens * owners), 1)
        source = (row % tokens) * owners + ((row // tokens) ^ me)
        pick = (col == source).astype(f32).astype(bf16)
        moved = jnp.dot(pick, flat, preferred_element_type=f32)
        for s in range(owners):
            outs[s][...] = moved[s * tokens : (s + 1) * tokens].astype(bf16)
        parts = [
            moved[s * tokens : (s + 1) * tokens, k : k + lanes]
            for s in range(owners)
            for k in range(0, cols, lanes)
        ]
        peak = functools.reduce(jnp.maximum, parts)

        @pl.when(step == 0)
        def _():
            peak_ref[...] = peak
            total_ref[...] = jnp.zeros_like(total_ref)

        old = peak_ref[...]
        new = jnp.maximum(old, peak)
        total = total_ref[...] * jnp.exp(old - new)
        for part in parts:
            total = total + jnp.exp(part - new)
        peak_ref[...] = new
        total_ref[...] = total

        @pl.when(step == pl.num_programs(0) - 1)
        def _():
            top = jnp.max(new, axis=1, keepdims=True)
            summed = jnp.sum(total * jnp.exp(new - top), axis=1, keepdims=True)
            stat_ref[0:1, :] = jnp.transpose(jnp.broadcast_to(top, (tokens, lanes)))[0:1]
            stat_ref[1:2, :] = jnp.transpose(jnp.broadcast_to(summed, (tokens, lanes)))[0:1]
            stat_ref[2:8, :] = jnp.zeros((6, tokens), f32)

    return pl.pallas_call(
        kernel,
        grid=(piece // cols,),
        in_specs=[pl.BlockSpec((tokens, 1, owners, cols), lambda r: (0, 0, 0, r))],
        out_specs=[pl.BlockSpec((tokens, cols), lambda r: (0, r))] * owners
        + [pl.BlockSpec((8, tokens), lambda r: (0, 0))],
        out_shape=[jax.ShapeDtypeStruct((tokens, piece), bf16)] * owners
        + [jax.ShapeDtypeStruct((8, tokens), f32)],
        scratch_shapes=[pltpu.VMEM((tokens, lanes), f32)] * 2,
        compiler_params=limits(40),
        name="split_teacher",
    )(teacher)


def take_pair(head_weight):
    width, _, _, piece = head_weight.shape
    rows = largest_tile(width, 256, lanes)
    steps = width // rows

    def kernel(w_ref, out_ref, taken, ready, in_sem, out_sem):
        core = lax.axis_index("aa") % 2
        row = lax.broadcasted_iota(jnp.int32, (2 * lanes, 2 * lanes), 0)
        col = lax.broadcasted_iota(jnp.int32, (2 * lanes, 2 * lanes), 1)
        pick = (col == (row % lanes) * 2 + row // lanes).astype(f32).astype(bf16)

        def fetch(i, slot):
            at = pl.ds(pl.multiple_of(i * rows, rows), rows)
            return pltpu.make_async_copy(
                w_ref.at[at, 0, pl.ds(2 * core, 2), :], taken.at[slot], in_sem.at[slot]
            )

        def store(i, slot):
            at = pl.ds(pl.multiple_of(i * rows, rows), rows)
            return pltpu.make_async_copy(ready.at[slot], out_ref.at[:, at, :], out_sem.at[slot])

        fetch(0, 0).start()

        def body(i, carry):
            slot = lax.rem(i, 2)

            @pl.when(i + 1 < steps)
            def _():
                fetch(i + 1, 1 - slot).start()

            fetch(i, slot).wait()

            @pl.when(i >= 2)
            def _():
                store(i - 2, slot).wait()

            for q in range(0, rows, lanes):
                block = taken[slot, q : q + lanes].reshape(2 * lanes, piece)
                moved = jnp.dot(pick, block, preferred_element_type=f32).astype(bf16)
                ready[slot, 0, q : q + lanes] = moved[:lanes]
                ready[slot, 1, q : q + lanes] = moved[lanes:]
            store(i, slot).start()
            return carry

        lax.fori_loop(0, steps, body, 0)
        for i in range(max(0, steps - 2), steps):
            store(i, i % 2).wait()

    return pl.pallas_call(
        kernel,
        in_specs=[anywhere],
        out_specs=anywhere,
        out_shape=jax.ShapeDtypeStruct((2, width, piece), bf16),
        scratch_shapes=[
            pltpu.VMEM((2, rows, 2, piece), bf16),
            pltpu.VMEM((2, 2, rows, piece), bf16),
            pltpu.SemaphoreType.DMA((2,)),
            pltpu.SemaphoreType.DMA((2,)),
        ],
        compiler_params=limits(32),
        cost_estimate=pl.CostEstimate(
            flops=4 * lanes * 2 * width * piece, bytes_accessed=8 * width * piece, transcendentals=0
        ),
        name="take_pair",
    )(head_weight)


def student_logits(hiddens, pair):
    rows, width = hiddens[0].shape
    blocks = len(hiddens)
    tokens = rows * blocks
    piece = pair.shape[2]
    cols = largest_tile(piece, 512, lanes)

    def kernel(*refs):
        given, w_ref = refs[:blocks], refs[blocks]
        out_ref, stat_ref, left, peak_ref, total_ref, sem = refs[blocks + 1 :]
        first = (pl.program_id(0) == 0) & (pl.program_id(1) == 0)
        last = (pl.program_id(0) == 1) & (pl.program_id(1) == pl.num_programs(1) - 1)
        me = lax.axis_index("aa")

        @pl.when(first)
        def _():
            def place(q):
                at = pl.ds(pl.multiple_of((me ^ q) * rows, rows), rows)
                return pltpu.make_async_copy(given[q], left.at[at], sem.at[q])

            for q in range(blocks):
                place(q).start()
            peak_ref[...] = jnp.full_like(peak_ref, -jnp.inf)
            total_ref[...] = jnp.zeros_like(total_ref)
            for q in range(blocks):
                place(q).wait()

        out_ref[0] = jnp.dot(left[...], w_ref[0], preferred_element_type=f32)

        @pl.loop(0, tokens // 64)
        def _(k):
            at = pl.ds(pl.multiple_of(k * 64, 64), 64)
            parts = [out_ref[0, at, j : j + lanes] for j in range(0, cols, lanes)]
            old = peak_ref[at]
            new = functools.reduce(jnp.maximum, parts, old)
            total = total_ref[at] * jnp.exp(old - new)
            for part in parts:
                total = total + jnp.exp(part - new)
            peak_ref[at] = new
            total_ref[at] = total

        @pl.when(last)
        def _():
            peak = peak_ref[...]
            top = jnp.max(peak, axis=1, keepdims=True)
            summed = jnp.sum(total_ref[...] * jnp.exp(peak - top), axis=1, keepdims=True)
            stat_ref[0:1, :] = jnp.transpose(jnp.broadcast_to(top, (tokens, lanes)))[0:1]
            stat_ref[1:2, :] = jnp.transpose(jnp.broadcast_to(summed, (tokens, lanes)))[0:1]
            stat_ref[2:8, :] = jnp.zeros((6, tokens), f32)

    return pl.pallas_call(
        kernel,
        grid=(2, piece // cols),
        in_specs=[anywhere] * blocks + [pl.BlockSpec((1, width, cols), lambda i, r: (i, 0, r))],
        out_specs=[
            pl.BlockSpec((1, tokens, cols), lambda i, r: (i, 0, r)),
            pl.BlockSpec((8, tokens), lambda i, r: (0, 0)),
        ],
        out_shape=[
            jax.ShapeDtypeStruct((2, tokens, piece), f32),
            jax.ShapeDtypeStruct((8, tokens), f32),
        ],
        scratch_shapes=[
            pltpu.VMEM((tokens, width), bf16),
            pltpu.VMEM((tokens, lanes), f32),
            pltpu.VMEM((tokens, lanes), f32),
            pltpu.SemaphoreType.DMA((blocks,)),
        ],
        compiler_params=limits(40),
        cost_estimate=pl.CostEstimate(
            flops=4 * tokens * width * piece, bytes_accessed=4 * width * piece, transcendentals=0
        ),
        name="student_logits",
    )(*hiddens, pair)


def merge(stats):
    peak = functools.reduce(jnp.maximum, [s[0:1] for s in stats])
    total = sum(s[1:2] * jnp.exp(s[0:1] - peak) for s in stats)
    return peak, total


def pack_stats(student_stats, teacher_stats):
    tokens = student_stats[0].shape[1]
    few = teacher_stats[0].shape[1]
    count = len(student_stats)

    def kernel(*refs):
        out_ref = refs[-1]
        peak, total = merge([r[...] for r in refs[:count]])
        out_ref[0:1, :] = peak
        out_ref[1:2, :] = total
        out_ref[2:8, :] = jnp.zeros((6, tokens), f32)
        peak, total = merge([r[...] for r in refs[count:-1]])
        out_ref[2:3, 0:few] = peak + jnp.log(total)

    return pl.pallas_call(
        kernel,
        in_specs=[whole_vmem] * (count + len(teacher_stats)),
        out_specs=whole_vmem,
        out_shape=jax.ShapeDtypeStruct((8, tokens), f32),
        name="pack_stats",
    )(*student_stats, *teacher_stats)


def all_log_sums(packed, few):
    count = len(packed)
    tokens = packed[0].shape[1]

    def kernel(*refs):
        student_ref, teacher_ref = refs[count:]
        me = lax.axis_index("ba")
        peak, total = merge([r[...] for r in refs[:count]])
        student_ref[...] = across(peak + jnp.log(total), tokens)
        for s in range(count):
            at = pl.ds(pl.multiple_of((me ^ s) * few, few), few)
            wide = jnp.broadcast_to(refs[s][2:3, 0:lanes], (lanes, lanes))
            teacher_ref[at, :] = jnp.transpose(wide)[0:few]

    return pl.pallas_call(
        kernel,
        in_specs=[whole_vmem] * count,
        out_specs=[whole_vmem] * 2,
        out_shape=[jax.ShapeDtypeStruct((tokens, lanes), f32)] * 2,
        name="all_log_sums",
    )(*packed)


def logit_gradient(order, own, met, student, student_sum, teacher_sum):
    count = order.shape[0] - 1
    _, tokens, piece = student.shape
    few = own.shape[0] // count
    cols = largest_tile(piece, 512, lanes)
    rows = 16
    half = tokens // 2

    def kernel(order_ref, own_ref, met_ref, s_ref, ssum_ref, tsum_ref, g_ref, div_ref):
        step = pl.program_id(0)
        x = order_ref[count]

        @pl.when(step == 0)
        def _():
            div_ref[...] = jnp.zeros_like(div_ref)

        mine = (order_ref[step] * few) // half == x
        counted = jnp.where(mine, 1.0, 0.0)

        @pl.loop(0, few // rows)
        def _(k):
            at = pl.ds(pl.multiple_of(k * rows, rows), rows)
            ssum = ssum_ref[at]
            tsum = tsum_ref[at]
            ssum = jnp.concatenate([ssum] * (cols // lanes), axis=1)
            tsum = jnp.concatenate([tsum] * (cols // lanes), axis=1)
            found = jnp.zeros((8, lanes), f32)
            for which, t_ref in ((x, own_ref), (1 - x, met_ref)):
                for j in range(0, piece, cols):
                    log_s = s_ref[which, at, j : j + cols] - ssum
                    log_t = t_ref[at, j : j + cols].astype(f32) - tsum
                    prob_t = jnp.exp(log_t)
                    g_ref[which, at, j : j + cols] = (
                        grad_scale * (jnp.exp(log_s) - prob_t)
                    ).astype(bf16)
                    part = prob_t * (log_t - log_s)
                    for m in range(0, rows, 8):
                        for n in range(0, cols, lanes):
                            found = found + part[m : m + 8, n : n + lanes]
            div_ref[...] += counted * found

    return pl.pallas_call(
        kernel,
        grid_spec=pltpu.PrefetchScalarGridSpec(
            num_scalar_prefetch=1,
            grid=(count,),
            in_specs=[
                pl.BlockSpec((few, piece), lambda s, o: (s, 0)),
                pl.BlockSpec((few, piece), lambda s, o: (s, 0)),
                pl.BlockSpec((2, few, piece), lambda s, o: (0, o[s], 0)),
                pl.BlockSpec((few, lanes), lambda s, o: (o[s], 0)),
                pl.BlockSpec((few, lanes), lambda s, o: (o[s], 0)),
            ],
            out_specs=[
                pl.BlockSpec((2, few, piece), lambda s, o: (0, o[s], 0)),
                pl.BlockSpec((8, lanes), lambda s, o: (0, 0)),
            ],
        ),
        out_shape=[
            jax.ShapeDtypeStruct((2, tokens, piece), bf16),
            jax.ShapeDtypeStruct((8, lanes), f32),
        ],
        compiler_params=limits(32),
        name="logit_gradient",
    )(order, own, met, student, student_sum, teacher_sum)


def hidden_share(position, gradient, pair):
    _, tokens, piece = gradient.shape
    width = pair.shape[1]
    rows = tokens // lax.axis_size("aa")
    cols = largest_tile(width, 384, lanes)

    def kernel(at_ref, keep_ref, send_ref, w_ref, kept_ref, sent_ref):
        total = jnp.zeros((2 * rows, cols), f32)
        for i in range(2):
            left = jnp.concatenate([keep_ref[i], send_ref[i]], axis=0)
            total = total + lax.dot_general(
                left, w_ref[i], (((1,), (1,)), ((), ())), preferred_element_type=f32
            )
        kept_ref[...] = total[:rows]
        sent_ref[...] = total[rows:].astype(bf16)

    return pl.pallas_call(
        kernel,
        grid_spec=pltpu.PrefetchScalarGridSpec(
            num_scalar_prefetch=1,
            grid=(width // cols,),
            in_specs=[
                pl.BlockSpec((2, rows, piece), lambda d, p: (0, p[0], 0)),
                pl.BlockSpec((2, rows, piece), lambda d, p: (0, p[1], 0)),
                pl.BlockSpec((2, cols, piece), lambda d, p: (0, d, 0)),
            ],
            out_specs=[pl.BlockSpec((rows, cols), lambda d, p: (0, d))] * 2,
        ),
        out_shape=[
            jax.ShapeDtypeStruct((rows, width), f32),
            jax.ShapeDtypeStruct((rows, width), bf16),
        ],
        compiler_params=limits(32),
        cost_estimate=pl.CostEstimate(
            flops=8 * rows * width * piece, bytes_accessed=4 * width * piece, transcendentals=0
        ),
        name="hidden_share",
    )(position, gradient, gradient, pair)


def share_out(kept, arrived):
    rows, width = kept.shape
    count = lax.axis_size("ba")
    few = rows // count
    if few % 16:
        order = lax.axis_index("ba") ^ jnp.arange(count)
        summed = (kept + arrived.astype(f32)).astype(bf16).reshape(count, few, width)
        return [summed[order[s]] for s in range(count)]

    def kernel(kept_ref, arrived_ref, *outs):
        me = lax.axis_index("ba")
        for s in range(count):
            at = pl.ds(pl.multiple_of((me ^ s) * few, few), few)
            outs[s][...] = (kept_ref[at] + arrived_ref[at].astype(f32)).astype(bf16)

    return pl.pallas_call(
        kernel,
        in_specs=[whole_vmem] * 2,
        out_specs=[whole_vmem] * count,
        out_shape=[jax.ShapeDtypeStruct((few, width), bf16)] * count,
        name="share_out",
    )(kept, arrived)


def put_together(blocks):
    count = len(blocks)
    few, width = blocks[0].shape
    if few % 16:
        order = lax.axis_index("ba") ^ jnp.arange(count)
        return jnp.stack(blocks)[order].reshape(count * few, width)

    def kernel(*refs):
        me = lax.axis_index("ba")
        for s in range(count):
            at = pl.ds(pl.multiple_of((me ^ s) * few, few), few)
            refs[count][at, :] = refs[s][...]

    return pl.pallas_call(
        kernel,
        in_specs=[whole_vmem] * count,
        out_specs=whole_vmem,
        out_shape=jax.ShapeDtypeStruct((count * few, width), bf16),
        name="put_together",
    )(*blocks)


def head_pair(hiddens, gradient, other, so_far):
    rows, width = hiddens[0].shape
    blocks = len(hiddens)
    tokens = rows * blocks
    piece = gradient.shape[2]
    share = width // blocks
    cols = largest_tile(piece, 512, lanes)
    steps = piece // cols
    aliased = [] if so_far is None else [so_far]

    def kernel(*refs):
        given, g_ref = refs[:blocks], refs[blocks]
        out_ref, held, left, ready, sem, out_sem = refs[blocks + 1 + len(aliased) :]
        step = pl.program_id(0)
        slot = lax.rem(step, 2)
        me = lax.axis_index("aa")
        base = 2 * ((me % 2) ^ other)

        @pl.when(step == 0)
        def _():
            def place(q):
                at = pl.ds(pl.multiple_of((me ^ q) * rows, rows), rows)
                part = pl.ds(pl.multiple_of(me * share, share), share)
                return pltpu.make_async_copy(given[q].at[:, part], held.at[at], sem.at[q])

            for q in range(blocks):
                place(q).start()
            for q in range(blocks):
                place(q).wait()
            row = lax.broadcasted_iota(jnp.int32, (2 * lanes, lanes), 0)
            col = lax.broadcasted_iota(jnp.int32, (2 * lanes, lanes), 1)
            for i in range(2):
                spread = (row == 2 * col + i).astype(f32).astype(bf16)
                for d in range(0, share, lanes):
                    left[2 * d : 2 * (d + lanes), i * tokens : (i + 1) * tokens] = lax.dot_general(
                        spread,
                        held[:, d : d + lanes],
                        (((1,), (1,)), ((), ())),
                        preferred_element_type=f32,
                    ).astype(bf16)

        def store(k, s):
            at = pl.ds(pl.multiple_of(k * cols, cols), cols)
            return pltpu.make_async_copy(
                ready.at[s], out_ref.at[:, 0, pl.ds(base, 2), at], out_sem.at[s]
            )

        @pl.when(step >= 2)
        def _():
            store(step - 2, slot).wait()

        right = g_ref[...].reshape(2 * tokens, cols)
        for d in range(0, 2 * share, 512):
            made = jnp.dot(left[d : d + 512], right, preferred_element_type=f32).astype(bf16)
            ready[slot, d // 2 : d // 2 + 256] = made.reshape(256, 2, cols)
        store(step, slot).start()

        @pl.when(step == steps - 1)
        def _():
            if steps > 1:
                store(step - 1, 1 - slot).wait()
            store(step, slot).wait()

    return pl.pallas_call(
        kernel,
        grid=(steps,),
        in_specs=[anywhere] * blocks
        + [pl.BlockSpec((2, tokens, cols), lambda r: (0, 0, r))]
        + [anywhere] * len(aliased),
        out_specs=anywhere,
        out_shape=jax.ShapeDtypeStruct((share, 1, 4, piece), bf16),
        scratch_shapes=[
            pltpu.VMEM((tokens, share), bf16),
            pltpu.VMEM((2 * share, 2 * tokens), bf16),
            pltpu.VMEM((2, share, 2, cols), bf16),
            pltpu.SemaphoreType.DMA((blocks,)),
            pltpu.SemaphoreType.DMA((2,)),
        ],
        input_output_aliases={blocks + 1: 0} if aliased else {},
        compiler_params=limits(40),
        cost_estimate=pl.CostEstimate(
            flops=8 * share * tokens * piece, bytes_accessed=4 * share * piece, transcendentals=0
        ),
        name="head_pair",
    )(*hiddens, gradient, *aliased)


def on_device(hidden, head_weight, teacher):
    me_a = lax.axis_index("aa")
    me_b = lax.axis_index("ba")
    count = lax.axis_size("ba")
    few = teacher.shape[0]
    tokens = few * count
    x = me_a // 2

    side = exchange(hidden, "aa", 2)
    core = exchange(hidden, "aa", 1)
    hiddens = [hidden, core, side, exchange(side, "aa", 1)]

    *blocks, teacher_stat = split_teacher(teacher)
    arrived = [blocks[0]] + [exchange(blocks[s], "ba", s) for s in range(1, count)]
    teacher_stats = [teacher_stat] + [exchange(teacher_stat, "aa", m) for m in (1, 2, 3)]

    pair = take_pair(head_weight)
    student, student_stat = student_logits(hiddens, pair)
    packed = pack_stats([student_stat, exchange(student_stat, "aa", 1)], teacher_stats)
    packed = [packed] + [exchange(packed, "ba", s) for s in range(1, count)]
    student_sum, teacher_sum = all_log_sums(packed, few)

    mine = jnp.concatenate(arrived, axis=0)
    met = lax.ppermute(mine, "aa", [(0, 2), (3, 1), (1, 0), (2, 3)])
    own = lax.ppermute(mine, "aa", [(0, 0), (1, 2), (2, 1), (3, 3)])
    order = jnp.concatenate([me_b ^ jnp.arange(count), x[None]]).astype(jnp.int32)
    gradient, found = logit_gradient(order, own, met, student, student_sum, teacher_sum)

    position = jnp.stack([me_a, me_a ^ 1]).astype(jnp.int32)
    kept, sent = hidden_share(position, gradient, pair)
    shares = share_out(kept, exchange(sent, "aa", 1))
    summed = shares[0].astype(f32)
    for s in range(1, count):
        summed = summed + exchange(shares[s], "ba", s).astype(f32)
    summed = summed.astype(bf16)
    grad_hidden = put_together([summed] + [exchange(summed, "ba", s) for s in range(1, count)])

    other = exchange(gradient, "aa", 1)
    grad_head = head_pair(hiddens, gradient, 0, None)
    grad_head = head_pair(hiddens, other, 1, grad_head)

    divergence = jnp.sum(found)[None]
    mask = 1
    while mask < lax.axis_size("aa"):
        divergence = divergence + exchange(divergence, "aa", mask)
        mask *= 2
    mask = 1
    while mask < count:
        divergence = divergence + exchange(divergence, "ba", mask)
        mask *= 2
    return divergence[0] / tokens, grad_hidden, grad_head


def solution(mesh):
    placed = (P("aa", None), P(None, "ba", None, None), P("ba", "aa", None, None))
    return jax.shard_map(
        on_device,
        mesh=mesh,
        in_specs=placed,
        out_specs=(P(), P("aa", None), P("aa", "ba", None, None)),
        check_vma=False,
    )
```

time: 391 us -> 277 us (0.71)
  blocking collectives: 181 us -> 0 us
  Pallas kernels: 0 us -> 101 us
  starting transfers between devices: 10.9 us -> 88 us
  local copies, waits for them, and re-layouts: 90.4 us -> 23.5 us
  matrix products: 57.1 us -> 0 us
  waiting for transfers between devices: 9.35 us -> 53.9 us
  other arithmetic: 25.2 us -> 1.76 us
  between operations: 15.9 us -> 5.92 us
    psum x3 -> x0, blocking collectives: 138 us -> none  [the longest x1 83.1 us: on_device(): grad_hidden = lax.psum(partial_hidden, 'ba').astype(jnp.bfloat16)]
    pallas_call x0 -> x11, Pallas kernels: none -> 101 us  [the longest x1 23.8 us: take_pair(): pl.pallas_call(kernel, in_specs=[anywhere], out_specs=anywhere, out_shape...]
    ppermute x0 -> x44, starting transfers between devices: none -> 88 us  [the longest x42 69.7 us: exchange(): return lax.ppermute(value, axis, [(i, i ^ mask) for i in range(count)])]
    unnamed x13 -> x79, local copies, waits for them, and re-layouts: 83.8 us -> 22.7 us
    dot_general x3 -> x0, matrix products: 57.1 us -> none  [the longest x1 23.3 us: on_device(): lax.dot_general(gradient, weight_flat, (((1,), (1,)), ((), ())), preferre...]
    ppermute x0 -> x44, waiting for transfers between devices: none -> 53.9 us  [the longest x42 53.9 us: exchange(): return lax.ppermute(value, axis, [(i, i ^ mask) for i in range(count)])]
    all_to_all x1 -> x0, blocking collectives: 22.4 us -> none  [on_device(): lax.all_to_all(hidden, 'aa', split_axis=1, concat_axis=0, tiled=True)]
    pmax x1 -> x0, blocking collectives: 19.7 us -> none  [on_device(): student_peak, target_peak = lax.pmax((student_peak, target_peak), 'ba')]
  transfers between devices with their start and end apart: 3 -> 44, of which waited for: 2 -> 19; matrix products, arithmetic and copies ran while one was open for 23% -> 3% of each run, Pallas kernels for 0% -> 29%
where the time goes in v1:
time: 277 us; the launch traced here: 274 us
  Pallas kernels  101 us (36%)
  starting transfers between devices  88 us (32%)
  waiting for transfers between devices  53.9 us (19%)
  local copies, waits for them, and re-layouts  23.5 us (8%)
  between operations  5.92 us (2%)
    ppermute x42, starting transfers between devices, exchange(): return lax.ppermute(value, axis, [(i, i ^ mask) for i in range(count)])  69.7 us
    ppermute x42, waiting for transfers between devices, exchange(): return lax.ppermute(value, axis, [(i, i ^ mask) for i in range(count)])  53.9 us
    pallas_call x1, Pallas kernels, take_pair(): pl.pallas_call(kernel, in_specs=[anywhere], out_specs=anywhere, out_shape...  23.8 us
    unnamed x79, local copies, waits for them, and re-layouts  22.7 us
    pallas_call x2, Pallas kernels, head_pair(): pl.pallas_call(kernel, grid=(steps,), in_specs=[anywhere] * blocks + [pl....  21.6 us
    pallas_call x1, Pallas kernels, student_logits(): pl.pallas_call(kernel, grid=(2, piece // cols), in_specs=[anywhere] * blo...  20.7 us
    ppermute x1, starting transfers between devices, on_device(): own = lax.ppermute(mine, 'aa', [(0, 0), (1, 2), (2, 1), (3, 3)])  17.1 us
    pallas_call x1, Pallas kernels, hidden_share(): pl.pallas_call(kernel, grid_spec=pltpu.PrefetchScalarGridSpec(num_scalar_...  15.6 us
  transfers between devices with their start and end apart: 44, of which 19 were waited for; matrix products, arithmetic and copies ran while one was open for 3% of the time, Pallas kernels for 29%

profile of v1, /device:TPU:0, one launch (start us, length us, event | category | flops | bytes accessed | tf_op | source)
XLA Modules:
  0.0 274.2 jit_solution(6571969186835815177)
XLA Ops:
  2.2 2.9 %split_teacher.1 = (bf16[64,2048]{1,0:T(8,128)(2,1)S(1)}, bf16[64,2048]{1,0:T(8,128)(2,1)S(1)}, bf16[64,2048]{1,0:T(8,128)(2,1)S(1)}, bf16[64,2048]{1,0:T(8,128)...) custom-call(bf16[64,1,8,2048]{3,2,1,0:T(8,128)(2,1)S(1)} %copy-done.2), custom_call_target="tpu_custom_call" | custom-call | tf_op jit(solution)/shard_map/split_teacher/pallas_call | solution.py:83
  5.2 3.0 %collective-permute-start = (bf16[64,2048]{1,0:T(8,128)(2,1)S(1)}, bf16[64,2048]{1,0:T(8,128)(2,1)S(1)}, u32[]{:S(2)}, u32[]{:S(2)}) collective-permute-start(bf16[64,2048]{1,0:T(8,128)(2,1)S(1)} %get-tuple-element.29), channel_id=1, source_target_pairs={{0,1},{1,0},{2,3},{3,2},{4,5},{5,4},{6,7},{7,6},{8,9},{9,8},{10,11... | collective-permute-start | bytes 786440 | tf_op jit(solution)/shard_map/ppermute | solution.py:31
  14.5 2.8 %collective-permute-start.3 = (bf16[64,2048]{1,0:T(8,128)(2,1)S(1)}, bf16[64,2048]{1,0:T(8,128)(2,1)S(1)}, u32[]{:S(2)}, u32[]{:S(2)}) collective-permute-start(bf16[64,2048]{1,0:T(8,128)(2,1)S(1)} %get-tuple-element.32), channel_id=1, source_target_pairs={{0,4},{1,5},{2,6},{3,7},{4,0},{5,1},{6,2},{7,3},{8,12},{9,13},{10,... | collective-permute-start | bytes 786440 | tf_op jit(solution)/shard_map/ppermute | solution.py:31
  18.1 6.4 %collective-permute-done.1 = bf16[64,2048]{1,0:T(8,128)(2,1)S(1)} collective-permute-done((bf16[64,2048]{1,0:T(8,128)(2,1)S(1)}, bf16[64,2048]{1,0:T(8,128)(2,1)S(1)}, u32[]{:S(2)}, u32[]{:S(2)}) %collective-permute-start.1) | collective-permute-done | bytes 262176 | tf_op jit(solution)/shard_map/ppermute | solution.py:31
  26.4 3.3 %collective-permute-done.2 = bf16[64,2048]{1,0:T(8,128)(2,1)S(1)} collective-permute-done((bf16[64,2048]{1,0:T(8,128)(2,1)S(1)}, bf16[64,2048]{1,0:T(8,128)(2,1)S(1)}, u32[]{:S(2)}, u32[]{:S(2)}) %collective-permute-start.2) | collective-permute-done | bytes 262176 | tf_op jit(solution)/shard_map/ppermute | solution.py:31
  29.7 3.5 %collective-permute-start.5 = (bf16[64,2048]{1,0:T(8,128)(2,1)S(1)}, bf16[64,2048]{1,0:T(8,128)(2,1)S(1)}, u32[]{:S(2)}, u32[]{:S(2)}) collective-permute-start(bf16[64,2048]{1,0:T(8,128)(2,1)S(1)} %get-tuple-element.34), channel_id=1, source_target_pairs={{0,6},{1,7},{2,4},{3,5},{4,2},{5,3},{6,0},{7,1},{8,14},{9,15},{10,... | collective-permute-start | bytes 786440 | tf_op jit(solution)/shard_map/ppermute | solution.py:31
  36.7 17.5 %collective-permute-done.4 = bf16[64,2048]{1,0:T(8,128)(2,1)S(1)} collective-permute-done((bf16[64,2048]{1,0:T(8,128)(2,1)S(1)}, bf16[64,2048]{1,0:T(8,128)(2,1)S(1)}, u32[]{:S(2)}, u32[]{:S(2)}) %collective-permute-start.4) | collective-permute-done | bytes 262176 | tf_op jit(solution)/shard_map/ppermute | solution.py:31
  57.7 17.1 %collective-permute-start.7 = (bf16[512,2048]{1,0:T(8,128)(2,1)}, bf16[512,2048]{1,0:T(8,128)(2,1)}, u32[]{:S(2)}, u32[]{:S(2)}) collective-permute-start(bf16[512,2048]{1,0:T(8,128)(2,1)} %constant_dynamic-update-slice_fusion), channel_id=1, source_target_pairs={{0,0},{8,16},{16,8},{24,24},{1,1},{9,17},{17,9},{25,25},{2,2},{10,... | collective-permute-start | bytes 6291464 | tf_op jit(solution)/shard_map/ppermute | solution.py:556
  74.8 23.8 %take_pair.1.refs_4_.w_ref = bf16[2,3072,2048]{2,1,0:T(8,128)(2,1)} custom-call(bf16[3072,1,4,2048]{3,2,1,0:T(4,128)(2,1)} %w_ref.1), custom_call_target="tpu_custom_call" | custom-call | flops 6442450944 | bytes 50331648 | tf_op jit(solution)/shard_map/take_pair/pallas_call | solution.py:145
  98.6 20.7 %student_logits.1 = (f32[2,512,2048]{2,1,0:T(8,128)S(1)}, f32[8,512]{1,0:T(8,128)S(1)}) custom-call(bf16[128,3072]{1,0:T(8,128)(2,1)S(1)} %copy-done.4, bf16[128,3072]{1,0:T(8,128)(2,1)S(1)} %collective-permute-done.9.refs_1_, bf16[128,3072]{1,0:T(8,128)(2,1)S(1)} %collective-permute-done.10.refs_2_, bf16[128,3072]{1,0:T(8,128)(2,1)S(1)} %collective-permute-done.11.refs_3_, ...), custom_call_target="tpu_custom_call" | custom-call | flops 12884901888 | bytes 25165824 | tf_op jit(solution)/shard_map/student_logits/pallas_call | solution.py:214
  119.3 3.4 %copy-done = f32[2,512,2048]{2,1,0:T(8,128)} copy-done((f32[2,512,2048]{2,1,0:T(8,128)}, f32[2,512,2048]{2,1,0:T(8,128)S(1)}, u32[]{:S(2)}) %copy-start) | copy-done | bytes 8388632
  129.7 2.8 %collective-permute-start.22 = (f32[8,512]{1,0:T(8,128)}, f32[8,512]{1,0:T(8,128)S(1)}, u32[]{:S(2)}, u32[]{:S(2)}) collective-permute-start(f32[8,512]{1,0:T(8,128)} %pack_stats.1.refs_0_), channel_id=1, source_target_pairs={{0,7},{1,6},{2,5},{3,4},{4,3},{5,2},{6,1},{7,0},{8,15},{9,14},{10,... | collective-permute-start | bytes 49160 | tf_op jit(solution)/shard_map/ppermute | solution.py:31
  134.2 8.7 %collective-permute-start.20 = (f32[8,512]{1,0:T(8,128)}, f32[8,512]{1,0:T(8,128)S(1)}, u32[]{:S(2)}, u32[]{:S(2)}) collective-permute-start(f32[8,512]{1,0:T(8,128)} %pack_stats.1.refs_0_), channel_id=1, source_target_pairs={{0,5},{1,4},{2,7},{3,6},{4,1},{5,0},{6,3},{7,2},{8,13},{9,12},{10,... | collective-permute-start | bytes 49160 | tf_op jit(solution)/shard_map/ppermute | solution.py:31
  154.5 3.4 %copy-done.1 = f32[2,512,2048]{2,1,0:T(8,128)S(1)} copy-done((f32[2,512,2048]{2,1,0:T(8,128)S(1)}, f32[2,512,2048]{2,1,0:T(8,128)}, u32[]{:S(2)}) %copy-start.1) | copy-done | bytes 8388632
  159.8 8.5 %logit_gradient.1 = (bf16[2,512,2048]{2,1,0:T(8,128)(2,1)}, f32[8,128]{1,0:T(8,128)S(1)}) custom-call(s32[9]{0:T(128)S(1)} %pad_add_fusion.order_ref, bf16[512,2048]{1,0:T(8,128)(2,1)} %collective-permute-done.7.own_ref, bf16[512,2048]{1,0:T(8,128)(2,1)S(1)} %collective-permute-done.8.met_ref, f32[2,512,2048]{2,1,0:T(8,128)S(1)} %copy-done.1, ...), custom_call_target="tpu_custom_call" | custom-call | tf_op jit(solution)/shard_map/logit_gradient/pallas_call | solution.py:333
  168.3 15.6 %hidden_share.1 = (f32[128,3072]{1,0:T(8,128)S(1)}, bf16[128,3072]{1,0:T(8,128)(2,1)S(1)}) custom-call(s32[2]{0:T(128)S(1)} %pad_add_fusion.1.at_ref, bf16[2,512,2048]{2,1,0:T(8,128)(2,1)} %get-tuple-element.42.keep_ref.send_ref.refs_4_, bf16[2,512,2048]{2,1,0:T(8,128)(2,1)} %get-tuple-element.42.keep_ref.send_ref.refs_4_, ...), custom_call_target="tpu_custom_call" | custom-call | flops 6442450944 | bytes 25165824 | tf_op jit(solution)/shard_map/hidden_share/pallas_call | solution.py:375
  188.4 2.6 share_out.1
  197.9 3.7 %collective-permute-start.34 = (bf16[16,3072]{1,0:T(8,128)(2,1)}, bf16[16,3072]{1,0:T(8,128)(2,1)S(1)}, u32[]{:S(2)}, u32[]{:S(2)}) collective-permute-start(bf16[16,3072]{1,0:T(8,128)(2,1)} %get-tuple-element.51), channel_id=1, source_target_pairs={{0,6},{1,7},{2,4},{3,5},{4,2},{5,3},{6,0},{7,1},{8,14},{9,15},{10,... | collective-permute-start | bytes 294920 | tf_op jit(solution)/shard_map/ppermute | solution.py:31
  204.8 4.6 %collective-permute-done.32 = bf16[16,3072]{1,0:T(8,128)(2,1)S(1)} collective-permute-done((bf16[16,3072]{1,0:T(8,128)(2,1)}, bf16[16,3072]{1,0:T(8,128)(2,1)S(1)}, u32[]{:S(2)}, u32[]{:S(2)}) %collective-permute-start.32) | collective-permute-done | bytes 98336 | tf_op jit(solution)/shard_map/ppermute | solution.py:31
  217.4 3.1 %collective-permute-start.40 = (bf16[16,3072]{1,0:T(8,128)(2,1)S(1)}, bf16[16,3072]{1,0:T(8,128)(2,1)S(1)}, u32[]{:S(2)}, u32[]{:S(2)}) collective-permute-start(bf16[16,3072]{1,0:T(8,128)(2,1)S(1)} %add_convert_fusion.refs_0_), channel_id=1, source_target_pairs={{0,5},{1,4},{2,7},{3,6},{4,1},{5,0},{6,3},{7,2},{8,13},{9,12},{10,... | collective-permute-start | bytes 294920 | tf_op jit(solution)/shard_map/ppermute | solution.py:31
  238.1 3.3 %collective-permute-done.27 = f32[1]{0:T(128)} collective-permute-done((f32[1]{0:T(128)}, f32[1]{0:T(128)}, u32[]{:S(2)}, u32[]{:S(2)}) %collective-permute-start.27) | collective-permute-done | bytes 36 | tf_op jit(solution)/shard_map/ppermute | solution.py:31
  241.4 2.8 %collective-permute-start.38 = (bf16[16,3072]{1,0:T(8,128)(2,1)S(1)}, bf16[16,3072]{1,0:T(8,128)(2,1)S(1)}, u32[]{:S(2)}, u32[]{:S(2)}) collective-permute-start(bf16[16,3072]{1,0:T(8,128)(2,1)S(1)} %add_convert_fusion.refs_0_), channel_id=1, source_target_pairs={{0,3},{1,2},{2,1},{3,0},{4,7},{5,6},{6,5},{7,4},{8,11},{9,10},{10,... | collective-permute-start | bytes 294920 | tf_op jit(solution)/shard_map/ppermute | solution.py:31
  246.1 10.8 %head_pair.2.refs_5_ = bf16[768,1,4,2048]{3,2,1,0:T(4,128)(2,1)} custom-call(bf16[128,3072]{1,0:T(8,128)(2,1)S(1)} %copy-done.4, bf16[128,3072]{1,0:T(8,128)(2,1)S(1)} %copy-done.8, bf16[128,3072]{1,0:T(8,128)(2,1)S(1)} %copy-done.6, bf16[128,3072]{1,0:T(8,128)(2,1)S(1)} %copy-done.10, bf16[2,512,2048]{2,1,0:T(8,128)(2,1)} %get-tuple-element.42.keep_ref.send_ref.refs_4_), custom_call_target="tpu_custom_call" | custom-call | flops 6442450944 | bytes 6291456 | tf_op jit(solution)/shard_map/head_pair/pallas_call | solution.py:508
  262.3 10.8 %head_pair.3 = bf16[768,1,4,2048]{3,2,1,0:T(4,128)(2,1)} custom-call(bf16[128,3072]{1,0:T(8,128)(2,1)S(1)} %copy-done.4, bf16[128,3072]{1,0:T(8,128)(2,1)S(1)} %copy-done.8, bf16[128,3072]{1,0:T(8,128)(2,1)S(1)} %copy-done.6, bf16[128,3072]{1,0:T(8,128)(2,1)S(1)} %copy-done.11, ...), custom_call_target="tpu_custom_call", output_to_operand_aliasing={{}: (5, {})} | custom-call | flops 6442450944 | bytes 6291456 | tf_op jit(solution)/shard_map/head_pair/pallas_call | solution.py:508
  (160 shorter events, 83.0 us)
Async XLA Ops:
  8.2 47.4 %collective-permute-start.10 = (bf16[128,3072]{1,0:T(8,128)(2,1)S(1)}, bf16[128,3072]{1,0:T(8,128)(2,1)S(1)}, u32[]{:S(2)}, u32[]{:S(2)}) collective-permute-start(bf16[128,3072]{1,0:T(8,128)(2,1)S(1)} %copy-done.4), channel_id=1, source_target_pairs={{0,16},{8,24},{16,0},{24,8},{1,17},{9,25},{17,1},{25,9},{2,18},{10... | collective-permute-start | bytes 2359304 | tf_op jit(solution)/shard_map/ppermute | solution.py:31
  9.7 88.9 %collective-permute-start.9 = (bf16[128,3072]{1,0:T(8,128)(2,1)S(1)}, bf16[128,3072]{1,0:T(8,128)(2,1)S(1)}, u32[]{:S(2)}, u32[]{:S(2)}) collective-permute-start(bf16[128,3072]{1,0:T(8,128)(2,1)S(1)} %copy-done.4), channel_id=1, source_target_pairs={{0,8},{8,0},{16,24},{24,16},{1,9},{9,1},{17,25},{25,17},{2,10},{10... | collective-permute-start | bytes 2359304 | tf_op jit(solution)/shard_map/ppermute | solution.py:31
  9.7 14.7 %collective-permute-start.1 = (bf16[64,2048]{1,0:T(8,128)(2,1)S(1)}, bf16[64,2048]{1,0:T(8,128)(2,1)S(1)}, u32[]{:S(2)}, u32[]{:S(2)}) collective-permute-start(bf16[64,2048]{1,0:T(8,128)(2,1)S(1)} %get-tuple-element.30), channel_id=1, source_target_pairs={{0,2},{1,3},{2,0},{3,1},{4,6},{5,7},{6,4},{7,5},{8,10},{9,11},{10,... | collective-permute-start | bytes 786440 | tf_op jit(solution)/shard_map/ppermute | solution.py:31
  11.3 18.4 %collective-permute-start.2 = (bf16[64,2048]{1,0:T(8,128)(2,1)S(1)}, bf16[64,2048]{1,0:T(8,128)(2,1)S(1)}, u32[]{:S(2)}, u32[]{:S(2)}) collective-permute-start(bf16[64,2048]{1,0:T(8,128)(2,1)S(1)} %get-tuple-element.31), channel_id=1, source_target_pairs={{0,3},{1,2},{2,1},{3,0},{4,7},{5,6},{6,5},{7,4},{8,11},{9,10},{10,... | collective-permute-start | bytes 786440 | tf_op jit(solution)/shard_map/ppermute | solution.py:31
  14.5 19.5 %collective-permute-start.3 = (bf16[64,2048]{1,0:T(8,128)(2,1)S(1)}, bf16[64,2048]{1,0:T(8,128)(2,1)S(1)}, u32[]{:S(2)}, u32[]{:S(2)}) collective-permute-start(bf16[64,2048]{1,0:T(8,128)(2,1)S(1)} %get-tuple-element.32), channel_id=1, source_target_pairs={{0,4},{1,5},{2,6},{3,7},{4,0},{5,1},{6,2},{7,3},{8,12},{9,13},{10,... | collective-permute-start | bytes 786440 | tf_op jit(solution)/shard_map/ppermute | solution.py:31
  24.4 29.8 %collective-permute-start.4 = (bf16[64,2048]{1,0:T(8,128)(2,1)S(1)}, bf16[64,2048]{1,0:T(8,128)(2,1)S(1)}, u32[]{:S(2)}, u32[]{:S(2)}) collective-permute-start(bf16[64,2048]{1,0:T(8,128)(2,1)S(1)} %get-tuple-element.33), channel_id=1, source_target_pairs={{0,5},{1,4},{2,7},{3,6},{4,1},{5,0},{6,3},{7,2},{8,13},{9,12},{10,... | collective-permute-start | bytes 786440 | tf_op jit(solution)/shard_map/ppermute | solution.py:31
  29.7 25.2 %collective-permute-start.5 = (bf16[64,2048]{1,0:T(8,128)(2,1)S(1)}, bf16[64,2048]{1,0:T(8,128)(2,1)S(1)}, u32[]{:S(2)}, u32[]{:S(2)}) collective-permute-start(bf16[64,2048]{1,0:T(8,128)(2,1)S(1)} %get-tuple-element.34), channel_id=1, source_target_pairs={{0,6},{1,7},{2,4},{3,5},{4,2},{5,3},{6,0},{7,1},{8,14},{9,15},{10,... | collective-permute-start | bytes 786440 | tf_op jit(solution)/shard_map/ppermute | solution.py:31
  34.0 21.7 %collective-permute-start.6 = (bf16[64,2048]{1,0:T(8,128)(2,1)S(1)}, bf16[64,2048]{1,0:T(8,128)(2,1)S(1)}, u32[]{:S(2)}, u32[]{:S(2)}) collective-permute-start(bf16[64,2048]{1,0:T(8,128)(2,1)S(1)} %get-tuple-element.35), channel_id=1, source_target_pairs={{0,7},{1,6},{2,5},{3,4},{4,3},{5,2},{6,1},{7,0},{8,15},{9,14},{10,... | collective-permute-start | bytes 786440 | tf_op jit(solution)/shard_map/ppermute | solution.py:31
  55.7 43.0 %collective-permute-start.11 = (bf16[128,3072]{1,0:T(8,128)(2,1)S(1)}, bf16[128,3072]{1,0:T(8,128)(2,1)S(1)}, u32[]{:S(2)}, u32[]{:S(2)}) collective-permute-start(bf16[128,3072]{1,0:T(8,128)(2,1)S(1)} %collective-permute-done.10.refs_2_), channel_id=1, source_target_pairs={{0,8},{8,0},{16,24},{24,16},{1,9},{9,1},{17,25},{25,17},{2,10},{10... | collective-permute-start | bytes 2359304 | tf_op jit(solution)/shard_map/ppermute | solution.py:31
  56.5 98.0 %collective-permute-start.8 = (bf16[512,2048]{1,0:T(8,128)(2,1)}, bf16[512,2048]{1,0:T(8,128)(2,1)S(1)}, u32[]{:S(2)}, u32[]{:S(2)}) collective-permute-start(bf16[512,2048]{1,0:T(8,128)(2,1)} %constant_dynamic-update-slice_fusion), channel_id=1, source_target_pairs={{0,16},{24,8},{8,0},{16,24},{1,17},{25,9},{9,1},{17,25},{2,18},{26... | collective-permute-start | bytes 6291464 | tf_op jit(solution)/shard_map/ppermute | solution.py:555
  57.7 96.8 %collective-permute-start.7 = (bf16[512,2048]{1,0:T(8,128)(2,1)}, bf16[512,2048]{1,0:T(8,128)(2,1)}, u32[]{:S(2)}, u32[]{:S(2)}) collective-permute-start(bf16[512,2048]{1,0:T(8,128)(2,1)} %constant_dynamic-update-slice_fusion), channel_id=1, source_target_pairs={{0,0},{8,16},{16,8},{24,24},{1,1},{9,17},{17,9},{25,25},{2,2},{10,... | collective-permute-start | bytes 6291464 | tf_op jit(solution)/shard_map/ppermute | solution.py:556
  129.7 13.3 %collective-permute-start.22 = (f32[8,512]{1,0:T(8,128)}, f32[8,512]{1,0:T(8,128)S(1)}, u32[]{:S(2)}, u32[]{:S(2)}) collective-permute-start(f32[8,512]{1,0:T(8,128)} %pack_stats.1.refs_0_), channel_id=1, source_target_pairs={{0,7},{1,6},{2,5},{3,4},{4,3},{5,2},{6,1},{7,0},{8,15},{9,14},{10,... | collective-permute-start | bytes 49160 | tf_op jit(solution)/shard_map/ppermute | solution.py:31
  132.5 12.4 %collective-permute-start.21 = (f32[8,512]{1,0:T(8,128)}, f32[8,512]{1,0:T(8,128)S(1)}, u32[]{:S(2)}, u32[]{:S(2)}) collective-permute-start(f32[8,512]{1,0:T(8,128)} %pack_stats.1.refs_0_), channel_id=1, source_target_pairs={{0,6},{1,7},{2,4},{3,5},{4,2},{5,3},{6,0},{7,1},{8,14},{9,15},{10,... | collective-permute-start | bytes 49160 | tf_op jit(solution)/shard_map/ppermute | solution.py:31
  168.3 92.9 %collective-permute-start.43 = (bf16[2,512,2048]{2,1,0:T(8,128)(2,1)}, bf16[2,512,2048]{2,1,0:T(8,128)(2,1)}, u32[]{:S(2)}, u32[]{:S(2)}) collective-permute-start(bf16[2,512,2048]{2,1,0:T(8,128)(2,1)} %get-tuple-element.42.keep_ref.send_ref.refs_4_), channel_id=1, source_target_pairs={{0,8},{8,0},{16,24},{24,16},{1,9},{9,1},{17,25},{25,17},{2,10},{10... | collective-permute-start | bytes 12582920 | tf_op jit(solution)/shard_map/ppermute | solution.py:31
  194.5 14.9 %collective-permute-start.32 = (bf16[16,3072]{1,0:T(8,128)(2,1)}, bf16[16,3072]{1,0:T(8,128)(2,1)S(1)}, u32[]{:S(2)}, u32[]{:S(2)}) collective-permute-start(bf16[16,3072]{1,0:T(8,128)(2,1)} %get-tuple-element.49), channel_id=1, source_target_pairs={{0,4},{1,5},{2,6},{3,7},{4,0},{5,1},{6,2},{7,3},{8,12},{9,13},{10,... | collective-permute-start | bytes 294920 | tf_op jit(solution)/shard_map/ppermute | solution.py:31
  196.3 15.2 %collective-permute-start.33 = (bf16[16,3072]{1,0:T(8,128)(2,1)}, bf16[16,3072]{1,0:T(8,128)(2,1)S(1)}, u32[]{:S(2)}, u32[]{:S(2)}) collective-permute-start(bf16[16,3072]{1,0:T(8,128)(2,1)} %get-tuple-element.50), channel_id=1, source_target_pairs={{0,5},{1,4},{2,7},{3,6},{4,1},{5,0},{6,3},{7,2},{8,13},{9,12},{10,... | collective-permute-start | bytes 294920 | tf_op jit(solution)/shard_map/ppermute | solution.py:31
  197.9 13.5 %collective-permute-start.34 = (bf16[16,3072]{1,0:T(8,128)(2,1)}, bf16[16,3072]{1,0:T(8,128)(2,1)S(1)}, u32[]{:S(2)}, u32[]{:S(2)}) collective-permute-start(bf16[16,3072]{1,0:T(8,128)(2,1)} %get-tuple-element.51), channel_id=1, source_target_pairs={{0,6},{1,7},{2,4},{3,5},{4,2},{5,3},{6,0},{7,1},{8,14},{9,15},{10,... | collective-permute-start | bytes 294920 | tf_op jit(solution)/shard_map/ppermute | solution.py:31
  212.5 28.9 %collective-permute-start.42 = (bf16[16,3072]{1,0:T(8,128)(2,1)S(1)}, bf16[16,3072]{1,0:T(8,128)(2,1)S(1)}, u32[]{:S(2)}, u32[]{:S(2)}) collective-permute-start(bf16[16,3072]{1,0:T(8,128)(2,1)S(1)} %add_convert_fusion.refs_0_), channel_id=1, source_target_pairs={{0,7},{1,6},{2,5},{3,4},{4,3},{5,2},{6,1},{7,0},{8,15},{9,14},{10,... | collective-permute-start | bytes 294920 | tf_op jit(solution)/shard_map/ppermute | solution.py:31
  215.1 29.2 %collective-permute-start.41 = (bf16[16,3072]{1,0:T(8,128)(2,1)S(1)}, bf16[16,3072]{1,0:T(8,128)(2,1)S(1)}, u32[]{:S(2)}, u32[]{:S(2)}) collective-permute-start(bf16[16,3072]{1,0:T(8,128)(2,1)S(1)} %add_convert_fusion.refs_0_), channel_id=1, source_target_pairs={{0,6},{1,7},{2,4},{3,5},{4,2},{5,3},{6,0},{7,1},{8,14},{9,15},{10,... | collective-permute-start | bytes 294920 | tf_op jit(solution)/shard_map/ppermute | solution.py:31
  217.4 26.9 %collective-permute-start.40 = (bf16[16,3072]{1,0:T(8,128)(2,1)S(1)}, bf16[16,3072]{1,0:T(8,128)(2,1)S(1)}, u32[]{:S(2)}, u32[]{:S(2)}) collective-permute-start(bf16[16,3072]{1,0:T(8,128)(2,1)S(1)} %add_convert_fusion.refs_0_), channel_id=1, source_target_pairs={{0,5},{1,4},{2,7},{3,6},{4,1},{5,0},{6,3},{7,2},{8,13},{9,12},{10,... | collective-permute-start | bytes 294920 | tf_op jit(solution)/shard_map/ppermute | solution.py:31
  241.4 16.2 %collective-permute-start.39 = (bf16[16,3072]{1,0:T(8,128)(2,1)S(1)}, bf16[16,3072]{1,0:T(8,128)(2,1)S(1)}, u32[]{:S(2)}, u32[]{:S(2)}) collective-permute-start(bf16[16,3072]{1,0:T(8,128)(2,1)S(1)} %add_convert_fusion.refs_0_), channel_id=1, source_target_pairs={{0,4},{1,5},{2,6},{3,7},{4,0},{5,1},{6,2},{7,3},{8,12},{9,13},{10,... | collective-permute-start | bytes 294920 | tf_op jit(solution)/shard_map/ppermute | solution.py:31
  241.4 16.2 %collective-permute-start.38 = (bf16[16,3072]{1,0:T(8,128)(2,1)S(1)}, bf16[16,3072]{1,0:T(8,128)(2,1)S(1)}, u32[]{:S(2)}, u32[]{:S(2)}) collective-permute-start(bf16[16,3072]{1,0:T(8,128)(2,1)S(1)} %add_convert_fusion.refs_0_), channel_id=1, source_target_pairs={{0,3},{1,2},{2,1},{3,0},{4,7},{5,6},{6,5},{7,4},{8,11},{9,10},{10,... | collective-permute-start | bytes 294920 | tf_op jit(solution)/shard_map/ppermute | solution.py:31
  244.2 13.4 %collective-permute-start.37 = (bf16[16,3072]{1,0:T(8,128)(2,1)S(1)}, bf16[16,3072]{1,0:T(8,128)(2,1)S(1)}, u32[]{:S(2)}, u32[]{:S(2)}) collective-permute-start(bf16[16,3072]{1,0:T(8,128)(2,1)S(1)} %add_convert_fusion.refs_0_), channel_id=1, source_target_pairs={{0,2},{1,3},{2,0},{3,1},{4,6},{5,7},{6,4},{7,5},{8,10},{9,11},{10,... | collective-permute-start | bytes 294920 | tf_op jit(solution)/shard_map/ppermute | solution.py:31
  244.3 13.4 %collective-permute-start.36 = (bf16[16,3072]{1,0:T(8,128)(2,1)S(1)}, bf16[16,3072]{1,0:T(8,128)(2,1)S(1)}, u32[]{:S(2)}, u32[]{:S(2)}) collective-permute-start(bf16[16,3072]{1,0:T(8,128)(2,1)S(1)} %add_convert_fusion.refs_0_), channel_id=1, source_target_pairs={{0,1},{1,0},{2,3},{3,2},{4,5},{5,4},{6,7},{7,6},{8,9},{9,8},{10,11... | collective-permute-start | bytes 294920 | tf_op jit(solution)/shard_map/ppermute | solution.py:31
  (56 other events, 572.6 us)

commit v2 on v1

v2 whole, which is shorter than its diff:
```python
import functools

import jax
import jax.numpy as jnp
from jax import lax
from jax.experimental import pallas as pl
from jax.experimental.pallas import tpu as pltpu
from jax.sharding import PartitionSpec as P

grad_scale = 256.0
lanes = 128
absent = -1e30
f32 = jnp.float32
bf16 = jnp.bfloat16
anywhere = pl.BlockSpec(memory_space=pl.ANY)
whole_vmem = pl.BlockSpec(memory_space=pltpu.VMEM)


def in_hbm(*values):
    return [pltpu.with_memory_space_constraint(value, pltpu.HBM) for value in values]


def in_vmem(value):
    return pltpu.with_memory_space_constraint(value, pltpu.VMEM)


def limits(mib):
    return pltpu.CompilerParams(vmem_limit_bytes=mib << 20)


def largest_tile(size, most, step):
    tile = min(size, most)
    while size % tile or tile % step:
        tile -= step
    return tile


def my_pair():
    me = lax.axis_index("aa")
    return (me % 2) ^ (me // 2)


def gate(values, deps):
    return lax.optimization_barrier((values, deps))[0]


def exchange(value, axis, mask):
    count = lax.axis_size(axis)
    return lax.ppermute(value, axis, [(i, i ^ mask) for i in range(count)])


def lane_row(column, rows):
    return jnp.transpose(jnp.broadcast_to(column, (rows, lanes)))[0:1]


def split_teacher(teacher):
    tokens, _, owners, piece = teacher.shape
    every = tokens * owners
    cols = largest_tile(piece, 512, lanes)

    def kernel(in_ref, *refs):
        outs, (stat_ref, peak_ref, total_ref) = refs[:owners], refs[owners:]
        step = pl.program_id(0)
        me = lax.axis_index("ba")
        flat = in_ref[:, 0].reshape(every, cols)
        row = lax.broadcasted_iota(jnp.int32, (every, every), 0)
        col = lax.broadcasted_iota(jnp.int32, (every, every), 1)
        source = (row % tokens) * owners + ((row // tokens) ^ me)
        pick = (col == source).astype(f32).astype(bf16)
        moved = jnp.dot(pick, flat, preferred_element_type=f32)
        for s in range(owners):
            outs[s][...] = moved[s * tokens : (s + 1) * tokens].astype(bf16)
        parts = [
            moved[s * tokens : (s + 1) * tokens, k : k + lanes]
            for s in range(owners)
            for k in range(0, cols, lanes)
        ]
        peak = functools.reduce(jnp.maximum, parts)

        @pl.when(step == 0)
        def _():
            peak_ref[...] = peak
            total_ref[...] = jnp.zeros_like(total_ref)

        old = peak_ref[...]
        new = jnp.maximum(old, peak)
        total = total_ref[...] * jnp.exp(old - new)
        for part in parts:
            total = total + jnp.exp(part - new)
        peak_ref[...] = new
        total_ref[...] = total

        @pl.when(step == pl.num_programs(0) - 1)
        def _():
            top = jnp.max(new, axis=1, keepdims=True)
            summed = jnp.sum(total * jnp.exp(new - top), axis=1, keepdims=True)
            token = lax.broadcasted_iota(jnp.int32, (tokens, every), 0) + me * tokens
            here = token == lax.broadcasted_iota(jnp.int32, (tokens, every), 1)
            peaks = jnp.max(jnp.where(here, top, absent), axis=0, keepdims=True)
            sums = jnp.sum(jnp.where(here, summed, 0.0), axis=0, keepdims=True)
            stat_ref[0:1, :] = peaks
            stat_ref[1:2, :] = sums
            stat_ref[2:8, :] = jnp.zeros((6, every), f32)

    return pl.pallas_call(
        kernel,
        grid=(piece // cols,),
        in_specs=[pl.BlockSpec((tokens, 1, owners, cols), lambda r: (0, 0, 0, r))],
        out_specs=[pl.BlockSpec((tokens, cols), lambda r: (0, r))] * owners
        + [pl.BlockSpec((8, every), lambda r: (0, 0))],
        out_shape=[pltpu.HBM((tokens, piece), bf16)] * owners
        + [jax.ShapeDtypeStruct((8, every), f32)],
        scratch_shapes=[pltpu.VMEM((tokens, lanes), f32)] * 2,
        compiler_params=limits(20),
        name="split_teacher",
    )(*in_hbm(teacher))


def take_pair(head_weight):
    width, _, _, piece = head_weight.shape
    rows = largest_tile(width, 256, lanes)
    steps = width // rows
    depth = min(4, steps)

    def kernel(w_ref, out_ref, taken, in_sem):
        pair = my_pair()
        row = lax.broadcasted_iota(jnp.int32, (2 * lanes, 2 * lanes), 0)
        col = lax.broadcasted_iota(jnp.int32, (2 * lanes, 2 * lanes), 1)
        pick = (col == (row % lanes) * 2 + row // lanes).astype(f32).astype(bf16)

        def fetch(i):
            return pltpu.make_async_copy(
                w_ref.at[pl.ds(i * rows, rows), 0, pl.ds(2 * pair, 2), :],
                taken.at[i % depth],
                in_sem.at[i % depth],
            )

        for i in range(depth):
            fetch(i).start()
        for i in range(steps):
            fetch(i).wait()
            for q in range(0, rows, lanes):
                block = taken[i % depth, q : q + lanes].reshape(2 * lanes, piece)
                moved = jnp.dot(pick, block, preferred_element_type=f32).astype(bf16)
                at = i * rows + q
                out_ref[0, at : at + lanes] = moved[:lanes]
                out_ref[1, at : at + lanes] = moved[lanes:]
            if i + depth < steps:
                fetch(i + depth).start()

    return pl.pallas_call(
        kernel,
        in_specs=[anywhere],
        out_specs=whole_vmem,
        out_shape=pltpu.VMEM((2, width, piece), bf16),
        scratch_shapes=[
            pltpu.VMEM((depth, rows, 2, piece), bf16),
            pltpu.SemaphoreType.DMA((depth,)),
        ],
        compiler_params=limits(20),
        cost_estimate=pl.CostEstimate(
            flops=16 * lanes * width * piece,
            bytes_accessed=4 * width * piece,
            transcendentals=0,
        ),
        name="take_pair",
    )(head_weight)


def student_logits(hiddens, pair, which):
    rows, width = hiddens[0].shape
    blocks = len(hiddens)
    tokens = rows * blocks
    piece = pair.shape[2]
    cols = largest_tile(piece, 512, lanes)

    def kernel(*refs):
        given, w_ref = refs[:blocks], refs[blocks]
        out_ref, stat_ref, left, peak_ref, total_ref, sem = refs[blocks + 1 :]
        step = pl.program_id(0)
        me = lax.axis_index("aa")

        @pl.when(step == 0)
        def _():
            def place(q):
                at = pl.ds(pl.multiple_of((me ^ q) * rows, rows), rows)
                return pltpu.make_async_copy(given[q], left.at[at], sem.at[q])

            for q in range(blocks):
                place(q).start()
            peak_ref[...] = jnp.full_like(peak_ref, absent)
            total_ref[...] = jnp.zeros_like(total_ref)
            for q in range(blocks):
                place(q).wait()

        at = pl.ds(pl.multiple_of(step * cols, cols), cols)
        out_ref[...] = jnp.dot(left[...], w_ref[which, :, at], preferred_element_type=f32)

        @pl.loop(0, tokens // 64)
        def _(k):
            at = pl.ds(pl.multiple_of(k * 64, 64), 64)
            parts = [out_ref[at, j : j + lanes] for j in range(0, cols, lanes)]
            old = peak_ref[at]
            new = functools.reduce(jnp.maximum, parts, old)
            total = total_ref[at] * jnp.exp(old - new)
            for part in parts:
                total = total + jnp.exp(part - new)
            peak_ref[at] = new
            total_ref[at] = total

        @pl.when(step == pl.num_programs(0) - 1)
        def _():
            peak = peak_ref[...]
            top = jnp.max(peak, axis=1, keepdims=True)
            summed = jnp.sum(total_ref[...] * jnp.exp(peak - top), axis=1, keepdims=True)
            stat_ref[0:1, :] = lane_row(top, tokens)
            stat_ref[1:2, :] = lane_row(summed, tokens)
            stat_ref[2:8, :] = jnp.zeros((6, tokens), f32)

    return pl.pallas_call(
        kernel,
        grid=(piece // cols,),
        in_specs=[anywhere] * blocks
        + [whole_vmem],
        out_specs=[
            pl.BlockSpec((tokens, cols), lambda r: (0, r)),
            pl.BlockSpec((8, tokens), lambda r: (0, 0)),
        ],
        out_shape=[
            pltpu.HBM((tokens, piece), f32),
            jax.ShapeDtypeStruct((8, tokens), f32),
        ],
        scratch_shapes=[
            pltpu.VMEM((tokens, width), bf16),
            pltpu.VMEM((tokens, lanes), f32),
            pltpu.VMEM((tokens, lanes), f32),
            pltpu.SemaphoreType.DMA((blocks,)),
        ],
        compiler_params=limits(20),
        cost_estimate=pl.CostEstimate(flops=1, bytes_accessed=1, transcendentals=0),
        name="student_logits",
    )(*in_hbm(*hiddens), in_vmem(pair))


def merge(stats, row=0):
    peak = functools.reduce(jnp.maximum, [s[row : row + 1] for s in stats])
    total = sum(s[row + 1 : row + 2] * jnp.exp(s[row : row + 1] - peak) for s in stats)
    return peak, total


def pack_stats(student_stats, teacher_stats):
    tokens = student_stats[0].shape[1]
    count = len(student_stats)

    def kernel(*refs):
        out_ref = refs[-1]
        peak, total = merge([r[...] for r in refs[:count]])
        out_ref[0:1, :] = peak
        out_ref[1:2, :] = total
        peak, total = merge([r[...] for r in refs[count:-1]])
        out_ref[2:3, :] = peak
        out_ref[3:4, :] = total
        out_ref[4:8, :] = jnp.zeros((4, tokens), f32)

    return pl.pallas_call(
        kernel,
        in_specs=[whole_vmem] * (count + len(teacher_stats)),
        out_specs=whole_vmem,
        out_shape=jax.ShapeDtypeStruct((8, tokens), f32),
        compiler_params=limits(20),
        name="pack_stats",
    )(*student_stats, *teacher_stats)


def merge_two(first, second):
    tokens = first.shape[1]

    def kernel(a_ref, b_ref, out_ref):
        both = [a_ref[...], b_ref[...]]
        for row in (0, 2):
            peak, total = merge(both, row)
            out_ref[row : row + 1, :] = peak
            out_ref[row + 1 : row + 2, :] = total
        out_ref[4:8, :] = jnp.zeros((4, tokens), f32)

    return pl.pallas_call(
        kernel,
        in_specs=[whole_vmem] * 2,
        out_specs=whole_vmem,
        out_shape=jax.ShapeDtypeStruct((8, tokens), f32),
        compiler_params=limits(20),
        name="merge_two",
    )(first, second)


def all_log_sums(first, second):
    tokens = first.shape[1]

    def kernel(a_ref, b_ref, *outs):
        both = [a_ref[...], b_ref[...]]
        for row, out_ref in zip((0, 2), outs):
            peak, total = merge(both, row)
            wide = jnp.broadcast_to(peak + jnp.log(total), (lanes, tokens))
            out_ref[...] = jnp.transpose(wide)

    return pl.pallas_call(
        kernel,
        in_specs=[whole_vmem] * 2,
        out_specs=[whole_vmem] * 2,
        out_shape=[pltpu.HBM((tokens, lanes), f32)] * 2,
        compiler_params=limits(20),
        name="all_log_sums",
    )(first, second)


def logit_gradient(plan, groups, students, student_sum, teacher_sum):
    kinds = len(groups)
    count = (plan.shape[0] - 1) // (3 + kinds)
    tokens, piece = students[0].shape
    half = tokens // 2
    few = half // count
    cols = largest_tile(piece, 512, lanes)
    rows = 16

    def kernel(plan_ref, *refs):
        teachers, s_refs = refs[: 4 * kinds], refs[4 * kinds : 4 * kinds + 2]
        ssum_ref, tsum_ref = refs[4 * kinds + 2 : 4 * kinds + 4]
        g_ref, div_ref = refs[-2:]
        step = pl.program_id(0)
        kind = plan_ref[(2 + kinds) * count + step]
        core = plan_ref[(3 + kinds) * count]

        @pl.when(step == 0)
        def _():
            div_ref[...] = jnp.zeros_like(div_ref)

        def work(ordered):
            @pl.loop(0, few // rows)
            def _(k):
                at = pl.ds(pl.multiple_of(k * rows, rows), rows)
                ssum = jnp.concatenate([ssum_ref[at]] * (cols // lanes), axis=1)
                tsum = jnp.concatenate([tsum_ref[at]] * (cols // lanes), axis=1)
                found = jnp.zeros((rows, cols), f32)
                for i, t_ref in enumerate(ordered):
                    for j in range(0, piece, cols):
                        log_s = s_refs[i][at, j : j + cols] - ssum
                        log_t = t_ref[at, j : j + cols].astype(f32) - tsum
                        prob_t = jnp.exp(log_t)
                        g_ref[i, at, j : j + cols] = (
                            grad_scale * (jnp.exp(log_s) - prob_t)
                        ).astype(bf16)
                        found = found + prob_t * (log_t - log_s)
                folded = [
                    found[m : m + 8, n : n + lanes]
                    for m in range(0, rows, 8)
                    for n in range(0, cols, lanes)
                ]
                div_ref[...] += sum(folded[1:], folded[0])

        for at_kind in range(kinds):
            for at_core in (0, 1):
                own_ref, side_ref, own_met_ref, side_met_ref = teachers[4 * at_kind : 4 * at_kind + 4]

                @pl.when((kind == at_kind) & (core == at_core))
                def _(ordered=((own_ref, own_met_ref), (side_met_ref, side_ref))[at_core]):
                    work(ordered)

    def block_of(kind, of_core):
        def at(s, p):
            return (jnp.where(p[(3 + kinds) * count] == of_core, p[(2 + kind) * count + s], 0), 0)

        return at

    return pl.pallas_call(
        kernel,
        grid_spec=pltpu.PrefetchScalarGridSpec(
            num_scalar_prefetch=1,
            grid=(count,),
            in_specs=[
                pl.BlockSpec((few, piece), block_of(kind, n % 2)) for kind in range(kinds) for n in range(4)
            ]
            + [pl.BlockSpec((few, piece), lambda s, p: (p[count + s], 0))] * 2
            + [pl.BlockSpec((few, lanes), lambda s, p: (p[count + s], 0))] * 2,
            out_specs=[
                pl.BlockSpec((2, few, piece), lambda s, p: (0, p[s], 0)),
                pl.BlockSpec((8, lanes), lambda s, p: (0, 0)),
            ],
        ),
        out_shape=[
            pltpu.HBM((2, half, piece), bf16),
            jax.ShapeDtypeStruct((8, lanes), f32),
        ],
        compiler_params=limits(20),
        cost_estimate=pl.CostEstimate(
            flops=8 * half * piece, bytes_accessed=16 * half * piece, transcendentals=4 * half * piece
        ),
        name="logit_gradient",
    )(
        plan,
        *in_hbm(*[part for group in groups for part in group]),
        *in_hbm(*students, student_sum, teacher_sum),
    )


def hidden_share(gradient, pair):
    _, tokens, piece = gradient.shape
    width = pair.shape[1]
    half = tokens // 2
    cols = largest_tile(width, 768, lanes)

    def kernel(g_ref, w_ref, kept_ref, sent_ref):
        core = lax.axis_index("aa") % 2
        total = sum(
            lax.dot_general(
                g_ref[i], w_ref[i], (((1,), (1,)), ((), ())), preferred_element_type=f32
            )
            for i in range(2)
        )

        @pl.when(core == 0)
        def _():
            kept_ref[...] = total[:half]
            sent_ref[...] = total[half:].astype(bf16)

        @pl.when(core == 1)
        def _():
            kept_ref[...] = total[half:]
            sent_ref[...] = total[:half].astype(bf16)

    return pl.pallas_call(
        kernel,
        grid=(width // cols,),
        in_specs=[
            pl.BlockSpec((2, tokens, piece), lambda d: (0, 0, 0)),
            pl.BlockSpec((2, cols, piece), lambda d: (0, d, 0)),
        ],
        out_specs=[pl.BlockSpec((half, cols), lambda d: (0, d))] * 2,
        out_shape=[
            jax.ShapeDtypeStruct((half, width), f32),
            jax.ShapeDtypeStruct((half, width), bf16),
        ],
        compiler_params=limits(40),
        cost_estimate=pl.CostEstimate(
            flops=4 * tokens * width * piece, bytes_accessed=4 * width * piece, transcendentals=0
        ),
        name="hidden_share",
    )(*in_hbm(gradient, pair))


def three_parts(value):
    high = lax.reduce_precision(value, 8, 7)
    rest = value - high
    middle = lax.reduce_precision(rest, 8, 7)
    return high, middle, rest - middle


def share_out(kept, arrived, found):
    rows, width = kept.shape
    count = lax.axis_size("ba")
    few = rows // count
    if few % 16:
        order = lax.axis_index("ba") ^ jnp.arange(count)
        summed = (kept + arrived.astype(f32)).astype(bf16).reshape(count, few, width)
        parts = jnp.stack(three_parts(jnp.sum(found))).astype(bf16)
        carried = jnp.zeros((few, lanes), bf16).at[0, :3].set(parts)
        return [jnp.concatenate([summed[order[s]], carried], axis=1) for s in range(count)]

    def kernel(kept_ref, arrived_ref, found_ref, *outs):
        me = lax.axis_index("ba")
        total = jnp.sum(found_ref[...], axis=0, keepdims=True)
        total = jnp.sum(total, axis=1, keepdims=True)
        high = total.astype(bf16).astype(f32)
        middle = (total - high).astype(bf16).astype(f32)
        low = total - high - middle
        lane = lax.broadcasted_iota(jnp.int32, (few, lanes), 1)
        lane = lane + lanes * lax.broadcasted_iota(jnp.int32, (few, lanes), 0)
        carried = jnp.where(lane == 0, high, jnp.where(lane == 1, middle, jnp.where(lane == 2, low, 0.0)))
        for s in range(count):
            at = pl.ds(pl.multiple_of((me ^ s) * few, few), few)
            outs[s][:, :width] = (kept_ref[at] + arrived_ref[at].astype(f32)).astype(bf16)
            outs[s][:, width:] = carried.astype(bf16)

    return pl.pallas_call(
        kernel,
        in_specs=[whole_vmem] * 3,
        out_specs=[whole_vmem] * count,
        out_shape=[jax.ShapeDtypeStruct((few, width + lanes), bf16)] * count,
        compiler_params=limits(20),
        name="share_out",
    )(kept, arrived, found)


def put_together(blocks):
    count = len(blocks)
    few, width = blocks[0].shape
    if few % 16:
        order = lax.axis_index("ba") ^ jnp.arange(count)
        return jnp.stack(blocks)[order].reshape(count * few, width)

    def kernel(*refs):
        me = lax.axis_index("ba")
        for s in range(count):
            at = pl.ds(pl.multiple_of((me ^ s) * few, few), few)
            refs[count][at, :] = refs[s][...]

    return pl.pallas_call(
        kernel,
        in_specs=[whole_vmem] * count,
        out_specs=whole_vmem,
        out_shape=jax.ShapeDtypeStruct((count * few, width), bf16),
        compiler_params=limits(20),
        name="put_together",
    )(*blocks)


def spread_features(hiddens):
    rows, width = hiddens[0].shape
    blocks = len(hiddens)
    tokens = rows * blocks
    share = width // blocks

    def kernel(*refs):
        given = refs[:blocks]
        left, held, sem = refs[blocks:]
        me = lax.axis_index("aa")
        def place(q):
            block = q // 2 * 2 + ((me % 2) ^ (q % 2))
            at = pl.ds(pl.multiple_of(block * rows, rows), rows)
            part = pl.ds(pl.multiple_of(me * share, share), share)
            return pltpu.make_async_copy(given[q].at[:, part], held.at[at], sem.at[q])

        for q in range(blocks):
            place(q).start()
        for q in range(blocks):
            place(q).wait()
        row = lax.broadcasted_iota(jnp.int32, (2 * lanes, lanes), 0)
        col = lax.broadcasted_iota(jnp.int32, (2 * lanes, lanes), 1)
        for i in range(2):
            spread = (row == 2 * col + i).astype(f32).astype(bf16)
            for d in range(0, share, lanes):
                left[2 * d : 2 * (d + lanes), i * tokens : (i + 1) * tokens] = lax.dot_general(
                    spread,
                    held[:, d : d + lanes],
                    (((1,), (1,)), ((), ())),
                    preferred_element_type=f32,
                ).astype(bf16)

    return pl.pallas_call(
        kernel,
        in_specs=[anywhere] * blocks,
        out_specs=whole_vmem,
        out_shape=jax.ShapeDtypeStruct((2 * share, 2 * tokens), bf16),
        scratch_shapes=[
            pltpu.VMEM((tokens, share), bf16),
            pltpu.SemaphoreType.DMA((blocks,)),
        ],
        compiler_params=limits(20),
        name="spread_features",
    )(*in_hbm(*hiddens))


def head_pair(left, own, other, partner, so_far):
    tokens = left.shape[1] // 2
    share = left.shape[0] // 2
    piece = own.shape[2]
    cols = largest_tile(piece, 512, lanes)
    steps = piece // cols
    aliased = [] if so_far is None else [so_far]

    def kernel(left_ref, own_ref, other_ref, *refs):
        out_ref, ready, out_sem = refs[len(aliased) :]
        step = pl.program_id(0)
        slot = lax.rem(step, 2)
        base = 2 * (my_pair() ^ partner)

        def store(k, s):
            at = pl.ds(pl.multiple_of(k * cols, cols), cols)
            return pltpu.make_async_copy(
                ready.at[s], out_ref.at[:, 0, pl.ds(base, 2), at], out_sem.at[s]
            )

        @pl.when(step >= 2)
        def _():
            store(step - 2, slot).wait()

        right = jnp.concatenate([own_ref[0], other_ref[0], own_ref[1], other_ref[1]], axis=0)
        for d in range(0, 2 * share, 512):
            made = jnp.dot(left_ref[d : d + 512], right, preferred_element_type=f32).astype(bf16)
            ready[slot, d // 2 : d // 2 + 256] = made.reshape(256, 2, cols)
        store(step, slot).start()

        @pl.when(step == steps - 1)
        def _():
            if steps > 1:
                store(step - 1, 1 - slot).wait()
            store(step, slot).wait()

    return pl.pallas_call(
        kernel,
        grid=(steps,),
        in_specs=[whole_vmem]
        + [pl.BlockSpec((2, tokens // 2, cols), lambda r: (0, 0, r))] * 2
        + [anywhere] * len(aliased),
        out_specs=anywhere,
        out_shape=jax.ShapeDtypeStruct((share, 1, 4, piece), bf16),
        scratch_shapes=[
            pltpu.VMEM((2, share, 2, cols), bf16),
            pltpu.SemaphoreType.DMA((2,)),
        ],
        input_output_aliases={3: 0} if aliased else {},
        compiler_params=limits(20),
        cost_estimate=pl.CostEstimate(
            flops=8 * share * tokens * piece, bytes_accessed=4 * share * piece, transcendentals=0
        ),
        name="head_pair",
    )(left, *in_hbm(own, other), *aliased)


def on_device(hidden, head_weight, teacher):
    me_a = lax.axis_index("aa")
    me_b = lax.axis_index("ba")
    count = lax.axis_size("ba")
    near = count // 2
    few = teacher.shape[0]
    width = hidden.shape[1]
    tokens = few * count
    chip, core = me_a // 2, me_a % 2

    side = exchange(hidden, "aa", 2)
    beside = exchange(hidden, "aa", 1)
    *blocks, teacher_stat = split_teacher(teacher)
    blocks, beside, head_weight = lax.optimization_barrier((blocks, beside, head_weight))
    middle = near + (count - near) * 3 // 4
    teacher_stats = [teacher_stat, exchange(teacher_stat, "aa", 2)]
    arrived = [exchange(block, "ba", s) if s else block for s, block in enumerate(blocks[:near])]
    pair = take_pair(head_weight)
    arrived, teacher_stats, early, side, pair = lax.optimization_barrier(
        (arrived, teacher_stats, blocks[near:middle], side, pair)
    )
    hiddens = [hidden, beside, side, exchange(side, "aa", 1)]
    arrived += [exchange(block, "ba", near + s) for s, block in enumerate(early)]

    def cross(parts):
        mine = jnp.concatenate(parts, axis=0)
        return [mine, exchange(mine, "aa", 2)]

    def swap(group):
        return group + [exchange(part, "aa", 1) for part in group]

    group_a = cross(arrived[:near])
    first, stat_first = student_logits(hiddens, pair, 0)
    late, first, stat_first, pair = lax.optimization_barrier(
        (blocks[middle:], first, stat_first, pair)
    )
    arrived += [exchange(late[s - middle], "ba", s) for s in range(middle, count)]
    second, stat_second = student_logits(hiddens, pair, 1)
    arrived[near:middle], stat_second = lax.optimization_barrier((arrived[near:middle], stat_second))
    packed = pack_stats([stat_first, stat_second], teacher_stats)
    group_a, packed = lax.optimization_barrier((group_a, packed))
    group_a = swap(group_a)
    packed = merge_two(packed, exchange(packed, "aa", 1))
    group_b = cross(arrived[near:middle])
    mask = 1
    while 2 * mask < count:
        met = exchange(packed, "ba", mask)
        if mask == 1:
            left = spread_features(hiddens)
            left, met = lax.optimization_barrier((left, met))
        packed = merge_two(packed, met)
        if 4 * mask == count:
            last_parts, packed = lax.optimization_barrier((arrived[middle:], packed))
            group_c = cross(last_parts)
        mask *= 2
    met = exchange(packed, "ba", mask)
    group_b, group_c, met = lax.optimization_barrier((group_b, group_c, met))
    group_b, group_c = swap(group_b), swap(group_c)
    sums = all_log_sums(packed, met)
    groups = [group_a, group_b, group_c]

    def plan(group):
        is_far = (me_b // near) ^ group
        step = jnp.arange(near)
        place = (me_b % near) ^ step
        short = middle - near
        kind = jnp.where(is_far == 0, 0, jnp.where(step < short, 1, 2))
        reads = [
            jnp.where(is_far == 0, step, 0),
            jnp.where(is_far == 1, jnp.minimum(step, short - 1), 0),
            jnp.where(is_far == 1, jnp.maximum(step - short, 0), 0),
        ]
        return jnp.concatenate(
            [place, place + near * group, *reads, kind, core[None]]
        ).astype(jnp.int32)

    students = [first, second]
    grad_own, found = logit_gradient(plan(chip), groups, students, *sums)
    kept, sent = hidden_share(grad_own, pair)
    shares = share_out(kept, exchange(sent, "aa", 1), found)
    own_met = exchange(grad_own, "aa", 1)
    sums, own_met, shares = lax.optimization_barrier((sums, own_met, shares))
    grad_other, _ = logit_gradient(plan(1 - chip), groups, students, *sums)
    reduced = [exchange(shares[s], "ba", s) for s in range(1, count)]
    reduced, grad_other = lax.optimization_barrier((reduced, grad_other))
    summed = shares[0].astype(f32)
    for part in reduced:
        summed = summed + part.astype(f32)
    divergence = jnp.sum(summed[:, width:])[None] / tokens
    summed = summed[:, :width].astype(bf16)

    other_met = exchange(grad_other, "aa", 1)
    divergence = divergence + exchange(divergence, "aa", 1)
    gathered = {s: exchange(summed, "ba", s) for s in range(near - 1, count)}
    grad_own, summed = lax.optimization_barrier((grad_own, summed))
    grad_head = head_pair(left, grad_own, grad_other, 0, None)
    summed, gathered, grad_head, divergence, other_met = lax.optimization_barrier(
        (summed, gathered, grad_head, divergence, other_met)
    )
    for s in range(1, near - 1):
        gathered[s] = exchange(summed, "ba", s)
    divergence = divergence + exchange(divergence, "aa", 2)
    grad_head = head_pair(left, own_met, other_met, 1, grad_head)
    gathered, grad_head = lax.optimization_barrier((gathered, grad_head))
    grad_hidden = put_together([summed] + [gathered[s] for s in range(1, count)])
    return divergence[0], grad_hidden, grad_head


def solution(mesh):
    placed = (P("aa", None), P(None, "ba", None, None), P("ba", "aa", None, None))
    return jax.shard_map(
        on_device,
        mesh=mesh,
        in_specs=placed,
        out_specs=(P(), P("aa", None), P("aa", "ba", None, None)),
        check_vma=False,
    )
```

time: 277 us -> 188 us (0.68)
  starting transfers between devices: 88 us -> 54.3 us
  waiting for transfers between devices: 53.9 us -> 25.1 us
  local copies, waits for them, and re-layouts: 23.5 us -> 9.5 us
  Pallas kernels: 101 us -> 92.1 us
    ppermute x42 -> x43, waiting for transfers between devices: 53.9 us -> 25.1 us  [exchange(): return lax.ppermute(value, axis, [(i, i ^ mask) for i in range(count)])]
    ppermute x2 -> x0, starting transfers between devices: 18.3 us -> none  [the longest x1 17.1 us: on_device(): own = lax.ppermute(mine, 'aa', [(0, 0), (1, 2), (2, 1), (3, 3)])]
    ppermute x42 -> x43, starting transfers between devices: 69.7 us -> 54.3 us  [exchange(): return lax.ppermute(value, axis, [(i, i ^ mask) for i in range(count)])]
    unnamed x79 -> x39, local copies, waits for them, and re-layouts: 22.7 us -> 7.87 us
    pallas_call x7 -> x12, Pallas kernels: 86.2 us -> 71.8 us  [the longest x2 23.8 us: student_logits(): pl.pallas_call(kernel, grid=(piece // cols,), in_specs=[anywhere] * block...]
    pallas_call x1 -> x2, Pallas kernels: 8.47 us -> 14.2 us  [logit_gradient(): pl.pallas_call(kernel, grid_spec=pltpu.PrefetchScalarGridSpec(num_scalar_...]
  transfers between devices with their start and end apart: 44 -> 43, of which waited for: 19 -> 12; matrix products, arithmetic and copies ran while one was open for 3% -> 4% of each run, Pallas kernels for 29% -> 45%
where the time goes in v2:
time: 188 us; the launch traced here: 187 us
  Pallas kernels  92.1 us (49%)
  starting transfers between devices  54.3 us (29%)
  waiting for transfers between devices  25.1 us (13%)
  local copies, waits for them, and re-layouts  9.5 us (5%)
  between operations  4.15 us (2%)
    ppermute x43, starting transfers between devices, exchange(): return lax.ppermute(value, axis, [(i, i ^ mask) for i in range(count)])  54.3 us
    ppermute x43, waiting for transfers between devices, exchange(): return lax.ppermute(value, axis, [(i, i ^ mask) for i in range(count)])  25.1 us
    pallas_call x2, Pallas kernels, student_logits(): pl.pallas_call(kernel, grid=(piece // cols,), in_specs=[anywhere] * block...  23.8 us
    pallas_call x2, Pallas kernels, head_pair(): pl.pallas_call(kernel, grid=(steps,), in_specs=[whole_vmem] + [pl.BlockSp...  19.3 us
    pallas_call x2, Pallas kernels, logit_gradient(): pl.pallas_call(kernel, grid_spec=pltpu.PrefetchScalarGridSpec(num_scalar_...  14.2 us
    pallas_call x1, Pallas kernels, hidden_share(): pl.pallas_call(kernel, grid=(width // cols,), in_specs=[pl.BlockSpec((2,...  12.9 us
    pallas_call x1, Pallas kernels, take_pair(): pl.pallas_call(kernel, in_specs=[anywhere], out_specs=whole_vmem, out_sha...  10.5 us
    unnamed x39, local copies, waits for them, and re-layouts  7.87 us
  transfers between devices with their start and end apart: 43, of which 12 were waited for; matrix products, arithmetic and copies ran while one was open for 4% of the time, Pallas kernels for 45%

profile of v2, /device:TPU:0, one launch (start us, length us, event | category | flops | bytes accessed | tf_op | source)
XLA Modules:
  0.0 187.1 jit_solution(10470132183186829966)
XLA Ops:
  1.1 2.6 %collective-permute-start.5 = (bf16[128,3072]{1,0:T(8,128)(2,1)}, bf16[128,3072]{1,0:T(8,128)(2,1)S(1)}, u32[]{:S(2)}, u32[]{:S(2)}) collective-permute-start(bf16[128,3072]{1,0:T(8,128)(2,1)} %refs_0_.5), channel_id=1, source_target_pairs={{0,16},{8,24},{16,0},{24,8},{1,17},{9,25},{17,1},{25,9},{2,18},{10... | collective-permute-start | bytes 2359304 | tf_op jit(solution)/shard_map/ppermute | solution.py:49
  3.7 5.2 %split_teacher.1 = (bf16[64,2048]{1,0:T(8,128)(2,1)}, bf16[64,2048]{1,0:T(8,128)(2,1)}, bf16[64,2048]{1,0:T(8,128)(2,1)}, bf16[64,2048]{1,0:T(8,128)(2,1)}, bf16...) custom-call(bf16[64,1,8,2048]{3,2,1,0:T(8,128)(2,1)} %in_ref.1), custom_call_target="tpu_custom_call" | custom-call | tf_op jit(solution)/shard_map/split_teacher/pallas_call | solution.py:105
  12.6 10.5 %take_pair.1.refs_4_.w_ref = bf16[2,3072,2048]{2,1,0:T(8,128)(2,1)S(1)} custom-call(bf16[3072,1,4,2048]{3,2,1,0:T(4,128)(2,1)} %w_ref), custom_call_target="tpu_custom_call" | custom-call | flops 12884901888 | bytes 25165824 | tf_op jit(solution)/shard_map/take_pair/pallas_call | solution.py:151
  24.5 2.7 %collective-permute-start.8 = (bf16[64,2048]{1,0:T(8,128)(2,1)S(1)}, bf16[64,2048]{1,0:T(8,128)(2,1)S(1)}, u32[]{:S(2)}, u32[]{:S(2)}) collective-permute-start(bf16[64,2048]{1,0:T(8,128)(2,1)S(1)} %copy-done.16), channel_id=1, source_target_pairs={{0,4},{1,5},{2,6},{3,7},{4,0},{5,1},{6,2},{7,3},{8,12},{9,13},{10,... | collective-permute-start | bytes 786440 | tf_op jit(solution)/shard_map/ppermute | solution.py:49
  28.5 3.6 %collective-permute-start.10 = (bf16[64,2048]{1,0:T(8,128)(2,1)S(1)}, bf16[64,2048]{1,0:T(8,128)(2,1)S(1)}, u32[]{:S(2)}, u32[]{:S(2)}) collective-permute-start(bf16[64,2048]{1,0:T(8,128)(2,1)S(1)} %copy-done.14), channel_id=1, source_target_pairs={{0,6},{1,7},{2,4},{3,5},{4,2},{5,3},{6,0},{7,1},{8,14},{9,15},{10,... | collective-permute-start | bytes 786440 | tf_op jit(solution)/shard_map/ppermute | solution.py:49
  37.4 11.8 %student_logits.2 = (f32[512,2048]{1,0:T(8,128)}, f32[8,512]{1,0:T(8,128)S(1)}) custom-call(bf16[128,3072]{1,0:T(8,128)(2,1)} %refs_0_.5, bf16[128,3072]{1,0:T(8,128)(2,1)} %copy-done.3, bf16[128,3072]{1,0:T(8,128)(2,1)} %copy-done.4, bf16[128,3072]{1,0:T(8,128)(2,1)} %copy-done.5, bf16[2,3072,2048]{2,1,0:T(8,128)(2,1)S(1)} %take_pair.1.refs_4_.w_ref), custom_call_target="tpu_custom_call" | custom-call | flops 1 | bytes 1 | tf_op jit(solution)/shard_map/student_logits/pallas_call | solution.py:220
  49.2 12.0 %student_logits.3 = (f32[512,2048]{1,0:T(8,128)}, f32[8,512]{1,0:T(8,128)S(1)}) custom-call(bf16[128,3072]{1,0:T(8,128)(2,1)} %refs_0_.5, bf16[128,3072]{1,0:T(8,128)(2,1)} %copy-done.3, bf16[128,3072]{1,0:T(8,128)(2,1)} %copy-done.4, bf16[128,3072]{1,0:T(8,128)(2,1)} %copy-done.5, bf16[2,3072,2048]{2,1,0:T(8,128)(2,1)S(1)} %take_pair.1.refs_4_.w_ref), custom_call_target="tpu_custom_call" | custom-call | flops 1 | bytes 1 | tf_op jit(solution)/shard_map/student_logits/pallas_call | solution.py:220
  64.0 2.7 %collective-permute-start.14 = (bf16[64,2048]{1,0:T(8,128)(2,1)S(1)}, bf16[64,2048]{1,0:T(8,128)(2,1)S(1)}, u32[]{:S(2)}, u32[]{:S(2)}) collective-permute-start(bf16[64,2048]{1,0:T(8,128)(2,1)S(1)} %copy-done.13), channel_id=1, source_target_pairs={{0,7},{1,6},{2,5},{3,4},{4,3},{5,2},{6,1},{7,0},{8,15},{9,14},{10,... | collective-permute-start | bytes 786440 | tf_op jit(solution)/shard_map/ppermute | solution.py:49
  71.2 4.1 %collective-permute-done.16.b_ref = f32[8,512]{1,0:T(8,128)S(1)} collective-permute-done((f32[8,512]{1,0:T(8,128)S(1)}, f32[8,512]{1,0:T(8,128)S(1)}, u32[]{:S(2)}, u32[]{:S(2)}) %collective-permute-start.16) | collective-permute-done | bytes 16416 | tf_op jit(solution)/shard_map/ppermute | solution.py:49
  75.4 3.7 %collective-permute-done.17.b_ref = f32[8,512]{1,0:T(8,128)S(1)} collective-permute-done((f32[8,512]{1,0:T(8,128)S(1)}, f32[8,512]{1,0:T(8,128)S(1)}, u32[]{:S(2)}, u32[]{:S(2)}) %collective-permute-start.17) | collective-permute-done | bytes 16416 | tf_op jit(solution)/shard_map/ppermute | solution.py:49
  82.3 3.6 %collective-permute-done.19.b_ref = f32[8,512]{1,0:T(8,128)S(1)} collective-permute-done((f32[8,512]{1,0:T(8,128)S(1)}, f32[8,512]{1,0:T(8,128)S(1)}, u32[]{:S(2)}, u32[]{:S(2)}) %collective-permute-start.19) | collective-permute-done | bytes 16416 | tf_op jit(solution)/shard_map/ppermute | solution.py:49
  85.9 3.1 %collective-permute-done.18.refs_9_ = bf16[64,2048]{1,0:T(8,128)(2,1)S(1)} collective-permute-done((bf16[64,2048]{1,0:T(8,128)(2,1)S(1)}, bf16[64,2048]{1,0:T(8,128)(2,1)S(1)}, u32[]{:S(2)}, u32[]{:S(2)}) %collective-permute-start.18) | collective-permute-done | bytes 262176 | tf_op jit(solution)/shard_map/ppermute | solution.py:49
  90.2 2.3 %collective-permute-done.22.refs_10_ = bf16[64,2048]{1,0:T(8,128)(2,1)} collective-permute-done((bf16[64,2048]{1,0:T(8,128)(2,1)S(1)}, bf16[64,2048]{1,0:T(8,128)(2,1)}, u32[]{:S(2)}, u32[]{:S(2)}) %collective-permute-start.22) | collective-permute-done | bytes 262176 | tf_op jit(solution)/shard_map/ppermute | solution.py:49
  94.4 7.2 %logit_gradient.2 = (bf16[2,256,2048]{2,1,0:T(8,128)(2,1)}, f32[8,128]{1,0:T(8,128)S(1)}) custom-call(s32[25]{0:T(128)S(1)} %concatenate.12.plan_ref, bf16[256,2048]{1,0:T(8,128)(2,1)} %constant_dynamic-update-slice_fusion.refs_0_, bf16[256,2048]{1,0:T(8,128)(2,1)} %collective-permute-done.6.refs_1_, bf16[256,2048]{1,0:T(8,128)(2,1)} %collective-permute-done.11.refs_2_, ...), custom_call_target="tpu_custom_call" | custom-call | flops 4194304 | bytes 8388608 | tf_op jit(solution)/shard_map/logit_gradient/pallas_call | solution.py:374
  102.0 12.9 %hidden_share.1 = (f32[128,3072]{1,0:T(8,128)S(1)}, bf16[128,3072]{1,0:T(8,128)(2,1)}) custom-call(bf16[2,256,2048]{2,1,0:T(8,128)(2,1)} %get-tuple-element.197.g_ref.own_ref, bf16[2,3072,2048]{2,1,0:T(8,128)(2,1)} %copy-done), custom_call_target="tpu_custom_call" | custom-call | flops 6442450944 | bytes 25165824 | tf_op jit(solution)/shard_map/hidden_share/pallas_call | solution.py:430
  116.3 2.4 %collective-permute-done.25.arrived_ref = bf16[128,3072]{1,0:T(8,128)(2,1)} collective-permute-done((bf16[128,3072]{1,0:T(8,128)(2,1)}, bf16[128,3072]{1,0:T(8,128)(2,1)}, u32[]{:S(2)}, u32[]{:S(2)}) %collective-permute-start.25) | collective-permute-done | bytes 786464 | tf_op jit(solution)/shard_map/ppermute | solution.py:49
  130.5 2.8 %collective-permute-start.32 = (bf16[16,3200]{1,0:T(8,128)(2,1)S(1)}, bf16[16,3200]{1,0:T(8,128)(2,1)}, u32[]{:S(2)}, u32[]{:S(2)}) collective-permute-start(bf16[16,3200]{1,0:T(8,128)(2,1)S(1)} %get-tuple-element.184), channel_id=1, source_target_pairs={{0,7},{1,6},{2,5},{3,4},{4,3},{5,2},{6,1},{7,0},{8,15},{9,14},{10,... | collective-permute-start | bytes 307208 | tf_op jit(solution)/shard_map/ppermute | solution.py:49
  133.4 7.0 %logit_gradient.3 = (bf16[2,256,2048]{2,1,0:T(8,128)(2,1)}, f32[8,128]{1,0:T(8,128)}) custom-call(s32[25]{0:T(128)S(1)} %concatenate.15.plan_ref, bf16[256,2048]{1,0:T(8,128)(2,1)} %constant_dynamic-update-slice_fusion.refs_0_, bf16[256,2048]{1,0:T(8,128)(2,1)} %collective-permute-done.6.refs_1_, bf16[256,2048]{1,0:T(8,128)(2,1)} %collective-permute-done.11.refs_2_, ...), custom_call_target="tpu_custom_call" | custom-call | flops 4194304 | bytes 8388608 | tf_op jit(solution)/shard_map/logit_gradient/pallas_call | solution.py:374
  144.4 2.3 %collective-permute-start.36 = (bf16[16,3072]{1,0:T(8,128)(2,1)S(1)}, bf16[16,3072]{1,0:T(8,128)(2,1)S(1)}, u32[]{:S(2)}, u32[]{:S(2)}) collective-permute-start(bf16[16,3072]{1,0:T(8,128)(2,1)S(1)} %slice.13.refs_0_), channel_id=1, source_target_pairs={{0,6},{1,7},{2,4},{3,5},{4,2},{5,3},{6,0},{7,1},{8,14},{9,15},{10,... | collective-permute-start | bytes 294920 | tf_op jit(solution)/shard_map/ppermute | solution.py:49
  146.7 4.3 %collective-permute-start.35 = (bf16[16,3072]{1,0:T(8,128)(2,1)S(1)}, bf16[16,3072]{1,0:T(8,128)(2,1)S(1)}, u32[]{:S(2)}, u32[]{:S(2)}) collective-permute-start(bf16[16,3072]{1,0:T(8,128)(2,1)S(1)} %slice.13.refs_0_), channel_id=1, source_target_pairs={{0,5},{1,4},{2,7},{3,6},{4,1},{5,0},{6,3},{7,2},{8,13},{9,12},{10,... | collective-permute-start | bytes 294920 | tf_op jit(solution)/shard_map/ppermute | solution.py:49
  155.8 3.0 %collective-permute-start.37 = (bf16[16,3072]{1,0:T(8,128)(2,1)S(1)}, bf16[16,3072]{1,0:T(8,128)(2,1)S(1)}, u32[]{:S(2)}, u32[]{:S(2)}) collective-permute-start(bf16[16,3072]{1,0:T(8,128)(2,1)S(1)} %slice.13.refs_0_), channel_id=1, source_target_pairs={{0,7},{1,6},{2,5},{3,4},{4,3},{5,2},{6,1},{7,0},{8,15},{9,14},{10,... | collective-permute-start | bytes 294920 | tf_op jit(solution)/shard_map/ppermute | solution.py:49
  158.8 9.7 %head_pair.2.refs_0_ = bf16[768,1,4,2048]{3,2,1,0:T(4,128)(2,1)} custom-call(bf16[1536,1024]{1,0:T(8,128)(2,1)S(1)} %spread_features.1.left_ref, bf16[2,256,2048]{2,1,0:T(8,128)(2,1)} %get-tuple-element.197.g_ref.own_ref, bf16[2,256,2048]{2,1,0:T(8,128)(2,1)} %get-tuple-element.198.other_ref), custom_call_target="tpu_custom_call" | custom-call | flops 6442450944 | bytes 6291456 | tf_op jit(solution)/shard_map/head_pair/pallas_call | solution.py:598
  171.7 3.0 %collective-permute-start.40 = (f32[1]{0:T(128)}, f32[1]{0:T(128)}, u32[]{:S(2)}, u32[]{:S(2)}) collective-permute-start(f32[1]{0:T(128)} %add.63), channel_id=1, source_target_pairs={{0,16},{8,24},{16,0},{24,8},{1,17},{9,25},{17,1},{25,9},{2,18},{10... | collective-permute-start | bytes 20 | tf_op jit(solution)/shard_map/ppermute | solution.py:49
  174.7 9.7 %head_pair.3 = bf16[768,1,4,2048]{3,2,1,0:T(4,128)(2,1)} custom-call(bf16[1536,1024]{1,0:T(8,128)(2,1)S(1)} %spread_features.1.left_ref, bf16[2,256,2048]{2,1,0:T(8,128)(2,1)} %collective-permute-done.24.own_ref, bf16[2,256,2048]{2,1,0:T(8,128)(2,1)} %collective-permute-done.39.other_ref, ...), custom_call_target="tpu_custom_call", output_to_operand_aliasing={{}: (3, {})} | custom-call | flops 6442450944 | bytes 6291456 | tf_op jit(solution)/shard_map/head_pair/pallas_call | solution.py:598
  (131 shorter events, 50.8 us)
Async XLA Ops:
  1.1 22.1 %collective-permute-start.5 = (bf16[128,3072]{1,0:T(8,128)(2,1)}, bf16[128,3072]{1,0:T(8,128)(2,1)S(1)}, u32[]{:S(2)}, u32[]{:S(2)}) collective-permute-start(bf16[128,3072]{1,0:T(8,128)(2,1)} %refs_0_.5), channel_id=1, source_target_pairs={{0,16},{8,24},{16,0},{24,8},{1,17},{9,25},{17,1},{25,9},{2,18},{10... | collective-permute-start | bytes 2359304 | tf_op jit(solution)/shard_map/ppermute | solution.py:49
  8.9 14.3 %collective-permute-start.4 = (f32[8,512]{1,0:T(8,128)S(1)}, f32[8,512]{1,0:T(8,128)S(1)}, u32[]{:S(2)}, u32[]{:S(2)}) collective-permute-start(f32[8,512]{1,0:T(8,128)S(1)} %get-tuple-element.144.refs_2_), channel_id=1, source_target_pairs={{0,16},{8,24},{16,0},{24,8},{1,17},{9,25},{17,1},{25,9},{2,18},{10... | collective-permute-start | bytes 49160 | tf_op jit(solution)/shard_map/ppermute | solution.py:49
  9.0 14.3 %collective-permute-start.1 = (bf16[64,2048]{1,0:T(8,128)(2,1)}, bf16[64,2048]{1,0:T(8,128)(2,1)S(1)}, u32[]{:S(2)}, u32[]{:S(2)}) collective-permute-start(bf16[64,2048]{1,0:T(8,128)(2,1)} %get-tuple-element.119), channel_id=1, source_target_pairs={{0,1},{1,0},{2,3},{3,2},{4,5},{5,4},{6,7},{7,6},{8,9},{9,8},{10,11... | collective-permute-start | bytes 786440 | tf_op jit(solution)/shard_map/ppermute | solution.py:49
  24.5 36.8 %collective-permute-start.8 = (bf16[64,2048]{1,0:T(8,128)(2,1)S(1)}, bf16[64,2048]{1,0:T(8,128)(2,1)S(1)}, u32[]{:S(2)}, u32[]{:S(2)}) collective-permute-start(bf16[64,2048]{1,0:T(8,128)(2,1)S(1)} %copy-done.16), channel_id=1, source_target_pairs={{0,4},{1,5},{2,6},{3,7},{4,0},{5,1},{6,2},{7,3},{8,12},{9,13},{10,... | collective-permute-start | bytes 786440 | tf_op jit(solution)/shard_map/ppermute | solution.py:49
  27.2 34.0 %collective-permute-start.9 = (bf16[64,2048]{1,0:T(8,128)(2,1)S(1)}, bf16[64,2048]{1,0:T(8,128)(2,1)S(1)}, u32[]{:S(2)}, u32[]{:S(2)}) collective-permute-start(bf16[64,2048]{1,0:T(8,128)(2,1)S(1)} %copy-done.15), channel_id=1, source_target_pairs={{0,5},{1,4},{2,7},{3,6},{4,1},{5,0},{6,3},{7,2},{8,13},{9,12},{10,... | collective-permute-start | bytes 786440 | tf_op jit(solution)/shard_map/ppermute | solution.py:49
  28.5 32.7 %collective-permute-start.10 = (bf16[64,2048]{1,0:T(8,128)(2,1)S(1)}, bf16[64,2048]{1,0:T(8,128)(2,1)S(1)}, u32[]{:S(2)}, u32[]{:S(2)}) collective-permute-start(bf16[64,2048]{1,0:T(8,128)(2,1)S(1)} %copy-done.14), channel_id=1, source_target_pairs={{0,6},{1,7},{2,4},{3,5},{4,2},{5,3},{6,0},{7,1},{8,14},{9,15},{10,... | collective-permute-start | bytes 786440 | tf_op jit(solution)/shard_map/ppermute | solution.py:49
  35.0 31.6 %collective-permute-start.6 = (bf16[256,2048]{1,0:T(8,128)(2,1)}, bf16[256,2048]{1,0:T(8,128)(2,1)}, u32[]{:S(2)}, u32[]{:S(2)}) collective-permute-start(bf16[256,2048]{1,0:T(8,128)(2,1)} %constant_dynamic-update-slice_fusion.refs_0_), channel_id=1, source_target_pairs={{0,16},{8,24},{16,0},{24,8},{1,17},{9,25},{17,1},{25,9},{2,18},{10... | collective-permute-start | bytes 3145736 | tf_op jit(solution)/shard_map/ppermute | solution.py:49
  63.4 25.5 %collective-permute-start.13 = (bf16[192,2048]{1,0:T(8,128)(2,1)}, bf16[192,2048]{1,0:T(8,128)(2,1)}, u32[]{:S(2)}, u32[]{:S(2)}) collective-permute-start(bf16[192,2048]{1,0:T(8,128)(2,1)} %constant_dynamic-update-slice_fusion.4.refs_4_), channel_id=1, source_target_pairs={{0,16},{8,24},{16,0},{24,8},{1,17},{9,25},{17,1},{25,9},{2,18},{10... | collective-permute-start | bytes 2359304 | tf_op jit(solution)/shard_map/ppermute | solution.py:49
  64.0 15.2 %collective-permute-start.14 = (bf16[64,2048]{1,0:T(8,128)(2,1)S(1)}, bf16[64,2048]{1,0:T(8,128)(2,1)S(1)}, u32[]{:S(2)}, u32[]{:S(2)}) collective-permute-start(bf16[64,2048]{1,0:T(8,128)(2,1)S(1)} %copy-done.13), channel_id=1, source_target_pairs={{0,7},{1,6},{2,5},{3,4},{4,3},{5,2},{6,1},{7,0},{8,15},{9,14},{10,... | collective-permute-start | bytes 786440 | tf_op jit(solution)/shard_map/ppermute | solution.py:49
  80.7 13.7 %collective-permute-start.11 = (bf16[256,2048]{1,0:T(8,128)(2,1)}, bf16[256,2048]{1,0:T(8,128)(2,1)}, u32[]{:S(2)}, u32[]{:S(2)}) collective-permute-start(bf16[256,2048]{1,0:T(8,128)(2,1)} %constant_dynamic-update-slice_fusion.refs_0_), channel_id=1, source_target_pairs={{0,8},{8,0},{16,24},{24,16},{1,9},{9,1},{17,25},{25,17},{2,10},{10... | collective-permute-start | bytes 3145736 | tf_op jit(solution)/shard_map/ppermute | solution.py:49
  80.7 13.7 %collective-permute-start.12 = (bf16[256,2048]{1,0:T(8,128)(2,1)}, bf16[256,2048]{1,0:T(8,128)(2,1)}, u32[]{:S(2)}, u32[]{:S(2)}) collective-permute-start(bf16[256,2048]{1,0:T(8,128)(2,1)} %collective-permute-done.6.refs_1_), channel_id=1, source_target_pairs={{0,8},{8,0},{16,24},{24,16},{1,9},{9,1},{17,25},{25,17},{2,10},{10... | collective-permute-start | bytes 3145736 | tf_op jit(solution)/shard_map/ppermute | solution.py:49
  101.6 20.5 %collective-permute-start.24 = (bf16[2,256,2048]{2,1,0:T(8,128)(2,1)}, bf16[2,256,2048]{2,1,0:T(8,128)(2,1)}, u32[]{:S(2)}, u32[]{:S(2)}) collective-permute-start(bf16[2,256,2048]{2,1,0:T(8,128)(2,1)} %get-tuple-element.197.g_ref.own_ref), channel_id=1, source_target_pairs={{0,8},{8,0},{16,24},{24,16},{1,9},{9,1},{17,25},{25,17},{2,10},{10... | collective-permute-start | bytes 6291464 | tf_op jit(solution)/shard_map/ppermute | solution.py:49
  123.4 17.0 %collective-permute-start.28 = (bf16[16,3200]{1,0:T(8,128)(2,1)}, bf16[16,3200]{1,0:T(8,128)(2,1)}, u32[]{:S(2)}, u32[]{:S(2)}) collective-permute-start(bf16[16,3200]{1,0:T(8,128)(2,1)} %get-tuple-element.180), channel_id=1, source_target_pairs={{0,3},{1,2},{2,1},{3,0},{4,7},{5,6},{6,5},{7,4},{8,11},{9,10},{10,... | collective-permute-start | bytes 307208 | tf_op jit(solution)/shard_map/ppermute | solution.py:49
  125.6 15.4 %collective-permute-start.29 = (bf16[16,3200]{1,0:T(8,128)(2,1)}, bf16[16,3200]{1,0:T(8,128)(2,1)}, u32[]{:S(2)}, u32[]{:S(2)}) collective-permute-start(bf16[16,3200]{1,0:T(8,128)(2,1)} %get-tuple-element.181), channel_id=1, source_target_pairs={{0,4},{1,5},{2,6},{3,7},{4,0},{5,1},{6,2},{7,3},{8,12},{9,13},{10,... | collective-permute-start | bytes 307208 | tf_op jit(solution)/shard_map/ppermute | solution.py:49
  127.0 16.1 %collective-permute-start.30 = (bf16[16,3200]{1,0:T(8,128)(2,1)}, bf16[16,3200]{1,0:T(8,128)(2,1)}, u32[]{:S(2)}, u32[]{:S(2)}) collective-permute-start(bf16[16,3200]{1,0:T(8,128)(2,1)} %get-tuple-element.182), channel_id=1, source_target_pairs={{0,5},{1,4},{2,7},{3,6},{4,1},{5,0},{6,3},{7,2},{8,13},{9,12},{10,... | collective-permute-start | bytes 307208 | tf_op jit(solution)/shard_map/ppermute | solution.py:49
  128.5 14.7 %collective-permute-start.31 = (bf16[16,3200]{1,0:T(8,128)(2,1)S(1)}, bf16[16,3200]{1,0:T(8,128)(2,1)}, u32[]{:S(2)}, u32[]{:S(2)}) collective-permute-start(bf16[16,3200]{1,0:T(8,128)(2,1)S(1)} %get-tuple-element.183), channel_id=1, source_target_pairs={{0,6},{1,7},{2,4},{3,5},{4,2},{5,3},{6,0},{7,1},{8,14},{9,15},{10,... | collective-permute-start | bytes 307208 | tf_op jit(solution)/shard_map/ppermute | solution.py:49
  130.5 12.7 %collective-permute-start.32 = (bf16[16,3200]{1,0:T(8,128)(2,1)S(1)}, bf16[16,3200]{1,0:T(8,128)(2,1)}, u32[]{:S(2)}, u32[]{:S(2)}) collective-permute-start(bf16[16,3200]{1,0:T(8,128)(2,1)S(1)} %get-tuple-element.184), channel_id=1, source_target_pairs={{0,7},{1,6},{2,5},{3,4},{4,3},{5,2},{6,1},{7,0},{8,15},{9,14},{10,... | collective-permute-start | bytes 307208 | tf_op jit(solution)/shard_map/ppermute | solution.py:49
  143.2 26.0 %collective-permute-start.39 = (bf16[2,256,2048]{2,1,0:T(8,128)(2,1)}, bf16[2,256,2048]{2,1,0:T(8,128)(2,1)}, u32[]{:S(2)}, u32[]{:S(2)}) collective-permute-start(bf16[2,256,2048]{2,1,0:T(8,128)(2,1)} %get-tuple-element.198.other_ref), channel_id=1, source_target_pairs={{0,8},{8,0},{16,24},{24,16},{1,9},{9,1},{17,25},{25,17},{2,10},{10... | collective-permute-start | bytes 6291464 | tf_op jit(solution)/shard_map/ppermute | solution.py:49
  146.7 22.4 %collective-permute-start.35 = (bf16[16,3072]{1,0:T(8,128)(2,1)S(1)}, bf16[16,3072]{1,0:T(8,128)(2,1)S(1)}, u32[]{:S(2)}, u32[]{:S(2)}) collective-permute-start(bf16[16,3072]{1,0:T(8,128)(2,1)S(1)} %slice.13.refs_0_), channel_id=1, source_target_pairs={{0,5},{1,4},{2,7},{3,6},{4,1},{5,0},{6,3},{7,2},{8,13},{9,12},{10,... | collective-permute-start | bytes 294920 | tf_op jit(solution)/shard_map/ppermute | solution.py:49
  151.1 18.1 %collective-permute-start.34 = (bf16[16,3072]{1,0:T(8,128)(2,1)S(1)}, bf16[16,3072]{1,0:T(8,128)(2,1)S(1)}, u32[]{:S(2)}, u32[]{:S(2)}) collective-permute-start(bf16[16,3072]{1,0:T(8,128)(2,1)S(1)} %slice.13.refs_0_), channel_id=1, source_target_pairs={{0,4},{1,5},{2,6},{3,7},{4,0},{5,1},{6,2},{7,3},{8,12},{9,13},{10,... | collective-permute-start | bytes 294920 | tf_op jit(solution)/shard_map/ppermute | solution.py:49
  153.5 15.7 %collective-permute-start.33 = (bf16[16,3072]{1,0:T(8,128)(2,1)S(1)}, bf16[16,3072]{1,0:T(8,128)(2,1)S(1)}, u32[]{:S(2)}, u32[]{:S(2)}) collective-permute-start(bf16[16,3072]{1,0:T(8,128)(2,1)S(1)} %slice.13.refs_0_), channel_id=1, source_target_pairs={{0,3},{1,2},{2,1},{3,0},{4,7},{5,6},{6,5},{7,4},{8,11},{9,10},{10,... | collective-permute-start | bytes 294920 | tf_op jit(solution)/shard_map/ppermute | solution.py:49
  155.8 13.4 %collective-permute-start.37 = (bf16[16,3072]{1,0:T(8,128)(2,1)S(1)}, bf16[16,3072]{1,0:T(8,128)(2,1)S(1)}, u32[]{:S(2)}, u32[]{:S(2)}) collective-permute-start(bf16[16,3072]{1,0:T(8,128)(2,1)S(1)} %slice.13.refs_0_), channel_id=1, source_target_pairs={{0,7},{1,6},{2,5},{3,4},{4,3},{5,2},{6,1},{7,0},{8,15},{9,14},{10,... | collective-permute-start | bytes 294920 | tf_op jit(solution)/shard_map/ppermute | solution.py:49
  169.2 15.8 %collective-permute-start.42 = (bf16[16,3072]{1,0:T(8,128)(2,1)S(1)}, bf16[16,3072]{1,0:T(8,128)(2,1)S(1)}, u32[]{:S(2)}, u32[]{:S(2)}) collective-permute-start(bf16[16,3072]{1,0:T(8,128)(2,1)S(1)} %slice.13.refs_0_), channel_id=1, source_target_pairs={{0,2},{1,3},{2,0},{3,1},{4,6},{5,7},{6,4},{7,5},{8,10},{9,11},{10,... | collective-permute-start | bytes 294920 | tf_op jit(solution)/shard_map/ppermute | solution.py:49
  169.5 15.5 %collective-permute-start.41 = (bf16[16,3072]{1,0:T(8,128)(2,1)S(1)}, bf16[16,3072]{1,0:T(8,128)(2,1)S(1)}, u32[]{:S(2)}, u32[]{:S(2)}) collective-permute-start(bf16[16,3072]{1,0:T(8,128)(2,1)S(1)} %slice.13.refs_0_), channel_id=1, source_target_pairs={{0,1},{1,0},{2,3},{3,2},{4,5},{5,4},{6,7},{7,6},{8,9},{9,8},{10,11... | collective-permute-start | bytes 294920 | tf_op jit(solution)/shard_map/ppermute | solution.py:49
  (36 other events, 312.2 us)

commit v3 on v2

--- a/solution.py
+++ b/solution.py
@@ -51,6 +51,34 @@
 
 def lane_row(column, rows):
     return jnp.transpose(jnp.broadcast_to(column, (rows, lanes)))[0:1]
+
+
+def join(parts):
+    starts = [sum(part.shape[0] for part in parts[:n]) for n in range(len(parts))]
+    total = starts[-1] + parts[-1].shape[0]
+    if any(part.shape[0] % 16 for part in parts):
+        return jnp.concatenate(parts, axis=0)
+
+    def kernel(*refs):
+        given, (out_ref, sem) = refs[: len(parts)], refs[len(parts) :]
+        copies = [
+            pltpu.make_async_copy(ref, out_ref.at[pl.ds(start, ref.shape[0])], sem.at[n])
+            for n, (ref, start) in enumerate(zip(given, starts))
+        ]
+        for copy in copies:
+            copy.start()
+        for copy in copies:
+            copy.wait()
+
+    return pl.pallas_call(
+        kernel,
+        in_specs=[anywhere] * len(parts),
+        out_specs=anywhere,
+        out_shape=pltpu.HBM((total, parts[0].shape[1]), bf16),
+        scratch_shapes=[pltpu.SemaphoreType.DMA((len(parts),))],
+        compiler_params=limits(4),
+        name="join",
+    )(*parts)
 
 
 def split_teacher(teacher):
@@ -167,20 +195,22 @@
     )(head_weight)
 
 
-def student_logits(hiddens, pair, which):
+def student_logits(hiddens, pair):
     rows, width = hiddens[0].shape
     blocks = len(hiddens)
     tokens = rows * blocks
     piece = pair.shape[2]
-    cols = largest_tile(piece, 512, lanes)
+    cols = largest_tile(piece, 1024, lanes)
+    part = largest_tile(cols, 256, lanes)
 
     def kernel(*refs):
         given, w_ref = refs[:blocks], refs[blocks]
         out_ref, stat_ref, left, peak_ref, total_ref, sem = refs[blocks + 1 :]
-        step = pl.program_id(0)
+        first = (pl.program_id(0) == 0) & (pl.program_id(1) == 0)
+        last = (pl.program_id(0) == 1) & (pl.program_id(1) == pl.num_programs(1) - 1)
         me = lax.axis_index("aa")
 
-        @pl.when(step == 0)
+        @pl.when(first)
         def _():
             def place(q):
                 at = pl.ds(pl.multiple_of((me ^ q) * rows, rows), rows)
@@ -193,22 +223,28 @@
             for q in range(blocks):
                 place(q).wait()
 
-        at = pl.ds(pl.multiple_of(step * cols, cols), cols)
-        out_ref[...] = jnp.dot(left[...], w_ref[which, :, at], preferred_element_type=f32)
-
-        @pl.loop(0, tokens // 64)
-        def _(k):
-            at = pl.ds(pl.multiple_of(k * 64, 64), 64)
-            parts = [out_ref[at, j : j + lanes] for j in range(0, cols, lanes)]
-            old = peak_ref[at]
-            new = functools.reduce(jnp.maximum, parts, old)
-            total = total_ref[at] * jnp.exp(old - new)
-            for part in parts:
-                total = total + jnp.exp(part - new)
-            peak_ref[at] = new
-            total_ref[at] = total
-
-        @pl.when(step == pl.num_programs(0) - 1)
+        def collect(start):
+            for k in range(0, tokens, 64):
+                at = pl.ds(k, 64)
+                parts = [out_ref[0, at, j : j + lanes] for j in range(start, start + part, lanes)]
+                old = peak_ref[at]
+                new = functools.reduce(jnp.maximum, parts, old)
+                total = total_ref[at] * jnp.exp(old - new)
+                for value in parts:
+                    total = total + jnp.exp(value - new)
+                peak_ref[at] = new
+                total_ref[at] = total
+
+        for n in range(0, cols, part):
+            at = pl.ds(pl.multiple_of(pl.program_id(1) * cols + n, part), part)
+            out_ref[0, :, n : n + part] = jnp.dot(
+                left[...], w_ref[pl.program_id(0), :, at], preferred_element_type=f32
+            )
+            if n:
+                collect(n - part)
+        collect(cols - part)
+
+        @pl.when(last)
         def _():
             peak = peak_ref[...]
             top = jnp.max(peak, axis=1, keepdims=True)
@@ -219,15 +255,15 @@
 
     return pl.pallas_call(
         kernel,
-        grid=(piece // cols,),
+        grid=(2, piece // cols),
         in_specs=[anywhere] * blocks
         + [whole_vmem],
         out_specs=[
-            pl.BlockSpec((tokens, cols), lambda r: (0, r)),
-            pl.BlockSpec((8, tokens), lambda r: (0, 0)),
+            pl.BlockSpec((1, tokens, cols), lambda i, r: (i, 0, r)),
+            pl.BlockSpec((8, tokens), lambda i, r: (0, 0)),
         ],
         out_shape=[
-            pltpu.HBM((tokens, piece), f32),
+            pltpu.HBM((2, tokens, piece), f32),
             jax.ShapeDtypeStruct((8, tokens), f32),
         ],
         scratch_shapes=[
@@ -313,77 +349,93 @@
     )(first, second)
 
 
-def logit_gradient(plan, groups, students, student_sum, teacher_sum):
-    kinds = len(groups)
-    count = (plan.shape[0] - 1) // (3 + kinds)
-    tokens, piece = students[0].shape
+def logit_gradient(plan, groups, student, student_sum, teacher_sum):
+    count = (plan.shape[0] - 3) // 2
+    _, tokens, piece = student.shape
     half = tokens // 2
-    few = half // count
+    few = tokens // count
+    per = 2 if count // 2 % 2 == 0 else 1
+    steps = count // 2 // per
     cols = largest_tile(piece, 512, lanes)
     rows = 16
 
     def kernel(plan_ref, *refs):
-        teachers, s_refs = refs[: 4 * kinds], refs[4 * kinds : 4 * kinds + 2]
-        ssum_ref, tsum_ref = refs[4 * kinds + 2 : 4 * kinds + 4]
-        g_ref, div_ref = refs[-2:]
+        teachers = [refs[4 * n : 4 * n + 4] for n in range(len(groups))]
+        s_ref, ssum_ref, tsum_ref, g_ref, div_ref, held, sem = refs[4 * len(groups) :]
         step = pl.program_id(0)
-        kind = plan_ref[(2 + kinds) * count + step]
-        core = plan_ref[(3 + kinds) * count]
+        slot = lax.rem(step, 2)
+        core = plan_ref[2]
+
+        def fetch(k, to):
+            for m in range(per):
+                s = (plan_ref[0] + k * per + m) ^ plan_ref[1]
+                block = pl.ds(pl.multiple_of(plan_ref[3 + s] * few, few), few)
+                for n, (own, side, own_met, side_met) in enumerate(teachers):
+                    for at_core, ordered in enumerate(((own, own_met), (side_met, side))):
+
+                        @pl.when((plan_ref[3 + count + s] == n) & (core == at_core))
+                        def _(ordered=ordered, block=block, m=m):
+                            for i in range(2):
+                                pltpu.make_async_copy(
+                                    ordered[i].at[block],
+                                    held.at[to, i, pl.ds(m * few, few)],
+                                    sem.at[to, i, m],
+                                ).start()
 
         @pl.when(step == 0)
         def _():
             div_ref[...] = jnp.zeros_like(div_ref)
-
-        def work(ordered):
-            @pl.loop(0, few // rows)
-            def _(k):
-                at = pl.ds(pl.multiple_of(k * rows, rows), rows)
-                ssum = jnp.concatenate([ssum_ref[at]] * (cols // lanes), axis=1)
-                tsum = jnp.concatenate([tsum_ref[at]] * (cols // lanes), axis=1)
-                found = jnp.zeros((rows, cols), f32)
-                for i, t_ref in enumerate(ordered):
-                    for j in range(0, piece, cols):
-                        log_s = s_refs[i][at, j : j + cols] - ssum
-                        log_t = t_ref[at, j : j + cols].astype(f32) - tsum
-                        prob_t = jnp.exp(log_t)
-                        g_ref[i, at, j : j + cols] = (
-                            grad_scale * (jnp.exp(log_s) - prob_t)
-                        ).astype(bf16)
-                        found = found + prob_t * (log_t - log_s)
-                folded = [
-                    found[m : m + 8, n : n + lanes]
-                    for m in range(0, rows, 8)
-                    for n in range(0, cols, lanes)
-                ]
-                div_ref[...] += sum(folded[1:], folded[0])
-
-        for at_kind in range(kinds):
-            for at_core in (0, 1):
-                own_ref, side_ref, own_met_ref, side_met_ref = teachers[4 * at_kind : 4 * at_kind + 4]
-
-                @pl.when((kind == at_kind) & (core == at_core))
-                def _(ordered=((own_ref, own_met_ref), (side_met_ref, side_ref))[at_core]):
-                    work(ordered)
-
-    def block_of(kind, of_core):
-        def at(s, p):
-            return (jnp.where(p[(3 + kinds) * count] == of_core, p[(2 + kind) * count + s], 0), 0)
-
-        return at
+            fetch(0, 0)
+
+        @pl.when(step + 1 < steps)
+        def _():
+            fetch(step + 1, 1 - slot)
+
+        for i in range(2):
+            for m in range(per):
+                pltpu.make_async_copy(
+                    teachers[0][0].at[pl.ds(0, few)],
+                    held.at[slot, i, pl.ds(m * few, few)],
+                    sem.at[slot, i, m],
+                ).wait()
+
+        @pl.loop(0, per * few // rows)
+        def _(k):
+            at = pl.ds(pl.multiple_of(k * rows, rows), rows)
+            ssum = jnp.concatenate([ssum_ref[at]] * (cols // lanes), axis=1)
+            tsum = jnp.concatenate([tsum_ref[at]] * (cols // lanes), axis=1)
+            found = jnp.zeros((rows, cols), f32)
+            for i in range(2):
+                for j in range(0, piece, cols):
+                    log_s = s_ref[i, at, j : j + cols] - ssum
+                    log_t = held[slot, i, at, j : j + cols].astype(f32) - tsum
+                    prob_t = jnp.exp(log_t)
+                    g_ref[i, at, j : j + cols] = (
+                        grad_scale * (jnp.exp(log_s) - prob_t)
+                    ).astype(bf16)
+                    found = found + prob_t * (log_t - log_s)
+            folded = [
+                found[m : m + 8, n : n + lanes]
+                for m in range(0, rows, 8)
+                for n in range(0, cols, lanes)
+            ]
+            div_ref[...] += sum(folded[1:], folded[0])
 
     return pl.pallas_call(
         kernel,
         grid_spec=pltpu.PrefetchScalarGridSpec(
             num_scalar_prefetch=1,
-            grid=(count,),
-            in_specs=[
-                pl.BlockSpec((few, piece), block_of(kind, n % 2)) for kind in range(kinds) for n in range(4)
-            ]
-            + [pl.BlockSpec((few, piece), lambda s, p: (p[count + s], 0))] * 2
-            + [pl.BlockSpec((few, lanes), lambda s, p: (p[count + s], 0))] * 2,
+            grid=(steps,),
+            in_specs=[anywhere] * (4 * len(groups))
+            + [pl.BlockSpec((2, per * few, piece), lambda s, p: (0, p[0] // per + s, 0))]
+            + [pl.BlockSpec((per * few, lanes), lambda s, p: (p[0] // per + s, 0))] * 2,
             out_specs=[
-                pl.BlockSpec((2, few, piece), lambda s, p: (0, p[s], 0)),
+                pl.BlockSpec((2, per * few, piece), lambda s, p: (0, s, 0)),
                 pl.BlockSpec((8, lanes), lambda s, p: (0, 0)),
+            ],
+            scratch_shapes=[
+                pltpu.VMEM((2, 2, per * few, piece), bf16),
+                pltpu.SemaphoreType.DMA((2, 2, per)),
             ],
         ),
         out_shape=[
@@ -398,7 +450,7 @@
     )(
         plan,
         *in_hbm(*[part for group in groups for part in group]),
-        *in_hbm(*students, student_sum, teacher_sum),
+        *in_hbm(student, student_sum, teacher_sum),
     )
 
 
@@ -406,40 +458,61 @@
     _, tokens, piece = gradient.shape
     width = pair.shape[1]
     half = tokens // 2
-    cols = largest_tile(width, 768, lanes)
-
-    def kernel(g_ref, w_ref, kept_ref, sent_ref):
+    cols = largest_tile(width, 512, lanes)
+    steps = width // cols
+    depth = min(3, steps)
+
+    def kernel(given_ref, w_ref, kept_ref, sent_ref, g_ref, taken, sem):
         core = lax.axis_index("aa") % 2
-        total = sum(
-            lax.dot_general(
-                g_ref[i], w_ref[i], (((1,), (1,)), ((), ())), preferred_element_type=f32
+
+        def fetch(k):
+            at = pl.ds(k * cols, cols)
+            return pltpu.make_async_copy(w_ref.at[:, at, :], taken.at[k % depth], sem.at[k % depth])
+
+        load = pltpu.make_async_copy(given_ref, g_ref, sem.at[depth])
+        load.start()
+        for k in range(depth):
+            fetch(k).start()
+        load.wait()
+        for k in range(steps):
+            fetch(k).wait()
+            total = sum(
+                lax.dot_general(
+                    g_ref[i],
+                    taken[k % depth, i],
+                    (((1,), (1,)), ((), ())),
+                    preferred_element_type=f32,
+                )
+                for i in range(2)
             )
-            for i in range(2)
-        )
-
-        @pl.when(core == 0)
-        def _():
-            kept_ref[...] = total[:half]
-            sent_ref[...] = total[half:].astype(bf16)
-
-        @pl.when(core == 1)
-        def _():
-            kept_ref[...] = total[half:]
-            sent_ref[...] = total[:half].astype(bf16)
-
-    return pl.pallas_call(
-        kernel,
-        grid=(width // cols,),
-        in_specs=[
-            pl.BlockSpec((2, tokens, piece), lambda d: (0, 0, 0)),
-            pl.BlockSpec((2, cols, piece), lambda d: (0, d, 0)),
+            if k + depth < steps:
+                fetch(k + depth).start()
+            at = slice(k * cols, (k + 1) * cols)
+
+            @pl.when(core == 0)
+            def _(total=total, at=at):
+                kept_ref[:, at] = total[:half]
+                sent_ref[:, at] = total[half:].astype(bf16)
+
+            @pl.when(core == 1)
+            def _(total=total, at=at):
+                kept_ref[:, at] = total[half:]
+                sent_ref[:, at] = total[:half].astype(bf16)
+
+    return pl.pallas_call(
+        kernel,
+        in_specs=[anywhere] * 2,
+        out_specs=[whole_vmem] * 2,
+        out_shape=[
+            pltpu.VMEM((half, width), f32),
+            pltpu.VMEM((half, width), bf16),
         ],
-        out_specs=[pl.BlockSpec((half, cols), lambda d: (0, d))] * 2,
-        out_shape=[
-            jax.ShapeDtypeStruct((half, width), f32),
-            jax.ShapeDtypeStruct((half, width), bf16),
+        scratch_shapes=[
+            pltpu.VMEM((2, tokens, piece), bf16),
+            pltpu.VMEM((depth, 2, cols, piece), bf16),
+            pltpu.SemaphoreType.DMA((depth + 1,)),
         ],
-        compiler_params=limits(40),
+        compiler_params=limits(24),
         cost_estimate=pl.CostEstimate(
             flops=4 * tokens * width * piece, bytes_accessed=4 * width * piece, transcendentals=0
         ),
@@ -487,33 +560,42 @@
         out_shape=[jax.ShapeDtypeStruct((few, width + lanes), bf16)] * count,
         compiler_params=limits(20),
         name="share_out",
-    )(kept, arrived, found)
-
-
-def put_together(blocks):
-    count = len(blocks)
-    few, width = blocks[0].shape
+    )(in_vmem(kept), in_vmem(arrived), found)
+
+
+def put_together(even, odd, few):
+    rows, width = even.shape
+    count = rows // few
     if few % 16:
-        order = lax.axis_index("ba") ^ jnp.arange(count)
-        return jnp.stack(blocks)[order].reshape(count * few, width)
-
-    def kernel(*refs):
+        mine = lax.axis_index("ba") ^ jnp.arange(2 * count)
+        both = jnp.stack([even.reshape(count, few, width), odd.reshape(count, few, width)], axis=1)
+        return both.reshape(2 * count, few, width)[mine].reshape(2 * rows, width)
+
+    def kernel(even_ref, odd_ref, out_ref, sem):
         me = lax.axis_index("ba")
-        for s in range(count):
-            at = pl.ds(pl.multiple_of((me ^ s) * few, few), few)
-            refs[count][at, :] = refs[s][...]
-
-    return pl.pallas_call(
-        kernel,
-        in_specs=[whole_vmem] * count,
-        out_specs=whole_vmem,
-        out_shape=jax.ShapeDtypeStruct((count * few, width), bf16),
-        compiler_params=limits(20),
+
+        def place(s):
+            to = pl.ds(pl.multiple_of((me ^ s) * few, few), few)
+            ref = (even_ref, odd_ref)[s % 2]
+            return pltpu.make_async_copy(ref.at[pl.ds(s // 2 * few, few)], out_ref.at[to], sem.at[s])
+
+        for s in range(2 * count):
+            place(s).start()
+        for s in range(2 * count):
+            place(s).wait()
+
+    return pl.pallas_call(
+        kernel,
+        in_specs=[anywhere] * 2,
+        out_specs=anywhere,
+        out_shape=pltpu.HBM((2 * rows, width), bf16),
+        scratch_shapes=[pltpu.SemaphoreType.DMA((2 * count,))],
+        compiler_params=limits(4),
         name="put_together",
-    )(*blocks)
-
-
-def spread_features(hiddens):
+    )(even, odd)
+
+
+def turn_features(hiddens):
     rows, width = hiddens[0].shape
     blocks = len(hiddens)
     tokens = rows * blocks
@@ -523,6 +605,7 @@
         given = refs[:blocks]
         left, held, sem = refs[blocks:]
         me = lax.axis_index("aa")
+
         def place(q):
             block = q // 2 * 2 + ((me % 2) ^ (q % 2))
             at = pl.ds(pl.multiple_of(block * rows, rows), rows)
@@ -533,42 +616,38 @@
             place(q).start()
         for q in range(blocks):
             place(q).wait()
-        row = lax.broadcasted_iota(jnp.int32, (2 * lanes, lanes), 0)
-        col = lax.broadcasted_iota(jnp.int32, (2 * lanes, lanes), 1)
-        for i in range(2):
-            spread = (row == 2 * col + i).astype(f32).astype(bf16)
-            for d in range(0, share, lanes):
-                left[2 * d : 2 * (d + lanes), i * tokens : (i + 1) * tokens] = lax.dot_general(
-                    spread,
-                    held[:, d : d + lanes],
-                    (((1,), (1,)), ((), ())),
-                    preferred_element_type=f32,
-                ).astype(bf16)
+        row = lax.broadcasted_iota(jnp.int32, (lanes, lanes), 0)
+        col = lax.broadcasted_iota(jnp.int32, (lanes, lanes), 1)
+        same = (row == col).astype(f32).astype(bf16)
+        for d in range(0, share, lanes):
+            left[d : d + lanes] = lax.dot_general(
+                same, held[:, d : d + lanes], (((1,), (1,)), ((), ())), preferred_element_type=f32
+            ).astype(bf16)
 
     return pl.pallas_call(
         kernel,
         in_specs=[anywhere] * blocks,
         out_specs=whole_vmem,
-        out_shape=jax.ShapeDtypeStruct((2 * share, 2 * tokens), bf16),
+        out_shape=jax.ShapeDtypeStruct((share, tokens), bf16),
         scratch_shapes=[
             pltpu.VMEM((tokens, share), bf16),
             pltpu.SemaphoreType.DMA((blocks,)),
         ],
         compiler_params=limits(20),
-        name="spread_features",
+        name="turn_features",
     )(*in_hbm(*hiddens))
 
 
 def head_pair(left, own, other, partner, so_far):
-    tokens = left.shape[1] // 2
-    share = left.shape[0] // 2
+    share, tokens = left.shape
     piece = own.shape[2]
     cols = largest_tile(piece, 512, lanes)
+    part = largest_tile(cols, 256, lanes)
     steps = piece // cols
     aliased = [] if so_far is None else [so_far]
 
     def kernel(left_ref, own_ref, other_ref, *refs):
-        out_ref, ready, out_sem = refs[len(aliased) :]
+        out_ref, mixed, ready, out_sem = refs[len(aliased) :]
         step = pl.program_id(0)
         slot = lax.rem(step, 2)
         base = 2 * (my_pair() ^ partner)
@@ -583,10 +662,25 @@
         def _():
             store(step - 2, slot).wait()
 
-        right = jnp.concatenate([own_ref[0], other_ref[0], own_ref[1], other_ref[1]], axis=0)
-        for d in range(0, 2 * share, 512):
-            made = jnp.dot(left_ref[d : d + 512], right, preferred_element_type=f32).astype(bf16)
-            ready[slot, d // 2 : d // 2 + 256] = made.reshape(256, 2, cols)
+        def unload(start):
+            for n in range(start // lanes, (start + part) // lanes):
+                ready[slot, :, :, n * lanes : (n + 1) * lanes] = (
+                    mixed[n].astype(bf16).reshape(share, 2, lanes)
+                )
+
+        for j in range(0, cols, part):
+            for i in range(2):
+                right = jnp.concatenate(
+                    [own_ref[i, :, j : j + part], other_ref[i, :, j : j + part]], axis=0
+                )
+                made = jnp.dot(left_ref[...], right, preferred_element_type=f32)
+                for n in range(part // lanes):
+                    mixed[j // lanes + n, pl.ds(i, share, stride=2), :] = made[
+                        :, n * lanes : (n + 1) * lanes
+                    ]
+            if j:
+                unload(j - part)
+        unload(cols - part)
         store(step, slot).start()
 
         @pl.when(step == steps - 1)
@@ -604,13 +698,14 @@
         out_specs=anywhere,
         out_shape=jax.ShapeDtypeStruct((share, 1, 4, piece), bf16),
         scratch_shapes=[
+            pltpu.VMEM((cols // lanes, 2 * share, lanes), f32),
             pltpu.VMEM((2, share, 2, cols), bf16),
             pltpu.SemaphoreType.DMA((2,)),
         ],
         input_output_aliases={3: 0} if aliased else {},
-        compiler_params=limits(20),
+        compiler_params=limits(30),
         cost_estimate=pl.CostEstimate(
-            flops=8 * share * tokens * piece, bytes_accessed=4 * share * piece, transcendentals=0
+            flops=4 * share * tokens * piece, bytes_accessed=4 * share * piece, transcendentals=0
         ),
         name="head_pair",
     )(left, *in_hbm(own, other), *aliased)
@@ -630,75 +725,59 @@
     beside = exchange(hidden, "aa", 1)
     *blocks, teacher_stat = split_teacher(teacher)
     blocks, beside, head_weight = lax.optimization_barrier((blocks, beside, head_weight))
-    middle = near + (count - near) * 3 // 4
-    teacher_stats = [teacher_stat, exchange(teacher_stat, "aa", 2)]
-    arrived = [exchange(block, "ba", s) if s else block for s, block in enumerate(blocks[:near])]
+    middle = near + 1
+    queue = [*range(near - 1), near, near + 1, near - 1, *range(near + 2, count)]
+    arrived = [exchange(blocks[s], "ba", s) if s else blocks[s] for s in queue[:middle]]
     pair = take_pair(head_weight)
-    arrived, teacher_stats, early, side, pair = lax.optimization_barrier(
-        (arrived, teacher_stats, blocks[near:middle], side, pair)
+    teacher_stat, late, side, pair = lax.optimization_barrier(
+        (teacher_stat, [blocks[s] for s in queue[middle:]], side, pair)
     )
     hiddens = [hidden, beside, side, exchange(side, "aa", 1)]
-    arrived += [exchange(block, "ba", near + s) for s, block in enumerate(early)]
+    arrived += [exchange(block, "ba", s) for block, s in zip(late, queue[middle:])]
+    teacher_stats = [teacher_stat, exchange(teacher_stat, "aa", 2)]
+    arrived[:middle], pair = lax.optimization_barrier((arrived[:middle], pair))
 
     def cross(parts):
-        mine = jnp.concatenate(parts, axis=0)
+        mine = join(parts)
         return [mine, exchange(mine, "aa", 2)]
 
     def swap(group):
         return group + [exchange(part, "aa", 1) for part in group]
 
-    group_a = cross(arrived[:near])
-    first, stat_first = student_logits(hiddens, pair, 0)
-    late, first, stat_first, pair = lax.optimization_barrier(
-        (blocks[middle:], first, stat_first, pair)
-    )
-    arrived += [exchange(late[s - middle], "ba", s) for s in range(middle, count)]
-    second, stat_second = student_logits(hiddens, pair, 1)
-    arrived[near:middle], stat_second = lax.optimization_barrier((arrived[near:middle], stat_second))
-    packed = pack_stats([stat_first, stat_second], teacher_stats)
+    group_a = cross(arrived[:middle])
+    student, student_stat = student_logits(hiddens, pair)
+    arrived[middle:], student_stat = lax.optimization_barrier((arrived[middle:], student_stat))
+    packed = pack_stats([student_stat], teacher_stats)
     group_a, packed = lax.optimization_barrier((group_a, packed))
     group_a = swap(group_a)
+    group_b = cross(arrived[middle:])
     packed = merge_two(packed, exchange(packed, "aa", 1))
-    group_b = cross(arrived[near:middle])
     mask = 1
     while 2 * mask < count:
         met = exchange(packed, "ba", mask)
         if mask == 1:
-            left = spread_features(hiddens)
+            left = turn_features(hiddens)
             left, met = lax.optimization_barrier((left, met))
         packed = merge_two(packed, met)
-        if 4 * mask == count:
-            last_parts, packed = lax.optimization_barrier((arrived[middle:], packed))
-            group_c = cross(last_parts)
         mask *= 2
-    met = exchange(packed, "ba", mask)
-    group_b, group_c, met = lax.optimization_barrier((group_b, group_c, met))
-    group_b, group_c = swap(group_b), swap(group_c)
-    sums = all_log_sums(packed, met)
-    groups = [group_a, group_b, group_c]
+    group_a, packed = lax.optimization_barrier((group_a, packed))
+    sums = all_log_sums(packed, exchange(packed, "ba", mask))
+    group_b, sums = lax.optimization_barrier((group_b, sums))
+    groups = [group_a, swap(group_b)]
+
+    order = [queue.index(s) for s in range(count)]
+    table = [n % middle if n < middle else n - middle for n in order] + [int(n >= middle) for n in order]
 
     def plan(group):
-        is_far = (me_b // near) ^ group
-        step = jnp.arange(near)
-        place = (me_b % near) ^ step
-        short = middle - near
-        kind = jnp.where(is_far == 0, 0, jnp.where(step < short, 1, 2))
-        reads = [
-            jnp.where(is_far == 0, step, 0),
-            jnp.where(is_far == 1, jnp.minimum(step, short - 1), 0),
-            jnp.where(is_far == 1, jnp.maximum(step - short, 0), 0),
-        ]
-        return jnp.concatenate(
-            [place, place + near * group, *reads, kind, core[None]]
-        ).astype(jnp.int32)
-
-    students = [first, second]
-    grad_own, found = logit_gradient(plan(chip), groups, students, *sums)
+        here = jnp.stack([near * group, me_b, core]).astype(jnp.int32)
+        return jnp.concatenate([here, jnp.array(table, jnp.int32)])
+
+    grad_own, found = logit_gradient(plan(chip), groups, student, *sums)
     kept, sent = hidden_share(grad_own, pair)
     shares = share_out(kept, exchange(sent, "aa", 1), found)
     own_met = exchange(grad_own, "aa", 1)
     sums, own_met, shares = lax.optimization_barrier((sums, own_met, shares))
-    grad_other, _ = logit_gradient(plan(1 - chip), groups, students, *sums)
+    grad_other, _ = logit_gradient(plan(1 - chip), groups, student, *sums)
     reduced = [exchange(shares[s], "ba", s) for s in range(1, count)]
     reduced, grad_other = lax.optimization_barrier((reduced, grad_other))
     summed = shares[0].astype(f32)
@@ -709,18 +788,19 @@
 
     other_met = exchange(grad_other, "aa", 1)
     divergence = divergence + exchange(divergence, "aa", 1)
-    gathered = {s: exchange(summed, "ba", s) for s in range(near - 1, count)}
-    grad_own, summed = lax.optimization_barrier((grad_own, summed))
+    gathered = [summed] + [exchange(summed, "ba", s) for s in range(2, count, 2)]
+    grad_own, gathered[0] = lax.optimization_barrier((grad_own, gathered[0]))
     grad_head = head_pair(left, grad_own, grad_other, 0, None)
-    summed, gathered, grad_head, divergence, other_met = lax.optimization_barrier(
-        (summed, gathered, grad_head, divergence, other_met)
+    gathered, grad_head, divergence, other_met = lax.optimization_barrier(
+        (gathered, grad_head, divergence, other_met)
     )
-    for s in range(1, near - 1):
-        gathered[s] = exchange(summed, "ba", s)
+    even = join(gathered)
+    odd = exchange(even, "ba", 1)
     divergence = divergence + exchange(divergence, "aa", 2)
+    even, other_met = lax.optimization_barrier((even, other_met))
     grad_head = head_pair(left, own_met, other_met, 1, grad_head)
-    gathered, grad_head = lax.optimization_barrier((gathered, grad_head))
-    grad_hidden = put_together([summed] + [gathered[s] for s in range(1, count)])
+    odd, grad_head = lax.optimization_barrier((odd, grad_head))
+    grad_hidden = put_together(even, odd, summed.shape[0])
     return divergence[0], grad_hidden, grad_head
 
 

time: 188 us -> 171 us (0.910)
  waiting for transfers between devices: 25.1 us -> 39.4 us
  starting transfers between devices: 54.3 us -> 42.2 us
  Pallas kernels: 92.1 us -> 82.9 us
  local copies, waits for them, and re-layouts: 9.5 us -> 1.01 us
    ppermute x43 -> x37, waiting for transfers between devices: 25.1 us -> 39.4 us  [exchange(): return lax.ppermute(value, axis, [(i, i ^ mask) for i in range(count)])]
    ppermute x43 -> x37, starting transfers between devices: 54.3 us -> 42.2 us  [exchange(): return lax.ppermute(value, axis, [(i, i ^ mask) for i in range(count)])]
    unnamed x39 -> x38, local copies, waits for them, and re-layouts: 7.87 us -> 1 us
    pallas_call x5 -> x7, Pallas kernels: 39.9 us -> 34.6 us  [the longest x1 18.5 us: student_logits(): pl.pallas_call(kernel, grid=(2, piece // cols), in_specs=[anywhere] * blo...]
  transfers between devices with their start and end apart: 43 -> 37, of which waited for: 12 -> 13; matrix products, arithmetic and copies ran while one was open for 4% -> 0% of each run, Pallas kernels for 45% -> 43%
where the time goes in v3:
time: 171 us
  Pallas kernels  82.9 us (48%)
  starting transfers between devices  42.2 us (25%)
  waiting for transfers between devices  39.4 us (23%)
  between operations  4.17 us (2%)
    ppermute x37, starting transfers between devices, exchange(): return lax.ppermute(value, axis, [(i, i ^ mask) for i in range(count)])  42.2 us
    ppermute x37, waiting for transfers between devices, exchange(): return lax.ppermute(value, axis, [(i, i ^ mask) for i in range(count)])  39.4 us
    pallas_call x1, Pallas kernels, student_logits(): pl.pallas_call(kernel, grid=(2, piece // cols), in_specs=[anywhere] * blo...  18.5 us
    pallas_call x2, Pallas kernels, head_pair(): pl.pallas_call(kernel, grid=(steps,), in_specs=[whole_vmem] + [pl.BlockSp...  18 us
    pallas_call x2, Pallas kernels, logit_gradient(): pl.pallas_call(kernel, grid_spec=pltpu.PrefetchScalarGridSpec(num_scalar_...  13.3 us
    pallas_call x1, Pallas kernels, hidden_share(): pl.pallas_call(kernel, in_specs=[anywhere] * 2, out_specs=[whole_vmem] *...  10.6 us
    pallas_call x1, Pallas kernels, take_pair(): pl.pallas_call(kernel, in_specs=[anywhere], out_specs=whole_vmem, out_sha...  10.5 us
    pallas_call x1, Pallas kernels, split_teacher(): pl.pallas_call(kernel, grid=(piece // cols,), in_specs=[pl.BlockSpec((tok...  5.13 us
  transfers between devices with their start and end apart: 37, of which 13 were waited for; matrix products, arithmetic and copies ran while one was open for 0% of the time, Pallas kernels for 43%

profile of v3, /device:TPU:0, one launch (start us, length us, event | category | flops | bytes accessed | tf_op | source)
XLA Modules:
  0.0 170.5 jit_solution(7924805166908677482)
XLA Ops:
  1.1 2.6 %collective-permute-start.5 = (bf16[128,3072]{1,0:T(8,128)(2,1)}, bf16[128,3072]{1,0:T(8,128)(2,1)S(1)}, u32[]{:S(2)}, u32[]{:S(2)}) collective-permute-start(bf16[128,3072]{1,0:T(8,128)(2,1)} %refs_0_.3), channel_id=1, source_target_pairs={{0,16},{8,24},{16,0},{24,8},{1,17},{9,25},{17,1},{25,9},{2,18},{10... | collective-permute-start | bytes 2359304 | tf_op jit(solution)/shard_map/ppermute | solution.py:49
  3.7 5.1 %split_teacher.1 = (bf16[64,2048]{1,0:T(8,128)(2,1)}, bf16[64,2048]{1,0:T(8,128)(2,1)}, bf16[64,2048]{1,0:T(8,128)(2,1)}, bf16[64,2048]{1,0:T(8,128)(2,1)}, bf16...) custom-call(bf16[64,1,8,2048]{3,2,1,0:T(8,128)(2,1)} %in_ref.1), custom_call_target="tpu_custom_call" | custom-call | tf_op jit(solution)/shard_map/split_teacher/pallas_call | solution.py:133
  12.0 2.6 %collective-permute-start.3 = (bf16[64,2048]{1,0:T(8,128)(2,1)}, bf16[64,2048]{1,0:T(8,128)(2,1)S(1)}, u32[]{:S(2)}, u32[]{:S(2)}) collective-permute-start(bf16[64,2048]{1,0:T(8,128)(2,1)} %get-tuple-element.112), channel_id=1, source_target_pairs={{0,4},{1,5},{2,6},{3,7},{4,0},{5,1},{6,2},{7,3},{8,12},{9,13},{10,... | collective-permute-start | bytes 786440 | tf_op jit(solution)/shard_map/ppermute | solution.py:49
  14.9 10.5 %take_pair.1.refs_4_.w_ref = bf16[2,3072,2048]{2,1,0:T(8,128)(2,1)S(1)} custom-call(bf16[3072,1,4,2048]{3,2,1,0:T(4,128)(2,1)} %w_ref), custom_call_target="tpu_custom_call" | custom-call | flops 12884901888 | bytes 25165824 | tf_op jit(solution)/shard_map/take_pair/pallas_call | solution.py:179
  25.6 8.1 %collective-permute-done.3.refs_3_ = bf16[64,2048]{1,0:T(8,128)(2,1)S(1)} collective-permute-done((bf16[64,2048]{1,0:T(8,128)(2,1)}, bf16[64,2048]{1,0:T(8,128)(2,1)S(1)}, u32[]{:S(2)}, u32[]{:S(2)}) %collective-permute-start.3) | collective-permute-done | bytes 262176 | tf_op jit(solution)/shard_map/ppermute | solution.py:49
  33.6 4.2 %collective-permute-done.4.refs_4_ = bf16[64,2048]{1,0:T(8,128)(2,1)S(1)} collective-permute-done((bf16[64,2048]{1,0:T(8,128)(2,1)}, bf16[64,2048]{1,0:T(8,128)(2,1)S(1)}, u32[]{:S(2)}, u32[]{:S(2)}) %collective-permute-start.4) | collective-permute-done | bytes 262176 | tf_op jit(solution)/shard_map/ppermute | solution.py:49
  39.6 2.5 %collective-permute-start.8 = (bf16[64,2048]{1,0:T(8,128)(2,1)S(1)}, bf16[64,2048]{1,0:T(8,128)(2,1)S(1)}, u32[]{:S(2)}, u32[]{:S(2)}) collective-permute-start(bf16[64,2048]{1,0:T(8,128)(2,1)S(1)} %copy-done.17), channel_id=1, source_target_pairs={{0,6},{1,7},{2,4},{3,5},{4,2},{5,3},{6,0},{7,1},{8,14},{9,15},{10,... | collective-permute-start | bytes 786440 | tf_op jit(solution)/shard_map/ppermute | solution.py:49
  42.1 2.3 %collective-permute-start.9 = (bf16[64,2048]{1,0:T(8,128)(2,1)S(1)}, bf16[64,2048]{1,0:T(8,128)(2,1)S(1)}, u32[]{:S(2)}, u32[]{:S(2)}) collective-permute-start(bf16[64,2048]{1,0:T(8,128)(2,1)S(1)} %copy-done.16), channel_id=1, source_target_pairs={{0,7},{1,6},{2,5},{3,4},{4,3},{5,2},{6,1},{7,0},{8,15},{9,14},{10,... | collective-permute-start | bytes 786440 | tf_op jit(solution)/shard_map/ppermute | solution.py:49
  45.9 18.5 %student_logits.1 = (f32[2,512,2048]{2,1,0:T(8,128)}, f32[8,512]{1,0:T(8,128)S(1)}) custom-call(bf16[128,3072]{1,0:T(8,128)(2,1)} %refs_0_.3, bf16[128,3072]{1,0:T(8,128)(2,1)} %copy-done.8, bf16[128,3072]{1,0:T(8,128)(2,1)} %copy-done.9, bf16[128,3072]{1,0:T(8,128)(2,1)} %copy-done.10, bf16[2,3072,2048]{2,1,0:T(8,128)(2,1)S(1)} %take_pair.1.refs_4_.w_ref), custom_call_target="tpu_custom_call" | custom-call | flops 1 | bytes 1 | tf_op jit(solution)/shard_map/student_logits/pallas_call | solution.py:256
  64.5 4.5 %collective-permute-done.11.refs_2_ = f32[8,512]{1,0:T(8,128)S(1)} collective-permute-done((f32[8,512]{1,0:T(8,128)S(1)}, f32[8,512]{1,0:T(8,128)S(1)}, u32[]{:S(2)}, u32[]{:S(2)}) %collective-permute-start.11) | collective-permute-done | bytes 16416 | tf_op jit(solution)/shard_map/ppermute | solution.py:49
  71.2 2.9 %collective-permute-done.14.b_ref = f32[8,512]{1,0:T(8,128)S(1)} collective-permute-done((f32[8,512]{1,0:T(8,128)S(1)}, f32[8,512]{1,0:T(8,128)S(1)}, u32[]{:S(2)}, u32[]{:S(2)}) %collective-permute-start.14) | collective-permute-done | bytes 16416 | tf_op jit(solution)/shard_map/ppermute | solution.py:49
  78.0 3.7 %collective-permute-done.16.b_ref = f32[8,512]{1,0:T(8,128)S(1)} collective-permute-done((f32[8,512]{1,0:T(8,128)S(1)}, f32[8,512]{1,0:T(8,128)S(1)}, u32[]{:S(2)}, u32[]{:S(2)}) %collective-permute-start.16) | collective-permute-done | bytes 16416 | tf_op jit(solution)/shard_map/ppermute | solution.py:49
  82.9 3.6 %collective-permute-done.18.b_ref = f32[8,512]{1,0:T(8,128)S(1)} collective-permute-done((f32[8,512]{1,0:T(8,128)S(1)}, f32[8,512]{1,0:T(8,128)S(1)}, u32[]{:S(2)}, u32[]{:S(2)}) %collective-permute-start.18) | collective-permute-done | bytes 16416 | tf_op jit(solution)/shard_map/ppermute | solution.py:49
  87.5 3.0 %collective-permute-done.17.refs_5_ = bf16[192,2048]{1,0:T(8,128)(2,1)} collective-permute-done((bf16[192,2048]{1,0:T(8,128)(2,1)}, bf16[192,2048]{1,0:T(8,128)(2,1)}, u32[]{:S(2)}, u32[]{:S(2)}) %collective-permute-start.17) | collective-permute-done | bytes 786464 | tf_op jit(solution)/shard_map/ppermute | solution.py:49
  91.1 2.1 %collective-permute-done.19.refs_6_ = bf16[192,2048]{1,0:T(8,128)(2,1)S(1)} collective-permute-done((bf16[192,2048]{1,0:T(8,128)(2,1)S(1)}, bf16[192,2048]{1,0:T(8,128)(2,1)S(1)}, u32[]{:S(2)}, u32[]{:S(2)}) %collective-permute-start.19) | collective-permute-done | bytes 786464 | tf_op jit(solution)/shard_map/ppermute | solution.py:49
  95.0 6.5 %logit_gradient.2 = (bf16[2,256,2048]{2,1,0:T(8,128)(2,1)}, f32[8,128]{1,0:T(8,128)S(1)}) custom-call(s32[19]{0:T(128)S(1)} %get-tuple-element.200.plan_ref, bf16[320,2048]{1,0:T(8,128)(2,1)} %join.3.refs_0_, bf16[320,2048]{1,0:T(8,128)(2,1)} %copy-done.5, bf16[320,2048]{1,0:T(8,128)(2,1)} %copy-done.6, bf16[320,2048]{1,0:T(8,128)(2,1)} %copy-done.7, ...), custom_call_target="tpu_custom_call" | custom-call | flops 4194304 | bytes 8388608 | tf_op jit(solution)/shard_map/logit_gradient/pallas_call | solution.py:424
  101.8 10.6 %hidden_share.1 = (f32[128,3072]{1,0:T(8,128)S(1)}, bf16[128,3072]{1,0:T(8,128)(2,1)S(1)}) custom-call(bf16[2,256,2048]{2,1,0:T(8,128)(2,1)} %get-tuple-element.185.given_ref.own_ref, bf16[2,3072,2048]{2,1,0:T(8,128)(2,1)} %copy-done), custom_call_target="tpu_custom_call" | custom-call | flops 6442450944 | bytes 25165824 | tf_op jit(solution)/shard_map/hidden_share/pallas_call | solution.py:502
  119.7 2.8 %collective-permute-start.27 = (bf16[16,3200]{1,0:T(8,128)(2,1)S(1)}, bf16[16,3200]{1,0:T(8,128)(2,1)S(1)}, u32[]{:S(2)}, u32[]{:S(2)}) collective-permute-start(bf16[16,3200]{1,0:T(8,128)(2,1)S(1)} %get-tuple-element.170), channel_id=1, source_target_pairs={{0,5},{1,4},{2,7},{3,6},{4,1},{5,0},{6,3},{7,2},{8,13},{9,12},{10,... | collective-permute-start | bytes 307208 | tf_op jit(solution)/shard_map/ppermute | solution.py:49
  122.5 2.5 %collective-permute-start.28 = (bf16[16,3200]{1,0:T(8,128)(2,1)S(1)}, bf16[16,3200]{1,0:T(8,128)(2,1)S(1)}, u32[]{:S(2)}, u32[]{:S(2)}) collective-permute-start(bf16[16,3200]{1,0:T(8,128)(2,1)S(1)} %get-tuple-element.171), channel_id=1, source_target_pairs={{0,6},{1,7},{2,4},{3,5},{4,2},{5,3},{6,0},{7,1},{8,14},{9,15},{10,... | collective-permute-start | bytes 307208 | tf_op jit(solution)/shard_map/ppermute | solution.py:49
  126.2 6.8 %logit_gradient.3 = (bf16[2,256,2048]{2,1,0:T(8,128)(2,1)}, f32[8,128]{1,0:T(8,128)}) custom-call(s32[19]{0:T(128)S(1)} %get-tuple-element.199.plan_ref, bf16[320,2048]{1,0:T(8,128)(2,1)} %join.3.refs_0_, bf16[320,2048]{1,0:T(8,128)(2,1)} %copy-done.5, bf16[320,2048]{1,0:T(8,128)(2,1)} %copy-done.6, bf16[320,2048]{1,0:T(8,128)(2,1)} %copy-done.7, ...), custom_call_target="tpu_custom_call" | custom-call | flops 4194304 | bytes 8388608 | tf_op jit(solution)/shard_map/logit_gradient/pallas_call | solution.py:424
  133.6 3.4 %collective-permute-done.27 = bf16[16,3200]{1,0:T(8,128)(2,1)S(1)} collective-permute-done((bf16[16,3200]{1,0:T(8,128)(2,1)S(1)}, bf16[16,3200]{1,0:T(8,128)(2,1)S(1)}, u32[]{:S(2)}, u32[]{:S(2)}) %collective-permute-start.27) | collective-permute-done | bytes 102432 | tf_op jit(solution)/shard_map/ppermute | solution.py:49
  137.1 4.7 %collective-permute-start.31 = (bf16[16,3072]{1,0:T(8,128)(2,1)S(1)}, bf16[16,3072]{1,0:T(8,128)(2,1)S(1)}, u32[]{:S(2)}, u32[]{:S(2)}) collective-permute-start(bf16[16,3072]{1,0:T(8,128)(2,1)S(1)} %slice.13.refs_0_), channel_id=1, source_target_pairs={{0,4},{1,5},{2,6},{3,7},{4,0},{5,1},{6,2},{7,3},{8,12},{9,13},{10,... | collective-permute-start | bytes 294920 | tf_op jit(solution)/shard_map/ppermute | solution.py:49
  145.4 9.0 %head_pair.2.refs_0_ = bf16[768,1,4,2048]{3,2,1,0:T(4,128)(2,1)} custom-call(bf16[768,512]{1,0:T(8,128)(2,1)S(1)} %turn_features.1.left_ref, bf16[2,256,2048]{2,1,0:T(8,128)(2,1)} %get-tuple-element.185.given_ref.own_ref, bf16[2,256,2048]{2,1,0:T(8,128)(2,1)} %get-tuple-element.186.other_ref), custom_call_target="tpu_custom_call" | custom-call | flops 3221225472 | bytes 6291456 | tf_op jit(solution)/shard_map/head_pair/pallas_call | solution.py:692
  158.8 9.0 %head_pair.3 = bf16[768,1,4,2048]{3,2,1,0:T(4,128)(2,1)} custom-call(bf16[768,512]{1,0:T(8,128)(2,1)S(1)} %turn_features.1.left_ref, bf16[2,256,2048]{2,1,0:T(8,128)(2,1)} %copy-done.13, bf16[2,256,2048]{2,1,0:T(8,128)(2,1)} %copy-done.14, bf16[768,1,4,2048]{3,2,1,0:T(4,128)(2,1)} %head_pair.2.refs_0_), custom_call_target="tpu_custom_call", output_to_operand_aliasing={{}: (3, {})} | custom-call | flops 3221225472 | bytes 6291456 | tf_op jit(solution)/shard_map/head_pair/pallas_call | solution.py:692
  (111 shorter events, 34.8 us)
Async XLA Ops:
  1.1 24.4 %collective-permute-start.5 = (bf16[128,3072]{1,0:T(8,128)(2,1)}, bf16[128,3072]{1,0:T(8,128)(2,1)S(1)}, u32[]{:S(2)}, u32[]{:S(2)}) collective-permute-start(bf16[128,3072]{1,0:T(8,128)(2,1)} %refs_0_.3), channel_id=1, source_target_pairs={{0,16},{8,24},{16,0},{24,8},{1,17},{9,25},{17,1},{25,9},{2,18},{10... | collective-permute-start | bytes 2359304 | tf_op jit(solution)/shard_map/ppermute | solution.py:49
  8.9 16.7 %collective-permute-start.1 = (bf16[64,2048]{1,0:T(8,128)(2,1)}, bf16[64,2048]{1,0:T(8,128)(2,1)S(1)}, u32[]{:S(2)}, u32[]{:S(2)}) collective-permute-start(bf16[64,2048]{1,0:T(8,128)(2,1)} %get-tuple-element.110), channel_id=1, source_target_pairs={{0,1},{1,0},{2,3},{3,2},{4,5},{5,4},{6,7},{7,6},{8,9},{9,8},{10,11... | collective-permute-start | bytes 786440 | tf_op jit(solution)/shard_map/ppermute | solution.py:49
  10.5 15.1 %collective-permute-start.2 = (bf16[64,2048]{1,0:T(8,128)(2,1)}, bf16[64,2048]{1,0:T(8,128)(2,1)S(1)}, u32[]{:S(2)}, u32[]{:S(2)}) collective-permute-start(bf16[64,2048]{1,0:T(8,128)(2,1)} %get-tuple-element.111), channel_id=1, source_target_pairs={{0,2},{1,3},{2,0},{3,1},{4,6},{5,7},{6,4},{7,5},{8,10},{9,11},{10,... | collective-permute-start | bytes 786440 | tf_op jit(solution)/shard_map/ppermute | solution.py:49
  12.0 21.6 %collective-permute-start.3 = (bf16[64,2048]{1,0:T(8,128)(2,1)}, bf16[64,2048]{1,0:T(8,128)(2,1)S(1)}, u32[]{:S(2)}, u32[]{:S(2)}) collective-permute-start(bf16[64,2048]{1,0:T(8,128)(2,1)} %get-tuple-element.112), channel_id=1, source_target_pairs={{0,4},{1,5},{2,6},{3,7},{4,0},{5,1},{6,2},{7,3},{8,12},{9,13},{10,... | collective-permute-start | bytes 786440 | tf_op jit(solution)/shard_map/ppermute | solution.py:49
  14.6 23.2 %collective-permute-start.4 = (bf16[64,2048]{1,0:T(8,128)(2,1)}, bf16[64,2048]{1,0:T(8,128)(2,1)S(1)}, u32[]{:S(2)}, u32[]{:S(2)}) collective-permute-start(bf16[64,2048]{1,0:T(8,128)(2,1)} %get-tuple-element.113), channel_id=1, source_target_pairs={{0,5},{1,4},{2,7},{3,6},{4,1},{5,0},{6,3},{7,2},{8,13},{9,12},{10,... | collective-permute-start | bytes 786440 | tf_op jit(solution)/shard_map/ppermute | solution.py:49
  39.0 30.1 %collective-permute-start.6 = (bf16[320,2048]{1,0:T(8,128)(2,1)}, bf16[320,2048]{1,0:T(8,128)(2,1)S(1)}, u32[]{:S(2)}, u32[]{:S(2)}) collective-permute-start(bf16[320,2048]{1,0:T(8,128)(2,1)} %join.3.refs_0_), channel_id=1, source_target_pairs={{0,16},{8,24},{16,0},{24,8},{1,17},{9,25},{17,1},{25,9},{2,18},{10... | collective-permute-start | bytes 3932168 | tf_op jit(solution)/shard_map/ppermute | solution.py:49
  39.6 24.9 %collective-permute-start.7 = (bf16[64,2048]{1,0:T(8,128)(2,1)S(1)}, bf16[64,2048]{1,0:T(8,128)(2,1)S(1)}, u32[]{:S(2)}, u32[]{:S(2)}) collective-permute-start(bf16[64,2048]{1,0:T(8,128)(2,1)S(1)} %copy-done.18), channel_id=1, source_target_pairs={{0,3},{1,2},{2,1},{3,0},{4,7},{5,6},{6,5},{7,4},{8,11},{9,10},{10,... | collective-permute-start | bytes 786440 | tf_op jit(solution)/shard_map/ppermute | solution.py:49
  39.6 24.9 %collective-permute-start.8 = (bf16[64,2048]{1,0:T(8,128)(2,1)S(1)}, bf16[64,2048]{1,0:T(8,128)(2,1)S(1)}, u32[]{:S(2)}, u32[]{:S(2)}) collective-permute-start(bf16[64,2048]{1,0:T(8,128)(2,1)S(1)} %copy-done.17), channel_id=1, source_target_pairs={{0,6},{1,7},{2,4},{3,5},{4,2},{5,3},{6,0},{7,1},{8,14},{9,15},{10,... | collective-permute-start | bytes 786440 | tf_op jit(solution)/shard_map/ppermute | solution.py:49
  42.1 22.4 %collective-permute-start.9 = (bf16[64,2048]{1,0:T(8,128)(2,1)S(1)}, bf16[64,2048]{1,0:T(8,128)(2,1)S(1)}, u32[]{:S(2)}, u32[]{:S(2)}) collective-permute-start(bf16[64,2048]{1,0:T(8,128)(2,1)S(1)} %copy-done.16), channel_id=1, source_target_pairs={{0,7},{1,6},{2,5},{3,4},{4,3},{5,2},{6,1},{7,0},{8,15},{9,14},{10,... | collective-permute-start | bytes 786440 | tf_op jit(solution)/shard_map/ppermute | solution.py:49
  44.4 24.6 %collective-permute-start.11 = (f32[8,512]{1,0:T(8,128)S(1)}, f32[8,512]{1,0:T(8,128)S(1)}, u32[]{:S(2)}, u32[]{:S(2)}) collective-permute-start(f32[8,512]{1,0:T(8,128)S(1)} %get-tuple-element.133.refs_1_), channel_id=1, source_target_pairs={{0,16},{8,24},{16,0},{24,8},{1,17},{9,25},{17,1},{25,9},{2,18},{10... | collective-permute-start | bytes 49160 | tf_op jit(solution)/shard_map/ppermute | solution.py:49
  69.1 12.7 %collective-permute-start.12 = (bf16[320,2048]{1,0:T(8,128)(2,1)S(1)}, bf16[320,2048]{1,0:T(8,128)(2,1)S(1)}, u32[]{:S(2)}, u32[]{:S(2)}) collective-permute-start(bf16[320,2048]{1,0:T(8,128)(2,1)S(1)} %copy-done.3), channel_id=1, source_target_pairs={{0,8},{8,0},{16,24},{24,16},{1,9},{9,1},{17,25},{25,17},{2,10},{10... | collective-permute-start | bytes 3932168 | tf_op jit(solution)/shard_map/ppermute | solution.py:49
  69.1 12.6 %collective-permute-start.13 = (bf16[320,2048]{1,0:T(8,128)(2,1)S(1)}, bf16[320,2048]{1,0:T(8,128)(2,1)S(1)}, u32[]{:S(2)}, u32[]{:S(2)}) collective-permute-start(bf16[320,2048]{1,0:T(8,128)(2,1)S(1)} %collective-permute-done.6.refs_1_), channel_id=1, source_target_pairs={{0,8},{8,0},{16,24},{24,16},{1,9},{9,1},{17,25},{25,17},{2,10},{10... | collective-permute-start | bytes 3932168 | tf_op jit(solution)/shard_map/ppermute | solution.py:49
  70.6 19.9 %collective-permute-start.17 = (bf16[192,2048]{1,0:T(8,128)(2,1)}, bf16[192,2048]{1,0:T(8,128)(2,1)}, u32[]{:S(2)}, u32[]{:S(2)}) collective-permute-start(bf16[192,2048]{1,0:T(8,128)(2,1)} %join.4.refs_4_), channel_id=1, source_target_pairs={{0,16},{8,24},{16,0},{24,8},{1,17},{9,25},{17,1},{25,9},{2,18},{10... | collective-permute-start | bytes 2359304 | tf_op jit(solution)/shard_map/ppermute | solution.py:49
  101.6 13.4 %collective-permute-start.21 = (bf16[2,256,2048]{2,1,0:T(8,128)(2,1)}, bf16[2,256,2048]{2,1,0:T(8,128)(2,1)S(1)}, u32[]{:S(2)}, u32[]{:S(2)}) collective-permute-start(bf16[2,256,2048]{2,1,0:T(8,128)(2,1)} %get-tuple-element.185.given_ref.own_ref), channel_id=1, source_target_pairs={{0,8},{8,0},{16,24},{24,16},{1,9},{9,1},{17,25},{25,17},{2,10},{10... | collective-permute-start | bytes 6291464 | tf_op jit(solution)/shard_map/ppermute | solution.py:49
  116.6 16.4 %collective-permute-start.25 = (bf16[16,3200]{1,0:T(8,128)(2,1)S(1)}, bf16[16,3200]{1,0:T(8,128)(2,1)S(1)}, u32[]{:S(2)}, u32[]{:S(2)}) collective-permute-start(bf16[16,3200]{1,0:T(8,128)(2,1)S(1)} %get-tuple-element.168), channel_id=1, source_target_pairs={{0,3},{1,2},{2,1},{3,0},{4,7},{5,6},{6,5},{7,4},{8,11},{9,10},{10,... | collective-permute-start | bytes 307208 | tf_op jit(solution)/shard_map/ppermute | solution.py:49
  118.6 15.0 %collective-permute-start.26 = (bf16[16,3200]{1,0:T(8,128)(2,1)S(1)}, bf16[16,3200]{1,0:T(8,128)(2,1)S(1)}, u32[]{:S(2)}, u32[]{:S(2)}) collective-permute-start(bf16[16,3200]{1,0:T(8,128)(2,1)S(1)} %get-tuple-element.169), channel_id=1, source_target_pairs={{0,4},{1,5},{2,6},{3,7},{4,0},{5,1},{6,2},{7,3},{8,12},{9,13},{10,... | collective-permute-start | bytes 307208 | tf_op jit(solution)/shard_map/ppermute | solution.py:49
  119.7 17.3 %collective-permute-start.27 = (bf16[16,3200]{1,0:T(8,128)(2,1)S(1)}, bf16[16,3200]{1,0:T(8,128)(2,1)S(1)}, u32[]{:S(2)}, u32[]{:S(2)}) collective-permute-start(bf16[16,3200]{1,0:T(8,128)(2,1)S(1)} %get-tuple-element.170), channel_id=1, source_target_pairs={{0,5},{1,4},{2,7},{3,6},{4,1},{5,0},{6,3},{7,2},{8,13},{9,12},{10,... | collective-permute-start | bytes 307208 | tf_op jit(solution)/shard_map/ppermute | solution.py:49
  122.5 14.5 %collective-permute-start.28 = (bf16[16,3200]{1,0:T(8,128)(2,1)S(1)}, bf16[16,3200]{1,0:T(8,128)(2,1)S(1)}, u32[]{:S(2)}, u32[]{:S(2)}) collective-permute-start(bf16[16,3200]{1,0:T(8,128)(2,1)S(1)} %get-tuple-element.171), channel_id=1, source_target_pairs={{0,6},{1,7},{2,4},{3,5},{4,2},{5,3},{6,0},{7,1},{8,14},{9,15},{10,... | collective-permute-start | bytes 307208 | tf_op jit(solution)/shard_map/ppermute | solution.py:49
  125.0 12.0 %collective-permute-start.29 = (bf16[16,3200]{1,0:T(8,128)(2,1)S(1)}, bf16[16,3200]{1,0:T(8,128)(2,1)S(1)}, u32[]{:S(2)}, u32[]{:S(2)}) collective-permute-start(bf16[16,3200]{1,0:T(8,128)(2,1)S(1)} %get-tuple-element.172), channel_id=1, source_target_pairs={{0,7},{1,6},{2,5},{3,4},{4,3},{5,2},{6,1},{7,0},{8,15},{9,14},{10,... | collective-permute-start | bytes 307208 | tf_op jit(solution)/shard_map/ppermute | solution.py:49
  136.9 18.2 %collective-permute-start.34 = (bf16[2,256,2048]{2,1,0:T(8,128)(2,1)}, bf16[2,256,2048]{2,1,0:T(8,128)(2,1)S(1)}, u32[]{:S(2)}, u32[]{:S(2)}) collective-permute-start(bf16[2,256,2048]{2,1,0:T(8,128)(2,1)} %get-tuple-element.186.other_ref), channel_id=1, source_target_pairs={{0,8},{8,0},{16,24},{24,16},{1,9},{9,1},{17,25},{25,17},{2,10},{10... | collective-permute-start | bytes 6291464 | tf_op jit(solution)/shard_map/ppermute | solution.py:49
  137.1 18.0 %collective-permute-start.31 = (bf16[16,3072]{1,0:T(8,128)(2,1)S(1)}, bf16[16,3072]{1,0:T(8,128)(2,1)S(1)}, u32[]{:S(2)}, u32[]{:S(2)}) collective-permute-start(bf16[16,3072]{1,0:T(8,128)(2,1)S(1)} %slice.13.refs_0_), channel_id=1, source_target_pairs={{0,4},{1,5},{2,6},{3,7},{4,0},{5,1},{6,2},{7,3},{8,12},{9,13},{10,... | collective-permute-start | bytes 294920 | tf_op jit(solution)/shard_map/ppermute | solution.py:49
  141.8 13.4 %collective-permute-start.30 = (bf16[16,3072]{1,0:T(8,128)(2,1)S(1)}, bf16[16,3072]{1,0:T(8,128)(2,1)S(1)}, u32[]{:S(2)}, u32[]{:S(2)}) collective-permute-start(bf16[16,3072]{1,0:T(8,128)(2,1)S(1)} %slice.13.refs_0_), channel_id=1, source_target_pairs={{0,2},{1,3},{2,0},{3,1},{4,6},{5,7},{6,4},{7,5},{8,10},{9,11},{10,... | collective-permute-start | bytes 294920 | tf_op jit(solution)/shard_map/ppermute | solution.py:49
  141.8 13.4 %collective-permute-start.32 = (bf16[16,3072]{1,0:T(8,128)(2,1)S(1)}, bf16[16,3072]{1,0:T(8,128)(2,1)S(1)}, u32[]{:S(2)}, u32[]{:S(2)}) collective-permute-start(bf16[16,3072]{1,0:T(8,128)(2,1)S(1)} %slice.13.refs_0_), channel_id=1, source_target_pairs={{0,6},{1,7},{2,4},{3,5},{4,2},{5,3},{6,0},{7,1},{8,14},{9,15},{10,... | collective-permute-start | bytes 294920 | tf_op jit(solution)/shard_map/ppermute | solution.py:49
  156.0 12.4 %collective-permute-start.36 = (bf16[64,3072]{1,0:T(8,128)(2,1)}, bf16[64,3072]{1,0:T(8,128)(2,1)S(1)}, u32[]{:S(2)}, u32[]{:S(2)}) collective-permute-start(bf16[64,3072]{1,0:T(8,128)(2,1)} %join.5.even_ref), channel_id=1, source_target_pairs={{0,1},{1,0},{2,3},{3,2},{4,5},{5,4},{6,7},{7,6},{8,9},{9,8},{10,11... | collective-permute-start | bytes 1179656 | tf_op jit(solution)/shard_map/ppermute | solution.py:49
  (32 other events, 357.4 us)

commit v4 on v3

--- a/solution.py
+++ b/solution.py
@@ -56,6 +56,8 @@
 def join(parts):
     starts = [sum(part.shape[0] for part in parts[:n]) for n in range(len(parts))]
     total = starts[-1] + parts[-1].shape[0]
+    if len(parts) == 1:
+        return parts[0]
     if any(part.shape[0] % 16 for part in parts):
         return jnp.concatenate(parts, axis=0)
 
@@ -84,7 +86,7 @@
 def split_teacher(teacher):
     tokens, _, owners, piece = teacher.shape
     every = tokens * owners
-    cols = largest_tile(piece, 512, lanes)
+    cols = largest_tile(piece, 1024, lanes)
 
     def kernel(in_ref, *refs):
         outs, (stat_ref, peak_ref, total_ref) = refs[:owners], refs[owners:]
@@ -729,13 +731,12 @@
     queue = [*range(near - 1), near, near + 1, near - 1, *range(near + 2, count)]
     arrived = [exchange(blocks[s], "ba", s) if s else blocks[s] for s in queue[:middle]]
     pair = take_pair(head_weight)
-    teacher_stat, late, side, pair = lax.optimization_barrier(
-        (teacher_stat, [blocks[s] for s in queue[middle:]], side, pair)
+    arrived[0], teacher_stat, late, side, pair = lax.optimization_barrier(
+        (arrived[0], teacher_stat, [blocks[s] for s in queue[middle:]], side, pair)
     )
     hiddens = [hidden, beside, side, exchange(side, "aa", 1)]
     arrived += [exchange(block, "ba", s) for block, s in zip(late, queue[middle:])]
     teacher_stats = [teacher_stat, exchange(teacher_stat, "aa", 2)]
-    arrived[:middle], pair = lax.optimization_barrier((arrived[:middle], pair))
 
     def cross(parts):
         mine = join(parts)
@@ -744,12 +745,16 @@
     def swap(group):
         return group + [exchange(part, "aa", 1) for part in group]
 
-    group_a = cross(arrived[:middle])
+    group_own = cross(arrived[:1])
+    arrived[1:middle], group_own, pair = lax.optimization_barrier(
+        (arrived[1:middle], group_own, pair)
+    )
+    group_a = cross(arrived[1:middle])
     student, student_stat = student_logits(hiddens, pair)
     arrived[middle:], student_stat = lax.optimization_barrier((arrived[middle:], student_stat))
     packed = pack_stats([student_stat], teacher_stats)
     group_a, packed = lax.optimization_barrier((group_a, packed))
-    group_a = swap(group_a)
+    group_own, group_a = swap(group_own), swap(group_a)
     group_b = cross(arrived[middle:])
     packed = merge_two(packed, exchange(packed, "aa", 1))
     mask = 1
@@ -760,13 +765,15 @@
             left, met = lax.optimization_barrier((left, met))
         packed = merge_two(packed, met)
         mask *= 2
-    group_a, packed = lax.optimization_barrier((group_a, packed))
+    group_own, group_a, packed = lax.optimization_barrier((group_own, group_a, packed))
     sums = all_log_sums(packed, exchange(packed, "ba", mask))
     group_b, sums = lax.optimization_barrier((group_b, sums))
-    groups = [group_a, swap(group_b)]
+    groups = [group_own, group_a, swap(group_b)]
 
     order = [queue.index(s) for s in range(count)]
-    table = [n % middle if n < middle else n - middle for n in order] + [int(n >= middle) for n in order]
+    bounds = [0, 1, middle]
+    kinds = [int(n >= 1) + int(n >= middle) for n in order]
+    table = [n - bounds[kind] for n, kind in zip(order, kinds)] + kinds
 
     def plan(group):
         here = jnp.stack([near * group, me_b, core]).astype(jnp.int32)

time: 171 us -> 168 us (0.982)
  waiting for transfers between devices: 39.4 us -> 29.6 us
  starting transfers between devices: 42.2 us -> 50.7 us
    ppermute x37 -> x40, waiting for transfers between devices: 39.4 us -> 29.6 us  [exchange(): return lax.ppermute(value, axis, [(i, i ^ mask) for i in range(count)])]
    ppermute x37 -> x40, starting transfers between devices: 42.2 us -> 50.7 us  [exchange(): return lax.ppermute(value, axis, [(i, i ^ mask) for i in range(count)])]
  transfers between devices with their start and end apart: 37 -> 40, of which waited for: 13 -> 12; matrix products, arithmetic and copies ran while one was open for 0% -> 0% of each run, Pallas kernels for 43% -> 43%
where the time goes in v4:
time: 168 us; the launch traced here: 167 us
  Pallas kernels  82.2 us (49%)
  starting transfers between devices  50.7 us (30%)
  waiting for transfers between devices  29.6 us (18%)
  between operations  4.14 us (2%)
    ppermute x40, starting transfers between devices, exchange(): return lax.ppermute(value, axis, [(i, i ^ mask) for i in range(count)])  50.7 us
    ppermute x40, waiting for transfers between devices, exchange(): return lax.ppermute(value, axis, [(i, i ^ mask) for i in range(count)])  29.6 us
    pallas_call x1, Pallas kernels, student_logits(): pl.pallas_call(kernel, grid=(2, piece // cols), in_specs=[anywhere] * blo...  18.5 us
    pallas_call x2, Pallas kernels, head_pair(): pl.pallas_call(kernel, grid=(steps,), in_specs=[whole_vmem] + [pl.BlockSp...  18 us
    pallas_call x2, Pallas kernels, logit_gradient(): pl.pallas_call(kernel, grid_spec=pltpu.PrefetchScalarGridSpec(num_scalar_...  13.3 us
    pallas_call x1, Pallas kernels, hidden_share(): pl.pallas_call(kernel, in_specs=[anywhere] * 2, out_specs=[whole_vmem] *...  10.6 us
    pallas_call x1, Pallas kernels, take_pair(): pl.pallas_call(kernel, in_specs=[anywhere], out_specs=whole_vmem, out_sha...  10.5 us
    pallas_call x1, Pallas kernels, split_teacher(): pl.pallas_call(kernel, grid=(piece // cols,), in_specs=[pl.BlockSpec((tok...  4.52 us
  transfers between devices with their start and end apart: 40, of which 12 were waited for; matrix products, arithmetic and copies ran while one was open for 0% of the time, Pallas kernels for 43%

profile of v4, /device:TPU:0, one launch (start us, length us, event | category | flops | bytes accessed | tf_op | source)
XLA Modules:
  0.0 167.5 jit_solution(1080588079572383761)
XLA Ops:
  1.1 2.6 %collective-permute-start.5 = (bf16[128,3072]{1,0:T(8,128)(2,1)}, bf16[128,3072]{1,0:T(8,128)(2,1)S(1)}, u32[]{:S(2)}, u32[]{:S(2)}) collective-permute-start(bf16[128,3072]{1,0:T(8,128)(2,1)} %refs_0_.3), channel_id=1, source_target_pairs={{0,16},{8,24},{16,0},{24,8},{1,17},{9,25},{17,1},{25,9},{2,18},{10... | collective-permute-start | bytes 2359304 | tf_op jit(solution)/shard_map/ppermute | solution.py:49
  3.7 4.5 %split_teacher.1 = (bf16[64,2048]{1,0:T(8,128)(2,1)}, bf16[64,2048]{1,0:T(8,128)(2,1)}, bf16[64,2048]{1,0:T(8,128)(2,1)}, bf16[64,2048]{1,0:T(8,128)(2,1)}, bf16...) custom-call(bf16[64,1,8,2048]{3,2,1,0:T(8,128)(2,1)} %in_ref.1), custom_call_target="tpu_custom_call" | custom-call | tf_op jit(solution)/shard_map/split_teacher/pallas_call | solution.py:135
  11.4 2.6 %collective-permute-start.3 = (bf16[64,2048]{1,0:T(8,128)(2,1)}, bf16[64,2048]{1,0:T(8,128)(2,1)S(1)}, u32[]{:S(2)}, u32[]{:S(2)}) collective-permute-start(bf16[64,2048]{1,0:T(8,128)(2,1)} %get-tuple-element.117), channel_id=1, source_target_pairs={{0,4},{1,5},{2,6},{3,7},{4,0},{5,1},{6,2},{7,3},{8,12},{9,13},{10,... | collective-permute-start | bytes 786440 | tf_op jit(solution)/shard_map/ppermute | solution.py:49
  14.3 10.5 %take_pair.1.refs_4_.w_ref = bf16[2,3072,2048]{2,1,0:T(8,128)(2,1)S(1)} custom-call(bf16[3072,1,4,2048]{3,2,1,0:T(4,128)(2,1)} %w_ref), custom_call_target="tpu_custom_call" | custom-call | flops 12884901888 | bytes 25165824 | tf_op jit(solution)/shard_map/take_pair/pallas_call | solution.py:181
  25.5 7.5 %collective-permute-done.3.refs_2_ = bf16[64,2048]{1,0:T(8,128)(2,1)S(1)} collective-permute-done((bf16[64,2048]{1,0:T(8,128)(2,1)}, bf16[64,2048]{1,0:T(8,128)(2,1)S(1)}, u32[]{:S(2)}, u32[]{:S(2)}) %collective-permute-start.3) | collective-permute-done | bytes 262176 | tf_op jit(solution)/shard_map/ppermute | solution.py:49
  33.0 4.2 %collective-permute-done.4.refs_3_ = bf16[64,2048]{1,0:T(8,128)(2,1)S(1)} collective-permute-done((bf16[64,2048]{1,0:T(8,128)(2,1)}, bf16[64,2048]{1,0:T(8,128)(2,1)S(1)}, u32[]{:S(2)}, u32[]{:S(2)}) %collective-permute-start.4) | collective-permute-done | bytes 262176 | tf_op jit(solution)/shard_map/ppermute | solution.py:49
  38.9 2.5 %collective-permute-start.11 = (bf16[64,2048]{1,0:T(8,128)(2,1)S(1)}, bf16[64,2048]{1,0:T(8,128)(2,1)S(1)}, u32[]{:S(2)}, u32[]{:S(2)}) collective-permute-start(bf16[64,2048]{1,0:T(8,128)(2,1)S(1)} %copy-done.20), channel_id=1, source_target_pairs={{0,6},{1,7},{2,4},{3,5},{4,2},{5,3},{6,0},{7,1},{8,14},{9,15},{10,... | collective-permute-start | bytes 786440 | tf_op jit(solution)/shard_map/ppermute | solution.py:49
  41.4 2.3 %collective-permute-start.12 = (bf16[64,2048]{1,0:T(8,128)(2,1)S(1)}, bf16[64,2048]{1,0:T(8,128)(2,1)S(1)}, u32[]{:S(2)}, u32[]{:S(2)}) collective-permute-start(bf16[64,2048]{1,0:T(8,128)(2,1)S(1)} %copy-done.19), channel_id=1, source_target_pairs={{0,7},{1,6},{2,5},{3,4},{4,3},{5,2},{6,1},{7,0},{8,15},{9,14},{10,... | collective-permute-start | bytes 786440 | tf_op jit(solution)/shard_map/ppermute | solution.py:49
  45.2 18.5 %student_logits.1 = (f32[2,512,2048]{2,1,0:T(8,128)}, f32[8,512]{1,0:T(8,128)S(1)}) custom-call(bf16[128,3072]{1,0:T(8,128)(2,1)} %refs_0_.3, bf16[128,3072]{1,0:T(8,128)(2,1)} %copy-done.7, bf16[128,3072]{1,0:T(8,128)(2,1)} %copy-done.8, bf16[128,3072]{1,0:T(8,128)(2,1)} %copy-done.9, bf16[2,3072,2048]{2,1,0:T(8,128)(2,1)S(1)} %take_pair.1.refs_4_.w_ref), custom_call_target="tpu_custom_call" | custom-call | flops 1 | bytes 1 | tf_op jit(solution)/shard_map/student_logits/pallas_call | solution.py:258
  71.9 3.3 %collective-permute-start.19 = (f32[8,512]{1,0:T(8,128)S(1)}, f32[8,512]{1,0:T(8,128)S(1)}, u32[]{:S(2)}, u32[]{:S(2)}) collective-permute-start(f32[8,512]{1,0:T(8,128)S(1)} %merge_two.4.a_ref), channel_id=1, source_target_pairs={{0,2},{1,3},{2,0},{3,1},{4,6},{5,7},{6,4},{7,5},{8,10},{9,11},{10,... | collective-permute-start | bytes 49160 | tf_op jit(solution)/shard_map/ppermute | solution.py:49
  78.6 3.1 %collective-permute-start.21 = (f32[8,512]{1,0:T(8,128)S(1)}, f32[8,512]{1,0:T(8,128)S(1)}, u32[]{:S(2)}, u32[]{:S(2)}) collective-permute-start(f32[8,512]{1,0:T(8,128)S(1)} %merge_two.5.a_ref), channel_id=1, source_target_pairs={{0,4},{1,5},{2,6},{3,7},{4,0},{5,1},{6,2},{7,3},{8,12},{9,13},{10,... | collective-permute-start | bytes 49160 | tf_op jit(solution)/shard_map/ppermute | solution.py:49
  85.8 2.0 %collective-permute-done.22.refs_10_ = bf16[192,2048]{1,0:T(8,128)(2,1)S(1)} collective-permute-done((bf16[192,2048]{1,0:T(8,128)(2,1)S(1)}, bf16[192,2048]{1,0:T(8,128)(2,1)S(1)}, u32[]{:S(2)}, u32[]{:S(2)}) %collective-permute-start.22) | collective-permute-done | bytes 786464 | tf_op jit(solution)/shard_map/ppermute | solution.py:49
  88.7 6.5 %logit_gradient.2 = (bf16[2,256,2048]{2,1,0:T(8,128)(2,1)}, f32[8,128]{1,0:T(8,128)S(1)}) custom-call(s32[19]{0:T(128)S(1)} %get-tuple-element.212.plan_ref, bf16[64,2048]{1,0:T(8,128)(2,1)} %get-tuple-element.146.refs_0_, bf16[64,2048]{1,0:T(8,128)(2,1)} %copy-done.15, bf16[64,2048]{1,0:T(8,128)(2,1)} %copy-done.16, bf16[64,2048]{1,0:T(8,128)(2,1)} %copy-done.17, ...), custom_call_target="tpu_custom_call" | custom-call | flops 4194304 | bytes 8388608 | tf_op jit(solution)/shard_map/logit_gradient/pallas_call | solution.py:426
  95.5 10.6 %hidden_share.1 = (f32[128,3072]{1,0:T(8,128)S(1)}, bf16[128,3072]{1,0:T(8,128)(2,1)S(1)}) custom-call(bf16[2,256,2048]{2,1,0:T(8,128)(2,1)} %get-tuple-element.197.given_ref.own_ref, bf16[2,3072,2048]{2,1,0:T(8,128)(2,1)} %copy-done), custom_call_target="tpu_custom_call" | custom-call | flops 6442450944 | bytes 25165824 | tf_op jit(solution)/shard_map/hidden_share/pallas_call | solution.py:504
  106.6 1.9 %collective-permute-done.25.arrived_ref = bf16[128,3072]{1,0:T(8,128)(2,1)S(1)} collective-permute-done((bf16[128,3072]{1,0:T(8,128)(2,1)S(1)}, bf16[128,3072]{1,0:T(8,128)(2,1)S(1)}, u32[]{:S(2)}, u32[]{:S(2)}) %collective-permute-start.25) | collective-permute-done | bytes 786464 | tf_op jit(solution)/shard_map/ppermute | solution.py:49
  109.6 4.0 %collective-permute-start.27 = (bf16[16,3200]{1,0:T(8,128)(2,1)S(1)}, bf16[16,3200]{1,0:T(8,128)(2,1)S(1)}, u32[]{:S(2)}, u32[]{:S(2)}) collective-permute-start(bf16[16,3200]{1,0:T(8,128)(2,1)S(1)} %get-tuple-element.179), channel_id=1, source_target_pairs={{0,2},{1,3},{2,0},{3,1},{4,6},{5,7},{6,4},{7,5},{8,10},{9,11},{10,... | collective-permute-start | bytes 307208 | tf_op jit(solution)/shard_map/ppermute | solution.py:49
  113.5 3.0 %collective-permute-start.29 = (bf16[16,3200]{1,0:T(8,128)(2,1)S(1)}, bf16[16,3200]{1,0:T(8,128)(2,1)S(1)}, u32[]{:S(2)}, u32[]{:S(2)}) collective-permute-start(bf16[16,3200]{1,0:T(8,128)(2,1)S(1)} %get-tuple-element.181), channel_id=1, source_target_pairs={{0,4},{1,5},{2,6},{3,7},{4,0},{5,1},{6,2},{7,3},{8,12},{9,13},{10,... | collective-permute-start | bytes 307208 | tf_op jit(solution)/shard_map/ppermute | solution.py:49
  117.5 2.4 %collective-permute-start.31 = (bf16[16,3200]{1,0:T(8,128)(2,1)S(1)}, bf16[16,3200]{1,0:T(8,128)(2,1)S(1)}, u32[]{:S(2)}, u32[]{:S(2)}) collective-permute-start(bf16[16,3200]{1,0:T(8,128)(2,1)S(1)} %get-tuple-element.183), channel_id=1, source_target_pairs={{0,6},{1,7},{2,4},{3,5},{4,2},{5,3},{6,0},{7,1},{8,14},{9,15},{10,... | collective-permute-start | bytes 307208 | tf_op jit(solution)/shard_map/ppermute | solution.py:49
  121.3 6.8 %logit_gradient.3 = (bf16[2,256,2048]{2,1,0:T(8,128)(2,1)}, f32[8,128]{1,0:T(8,128)}) custom-call(s32[19]{0:T(128)S(1)} %get-tuple-element.211.plan_ref, bf16[64,2048]{1,0:T(8,128)(2,1)} %get-tuple-element.146.refs_0_, bf16[64,2048]{1,0:T(8,128)(2,1)} %copy-done.15, bf16[64,2048]{1,0:T(8,128)(2,1)} %copy-done.16, bf16[64,2048]{1,0:T(8,128)(2,1)} %copy-done.17, ...), custom_call_target="tpu_custom_call" | custom-call | flops 4194304 | bytes 8388608 | tf_op jit(solution)/shard_map/logit_gradient/pallas_call | solution.py:426
  128.2 3.9 %collective-permute-done.30 = bf16[16,3200]{1,0:T(8,128)(2,1)S(1)} collective-permute-done((bf16[16,3200]{1,0:T(8,128)(2,1)S(1)}, bf16[16,3200]{1,0:T(8,128)(2,1)S(1)}, u32[]{:S(2)}, u32[]{:S(2)}) %collective-permute-start.30) | collective-permute-done | bytes 102432 | tf_op jit(solution)/shard_map/ppermute | solution.py:49
  132.2 5.0 %collective-permute-start.34 = (bf16[16,3072]{1,0:T(8,128)(2,1)S(1)}, bf16[16,3072]{1,0:T(8,128)(2,1)S(1)}, u32[]{:S(2)}, u32[]{:S(2)}) collective-permute-start(bf16[16,3072]{1,0:T(8,128)(2,1)S(1)} %slice.13.refs_0_), channel_id=1, source_target_pairs={{0,4},{1,5},{2,6},{3,7},{4,0},{5,1},{6,2},{7,3},{8,12},{9,13},{10,... | collective-permute-start | bytes 294920 | tf_op jit(solution)/shard_map/ppermute | solution.py:49
  140.8 9.0 %head_pair.2.refs_0_ = bf16[768,1,4,2048]{3,2,1,0:T(4,128)(2,1)} custom-call(bf16[768,512]{1,0:T(8,128)(2,1)S(1)} %turn_features.1.left_ref, bf16[2,256,2048]{2,1,0:T(8,128)(2,1)} %get-tuple-element.197.given_ref.own_ref, bf16[2,256,2048]{2,1,0:T(8,128)(2,1)} %get-tuple-element.198.other_ref), custom_call_target="tpu_custom_call" | custom-call | flops 3221225472 | bytes 6291456 | tf_op jit(solution)/shard_map/head_pair/pallas_call | solution.py:694
  152.9 2.8 %collective-permute-start.38 = (f32[1]{0:T(128)}, f32[1]{0:T(128)}, u32[]{:S(2)}, u32[]{:S(2)}) collective-permute-start(f32[1]{0:T(128)} %add.40), channel_id=1, source_target_pairs={{0,16},{8,24},{16,0},{24,8},{1,17},{9,25},{17,1},{25,9},{2,18},{10... | collective-permute-start | bytes 20 | tf_op jit(solution)/shard_map/ppermute | solution.py:49
  155.7 9.0 %head_pair.3 = bf16[768,1,4,2048]{3,2,1,0:T(4,128)(2,1)} custom-call(bf16[768,512]{1,0:T(8,128)(2,1)S(1)} %turn_features.1.left_ref, bf16[2,256,2048]{2,1,0:T(8,128)(2,1)} %copy-done.12, bf16[2,256,2048]{2,1,0:T(8,128)(2,1)} %copy-done.13, bf16[768,1,4,2048]{3,2,1,0:T(4,128)(2,1)} %head_pair.2.refs_0_), custom_call_target="tpu_custom_call", output_to_operand_aliasing={{}: (3, {})} | custom-call | flops 3221225472 | bytes 6291456 | tf_op jit(solution)/shard_map/head_pair/pallas_call | solution.py:694
  (123 shorter events, 34.9 us)
Async XLA Ops:
  1.1 23.7 %collective-permute-start.5 = (bf16[128,3072]{1,0:T(8,128)(2,1)}, bf16[128,3072]{1,0:T(8,128)(2,1)S(1)}, u32[]{:S(2)}, u32[]{:S(2)}) collective-permute-start(bf16[128,3072]{1,0:T(8,128)(2,1)} %refs_0_.3), channel_id=1, source_target_pairs={{0,16},{8,24},{16,0},{24,8},{1,17},{9,25},{17,1},{25,9},{2,18},{10... | collective-permute-start | bytes 2359304 | tf_op jit(solution)/shard_map/ppermute | solution.py:49
  8.3 17.2 %collective-permute-start.1 = (bf16[64,2048]{1,0:T(8,128)(2,1)}, bf16[64,2048]{1,0:T(8,128)(2,1)S(1)}, u32[]{:S(2)}, u32[]{:S(2)}) collective-permute-start(bf16[64,2048]{1,0:T(8,128)(2,1)} %get-tuple-element.115), channel_id=1, source_target_pairs={{0,1},{1,0},{2,3},{3,2},{4,5},{5,4},{6,7},{7,6},{8,9},{9,8},{10,11... | collective-permute-start | bytes 786440 | tf_op jit(solution)/shard_map/ppermute | solution.py:49
  9.8 15.6 %collective-permute-start.2 = (bf16[64,2048]{1,0:T(8,128)(2,1)}, bf16[64,2048]{1,0:T(8,128)(2,1)S(1)}, u32[]{:S(2)}, u32[]{:S(2)}) collective-permute-start(bf16[64,2048]{1,0:T(8,128)(2,1)} %get-tuple-element.116), channel_id=1, source_target_pairs={{0,2},{1,3},{2,0},{3,1},{4,6},{5,7},{6,4},{7,5},{8,10},{9,11},{10,... | collective-permute-start | bytes 786440 | tf_op jit(solution)/shard_map/ppermute | solution.py:49
  11.4 21.6 %collective-permute-start.3 = (bf16[64,2048]{1,0:T(8,128)(2,1)}, bf16[64,2048]{1,0:T(8,128)(2,1)S(1)}, u32[]{:S(2)}, u32[]{:S(2)}) collective-permute-start(bf16[64,2048]{1,0:T(8,128)(2,1)} %get-tuple-element.117), channel_id=1, source_target_pairs={{0,4},{1,5},{2,6},{3,7},{4,0},{5,1},{6,2},{7,3},{8,12},{9,13},{10,... | collective-permute-start | bytes 786440 | tf_op jit(solution)/shard_map/ppermute | solution.py:49
  14.0 23.2 %collective-permute-start.4 = (bf16[64,2048]{1,0:T(8,128)(2,1)}, bf16[64,2048]{1,0:T(8,128)(2,1)S(1)}, u32[]{:S(2)}, u32[]{:S(2)}) collective-permute-start(bf16[64,2048]{1,0:T(8,128)(2,1)} %get-tuple-element.118), channel_id=1, source_target_pairs={{0,5},{1,4},{2,7},{3,6},{4,1},{5,0},{6,3},{7,2},{8,13},{9,12},{10,... | collective-permute-start | bytes 786440 | tf_op jit(solution)/shard_map/ppermute | solution.py:49
  24.9 12.3 %collective-permute-start.6 = (bf16[64,2048]{1,0:T(8,128)(2,1)S(1)}, bf16[64,2048]{1,0:T(8,128)(2,1)S(1)}, u32[]{:S(2)}, u32[]{:S(2)}) collective-permute-start(bf16[64,2048]{1,0:T(8,128)(2,1)S(1)} %copy-done.14), channel_id=1, source_target_pairs={{0,16},{8,24},{16,0},{24,8},{1,17},{9,25},{17,1},{25,9},{2,18},{10... | collective-permute-start | bytes 786440 | tf_op jit(solution)/shard_map/ppermute | solution.py:49
  38.2 25.6 %collective-permute-start.9 = (bf16[256,2048]{1,0:T(8,128)(2,1)}, bf16[256,2048]{1,0:T(8,128)(2,1)S(1)}, u32[]{:S(2)}, u32[]{:S(2)}) collective-permute-start(bf16[256,2048]{1,0:T(8,128)(2,1)} %join.3.refs_4_), channel_id=1, source_target_pairs={{0,16},{8,24},{16,0},{24,8},{1,17},{9,25},{17,1},{25,9},{2,18},{10... | collective-permute-start | bytes 3145736 | tf_op jit(solution)/shard_map/ppermute | solution.py:49
  38.8 24.9 %collective-permute-start.10 = (bf16[64,2048]{1,0:T(8,128)(2,1)S(1)}, bf16[64,2048]{1,0:T(8,128)(2,1)S(1)}, u32[]{:S(2)}, u32[]{:S(2)}) collective-permute-start(bf16[64,2048]{1,0:T(8,128)(2,1)S(1)} %copy-done.21), channel_id=1, source_target_pairs={{0,3},{1,2},{2,1},{3,0},{4,7},{5,6},{6,5},{7,4},{8,11},{9,10},{10,... | collective-permute-start | bytes 786440 | tf_op jit(solution)/shard_map/ppermute | solution.py:49
  38.9 24.9 %collective-permute-start.11 = (bf16[64,2048]{1,0:T(8,128)(2,1)S(1)}, bf16[64,2048]{1,0:T(8,128)(2,1)S(1)}, u32[]{:S(2)}, u32[]{:S(2)}) collective-permute-start(bf16[64,2048]{1,0:T(8,128)(2,1)S(1)} %copy-done.20), channel_id=1, source_target_pairs={{0,6},{1,7},{2,4},{3,5},{4,2},{5,3},{6,0},{7,1},{8,14},{9,15},{10,... | collective-permute-start | bytes 786440 | tf_op jit(solution)/shard_map/ppermute | solution.py:49
  41.4 22.4 %collective-permute-start.12 = (bf16[64,2048]{1,0:T(8,128)(2,1)S(1)}, bf16[64,2048]{1,0:T(8,128)(2,1)S(1)}, u32[]{:S(2)}, u32[]{:S(2)}) collective-permute-start(bf16[64,2048]{1,0:T(8,128)(2,1)S(1)} %copy-done.19), channel_id=1, source_target_pairs={{0,7},{1,6},{2,5},{3,4},{4,3},{5,2},{6,1},{7,0},{8,15},{9,14},{10,... | collective-permute-start | bytes 786440 | tf_op jit(solution)/shard_map/ppermute | solution.py:49
  43.7 20.1 %collective-permute-start.14 = (f32[8,512]{1,0:T(8,128)S(1)}, f32[8,512]{1,0:T(8,128)S(1)}, u32[]{:S(2)}, u32[]{:S(2)}) collective-permute-start(f32[8,512]{1,0:T(8,128)S(1)} %get-tuple-element.141.refs_1_), channel_id=1, source_target_pairs={{0,16},{8,24},{16,0},{24,8},{1,17},{9,25},{17,1},{25,9},{2,18},{10... | collective-permute-start | bytes 49160 | tf_op jit(solution)/shard_map/ppermute | solution.py:49
  63.8 14.7 %collective-permute-start.15 = (bf16[256,2048]{1,0:T(8,128)(2,1)S(1)}, bf16[256,2048]{1,0:T(8,128)(2,1)S(1)}, u32[]{:S(2)}, u32[]{:S(2)}) collective-permute-start(bf16[256,2048]{1,0:T(8,128)(2,1)S(1)} %copy-done.2), channel_id=1, source_target_pairs={{0,8},{8,0},{16,24},{24,16},{1,9},{9,1},{17,25},{25,17},{2,10},{10... | collective-permute-start | bytes 3145736 | tf_op jit(solution)/shard_map/ppermute | solution.py:49
  63.9 14.6 %collective-permute-start.16 = (bf16[256,2048]{1,0:T(8,128)(2,1)S(1)}, bf16[256,2048]{1,0:T(8,128)(2,1)S(1)}, u32[]{:S(2)}, u32[]{:S(2)}) collective-permute-start(bf16[256,2048]{1,0:T(8,128)(2,1)S(1)} %collective-permute-done.9.refs_5_), channel_id=1, source_target_pairs={{0,8},{8,0},{16,24},{24,16},{1,9},{9,1},{17,25},{25,17},{2,10},{10... | collective-permute-start | bytes 3145736 | tf_op jit(solution)/shard_map/ppermute | solution.py:49
  65.4 19.8 %collective-permute-start.20 = (bf16[192,2048]{1,0:T(8,128)(2,1)}, bf16[192,2048]{1,0:T(8,128)(2,1)S(1)}, u32[]{:S(2)}, u32[]{:S(2)}) collective-permute-start(bf16[192,2048]{1,0:T(8,128)(2,1)} %join.4.refs_8_), channel_id=1, source_target_pairs={{0,16},{8,24},{16,0},{24,8},{1,17},{9,25},{17,1},{25,9},{2,18},{10... | collective-permute-start | bytes 2359304 | tf_op jit(solution)/shard_map/ppermute | solution.py:49
  95.3 13.4 %collective-permute-start.24 = (bf16[2,256,2048]{2,1,0:T(8,128)(2,1)}, bf16[2,256,2048]{2,1,0:T(8,128)(2,1)S(1)}, u32[]{:S(2)}, u32[]{:S(2)}) collective-permute-start(bf16[2,256,2048]{2,1,0:T(8,128)(2,1)} %get-tuple-element.197.given_ref.own_ref), channel_id=1, source_target_pairs={{0,8},{8,0},{16,24},{24,16},{1,9},{9,1},{17,25},{25,17},{2,10},{10... | collective-permute-start | bytes 6291464 | tf_op jit(solution)/shard_map/ppermute | solution.py:49
  113.5 14.6 %collective-permute-start.28 = (bf16[16,3200]{1,0:T(8,128)(2,1)S(1)}, bf16[16,3200]{1,0:T(8,128)(2,1)S(1)}, u32[]{:S(2)}, u32[]{:S(2)}) collective-permute-start(bf16[16,3200]{1,0:T(8,128)(2,1)S(1)} %get-tuple-element.180), channel_id=1, source_target_pairs={{0,3},{1,2},{2,1},{3,0},{4,7},{5,6},{6,5},{7,4},{8,11},{9,10},{10,... | collective-permute-start | bytes 307208 | tf_op jit(solution)/shard_map/ppermute | solution.py:49
  113.5 14.6 %collective-permute-start.29 = (bf16[16,3200]{1,0:T(8,128)(2,1)S(1)}, bf16[16,3200]{1,0:T(8,128)(2,1)S(1)}, u32[]{:S(2)}, u32[]{:S(2)}) collective-permute-start(bf16[16,3200]{1,0:T(8,128)(2,1)S(1)} %get-tuple-element.181), channel_id=1, source_target_pairs={{0,4},{1,5},{2,6},{3,7},{4,0},{5,1},{6,2},{7,3},{8,12},{9,13},{10,... | collective-permute-start | bytes 307208 | tf_op jit(solution)/shard_map/ppermute | solution.py:49
  116.5 15.5 %collective-permute-start.30 = (bf16[16,3200]{1,0:T(8,128)(2,1)S(1)}, bf16[16,3200]{1,0:T(8,128)(2,1)S(1)}, u32[]{:S(2)}, u32[]{:S(2)}) collective-permute-start(bf16[16,3200]{1,0:T(8,128)(2,1)S(1)} %get-tuple-element.182), channel_id=1, source_target_pairs={{0,5},{1,4},{2,7},{3,6},{4,1},{5,0},{6,3},{7,2},{8,13},{9,12},{10,... | collective-permute-start | bytes 307208 | tf_op jit(solution)/shard_map/ppermute | solution.py:49
  117.5 14.5 %collective-permute-start.31 = (bf16[16,3200]{1,0:T(8,128)(2,1)S(1)}, bf16[16,3200]{1,0:T(8,128)(2,1)S(1)}, u32[]{:S(2)}, u32[]{:S(2)}) collective-permute-start(bf16[16,3200]{1,0:T(8,128)(2,1)S(1)} %get-tuple-element.183), channel_id=1, source_target_pairs={{0,6},{1,7},{2,4},{3,5},{4,2},{5,3},{6,0},{7,1},{8,14},{9,15},{10,... | collective-permute-start | bytes 307208 | tf_op jit(solution)/shard_map/ppermute | solution.py:49
  132.0 18.5 %collective-permute-start.37 = (bf16[2,256,2048]{2,1,0:T(8,128)(2,1)}, bf16[2,256,2048]{2,1,0:T(8,128)(2,1)S(1)}, u32[]{:S(2)}, u32[]{:S(2)}) collective-permute-start(bf16[2,256,2048]{2,1,0:T(8,128)(2,1)} %get-tuple-element.198.other_ref), channel_id=1, source_target_pairs={{0,8},{8,0},{16,24},{24,16},{1,9},{9,1},{17,25},{25,17},{2,10},{10... | collective-permute-start | bytes 6291464 | tf_op jit(solution)/shard_map/ppermute | solution.py:49
  132.2 18.3 %collective-permute-start.34 = (bf16[16,3072]{1,0:T(8,128)(2,1)S(1)}, bf16[16,3072]{1,0:T(8,128)(2,1)S(1)}, u32[]{:S(2)}, u32[]{:S(2)}) collective-permute-start(bf16[16,3072]{1,0:T(8,128)(2,1)S(1)} %slice.13.refs_0_), channel_id=1, source_target_pairs={{0,4},{1,5},{2,6},{3,7},{4,0},{5,1},{6,2},{7,3},{8,12},{9,13},{10,... | collective-permute-start | bytes 294920 | tf_op jit(solution)/shard_map/ppermute | solution.py:49
  137.2 13.3 %collective-permute-start.33 = (bf16[16,3072]{1,0:T(8,128)(2,1)S(1)}, bf16[16,3072]{1,0:T(8,128)(2,1)S(1)}, u32[]{:S(2)}, u32[]{:S(2)}) collective-permute-start(bf16[16,3072]{1,0:T(8,128)(2,1)S(1)} %slice.13.refs_0_), channel_id=1, source_target_pairs={{0,2},{1,3},{2,0},{3,1},{4,6},{5,7},{6,4},{7,5},{8,10},{9,11},{10,... | collective-permute-start | bytes 294920 | tf_op jit(solution)/shard_map/ppermute | solution.py:49
  137.2 13.3 %collective-permute-start.35 = (bf16[16,3072]{1,0:T(8,128)(2,1)S(1)}, bf16[16,3072]{1,0:T(8,128)(2,1)S(1)}, u32[]{:S(2)}, u32[]{:S(2)}) collective-permute-start(bf16[16,3072]{1,0:T(8,128)(2,1)S(1)} %slice.13.refs_0_), channel_id=1, source_target_pairs={{0,6},{1,7},{2,4},{3,5},{4,2},{5,3},{6,0},{7,1},{8,14},{9,15},{10,... | collective-permute-start | bytes 294920 | tf_op jit(solution)/shard_map/ppermute | solution.py:49
  151.4 14.0 %collective-permute-start.39 = (bf16[64,3072]{1,0:T(8,128)(2,1)}, bf16[64,3072]{1,0:T(8,128)(2,1)S(1)}, u32[]{:S(2)}, u32[]{:S(2)}) collective-permute-start(bf16[64,3072]{1,0:T(8,128)(2,1)} %join.5.even_ref), channel_id=1, source_target_pairs={{0,1},{1,0},{2,3},{3,2},{4,5},{5,4},{6,7},{7,6},{8,9},{9,8},{10,11... | collective-permute-start | bytes 1179656 | tf_op jit(solution)/shard_map/ppermute | solution.py:49
  (38 other events, 415.9 us)

commit v5 on v4

--- a/solution.py
+++ b/solution.py
@@ -794,7 +794,6 @@
     summed = summed[:, :width].astype(bf16)
 
     other_met = exchange(grad_other, "aa", 1)
-    divergence = divergence + exchange(divergence, "aa", 1)
     gathered = [summed] + [exchange(summed, "ba", s) for s in range(2, count, 2)]
     grad_own, gathered[0] = lax.optimization_barrier((grad_own, gathered[0]))
     grad_head = head_pair(left, grad_own, grad_other, 0, None)
@@ -803,11 +802,12 @@
     )
     even = join(gathered)
     odd = exchange(even, "ba", 1)
-    divergence = divergence + exchange(divergence, "aa", 2)
+    beside, side, across = [exchange(divergence, "aa", m) for m in (1, 2, 3)]
     even, other_met = lax.optimization_barrier((even, other_met))
     grad_head = head_pair(left, own_met, other_met, 1, grad_head)
     odd, grad_head = lax.optimization_barrier((odd, grad_head))
     grad_hidden = put_together(even, odd, summed.shape[0])
+    divergence = (divergence + beside) + (side + across)
     return divergence[0], grad_hidden, grad_head
 
 

time: 168 us -> 170 us (1.012)
    ppermute x40 -> x41, starting transfers between devices: 50.7 us -> 51.9 us  [exchange(): return lax.ppermute(value, axis, [(i, i ^ mask) for i in range(count)])]
    ppermute x40 -> x41, waiting for transfers between devices: 29.6 us -> 29.6 us  [exchange(): return lax.ppermute(value, axis, [(i, i ^ mask) for i in range(count)])]
  transfers between devices with their start and end apart: 40 -> 41, of which waited for: 12 -> 12; matrix products, arithmetic and copies ran while one was open for 0% -> 0% of each run, Pallas kernels for 43% -> 43%
where the time goes in v5:
time: 170 us; the launch traced here: 169 us
  Pallas kernels  82.1 us (48%)
  starting transfers between devices  51.9 us (31%)
  waiting for transfers between devices  29.6 us (17%)
  between operations  4.82 us (3%)
    ppermute x41, starting transfers between devices, exchange(): return lax.ppermute(value, axis, [(i, i ^ mask) for i in range(count)])  51.9 us
    ppermute x41, waiting for transfers between devices, exchange(): return lax.ppermute(value, axis, [(i, i ^ mask) for i in range(count)])  29.6 us
    pallas_call x1, Pallas kernels, student_logits(): pl.pallas_call(kernel, grid=(2, piece // cols), in_specs=[anywhere] * blo...  18.5 us
    pallas_call x2, Pallas kernels, head_pair(): pl.pallas_call(kernel, grid=(steps,), in_specs=[whole_vmem] + [pl.BlockSp...  18 us
    pallas_call x2, Pallas kernels, logit_gradient(): pl.pallas_call(kernel, grid_spec=pltpu.PrefetchScalarGridSpec(num_scalar_...  13.3 us
    pallas_call x1, Pallas kernels, hidden_share(): pl.pallas_call(kernel, in_specs=[anywhere] * 2, out_specs=[whole_vmem] *...  10.6 us
    pallas_call x1, Pallas kernels, take_pair(): pl.pallas_call(kernel, in_specs=[anywhere], out_specs=whole_vmem, out_sha...  10.5 us
    pallas_call x1, Pallas kernels, split_teacher(): pl.pallas_call(kernel, grid=(piece // cols,), in_specs=[pl.BlockSpec((tok...  4.52 us
  transfers between devices with their start and end apart: 41, of which 12 were waited for; matrix products, arithmetic and copies ran while one was open for 0% of the time, Pallas kernels for 43%

profile of v5, /device:TPU:0, one launch (start us, length us, event | category | flops | bytes accessed | tf_op | source)
XLA Modules:
  0.0 169.4 jit_solution(12346330526065962965)
XLA Ops:
  1.1 2.6 %collective-permute-start.5 = (bf16[128,3072]{1,0:T(8,128)(2,1)}, bf16[128,3072]{1,0:T(8,128)(2,1)S(1)}, u32[]{:S(2)}, u32[]{:S(2)}) collective-permute-start(bf16[128,3072]{1,0:T(8,128)(2,1)} %refs_0_.3), channel_id=1, source_target_pairs={{0,16},{8,24},{16,0},{24,8},{1,17},{9,25},{17,1},{25,9},{2,18},{10... | collective-permute-start | bytes 2359304 | tf_op jit(solution)/shard_map/ppermute | solution.py:49
  3.7 4.5 %split_teacher.1 = (bf16[64,2048]{1,0:T(8,128)(2,1)}, bf16[64,2048]{1,0:T(8,128)(2,1)}, bf16[64,2048]{1,0:T(8,128)(2,1)}, bf16[64,2048]{1,0:T(8,128)(2,1)}, bf16...) custom-call(bf16[64,1,8,2048]{3,2,1,0:T(8,128)(2,1)} %in_ref.1), custom_call_target="tpu_custom_call" | custom-call | tf_op jit(solution)/shard_map/split_teacher/pallas_call | solution.py:135
  11.4 2.6 %collective-permute-start.3 = (bf16[64,2048]{1,0:T(8,128)(2,1)}, bf16[64,2048]{1,0:T(8,128)(2,1)S(1)}, u32[]{:S(2)}, u32[]{:S(2)}) collective-permute-start(bf16[64,2048]{1,0:T(8,128)(2,1)} %get-tuple-element.117), channel_id=1, source_target_pairs={{0,4},{1,5},{2,6},{3,7},{4,0},{5,1},{6,2},{7,3},{8,12},{9,13},{10,... | collective-permute-start | bytes 786440 | tf_op jit(solution)/shard_map/ppermute | solution.py:49
  14.3 10.5 %take_pair.1.refs_4_.w_ref = bf16[2,3072,2048]{2,1,0:T(8,128)(2,1)S(1)} custom-call(bf16[3072,1,4,2048]{3,2,1,0:T(4,128)(2,1)} %w_ref), custom_call_target="tpu_custom_call" | custom-call | flops 12884901888 | bytes 25165824 | tf_op jit(solution)/shard_map/take_pair/pallas_call | solution.py:181
  25.5 7.5 %collective-permute-done.3.refs_2_ = bf16[64,2048]{1,0:T(8,128)(2,1)S(1)} collective-permute-done((bf16[64,2048]{1,0:T(8,128)(2,1)}, bf16[64,2048]{1,0:T(8,128)(2,1)S(1)}, u32[]{:S(2)}, u32[]{:S(2)}) %collective-permute-start.3) | collective-permute-done | bytes 262176 | tf_op jit(solution)/shard_map/ppermute | solution.py:49
  33.0 4.2 %collective-permute-done.4.refs_3_ = bf16[64,2048]{1,0:T(8,128)(2,1)S(1)} collective-permute-done((bf16[64,2048]{1,0:T(8,128)(2,1)}, bf16[64,2048]{1,0:T(8,128)(2,1)S(1)}, u32[]{:S(2)}, u32[]{:S(2)}) %collective-permute-start.4) | collective-permute-done | bytes 262176 | tf_op jit(solution)/shard_map/ppermute | solution.py:49
  38.8 2.5 %collective-permute-start.11 = (bf16[64,2048]{1,0:T(8,128)(2,1)S(1)}, bf16[64,2048]{1,0:T(8,128)(2,1)S(1)}, u32[]{:S(2)}, u32[]{:S(2)}) collective-permute-start(bf16[64,2048]{1,0:T(8,128)(2,1)S(1)} %copy-done.20), channel_id=1, source_target_pairs={{0,6},{1,7},{2,4},{3,5},{4,2},{5,3},{6,0},{7,1},{8,14},{9,15},{10,... | collective-permute-start | bytes 786440 | tf_op jit(solution)/shard_map/ppermute | solution.py:49
  41.4 2.3 %collective-permute-start.12 = (bf16[64,2048]{1,0:T(8,128)(2,1)S(1)}, bf16[64,2048]{1,0:T(8,128)(2,1)S(1)}, u32[]{:S(2)}, u32[]{:S(2)}) collective-permute-start(bf16[64,2048]{1,0:T(8,128)(2,1)S(1)} %copy-done.19), channel_id=1, source_target_pairs={{0,7},{1,6},{2,5},{3,4},{4,3},{5,2},{6,1},{7,0},{8,15},{9,14},{10,... | collective-permute-start | bytes 786440 | tf_op jit(solution)/shard_map/ppermute | solution.py:49
  45.2 18.5 %student_logits.1 = (f32[2,512,2048]{2,1,0:T(8,128)}, f32[8,512]{1,0:T(8,128)S(1)}) custom-call(bf16[128,3072]{1,0:T(8,128)(2,1)} %refs_0_.3, bf16[128,3072]{1,0:T(8,128)(2,1)} %copy-done.7, bf16[128,3072]{1,0:T(8,128)(2,1)} %copy-done.8, bf16[128,3072]{1,0:T(8,128)(2,1)} %copy-done.9, bf16[2,3072,2048]{2,1,0:T(8,128)(2,1)S(1)} %take_pair.1.refs_4_.w_ref), custom_call_target="tpu_custom_call" | custom-call | flops 1 | bytes 1 | tf_op jit(solution)/shard_map/student_logits/pallas_call | solution.py:258
  71.9 3.3 %collective-permute-start.19 = (f32[8,512]{1,0:T(8,128)S(1)}, f32[8,512]{1,0:T(8,128)S(1)}, u32[]{:S(2)}, u32[]{:S(2)}) collective-permute-start(f32[8,512]{1,0:T(8,128)S(1)} %merge_two.4.a_ref), channel_id=1, source_target_pairs={{0,2},{1,3},{2,0},{3,1},{4,6},{5,7},{6,4},{7,5},{8,10},{9,11},{10,... | collective-permute-start | bytes 49160 | tf_op jit(solution)/shard_map/ppermute | solution.py:49
  78.6 3.1 %collective-permute-start.21 = (f32[8,512]{1,0:T(8,128)S(1)}, f32[8,512]{1,0:T(8,128)S(1)}, u32[]{:S(2)}, u32[]{:S(2)}) collective-permute-start(f32[8,512]{1,0:T(8,128)S(1)} %merge_two.5.a_ref), channel_id=1, source_target_pairs={{0,4},{1,5},{2,6},{3,7},{4,0},{5,1},{6,2},{7,3},{8,12},{9,13},{10,... | collective-permute-start | bytes 49160 | tf_op jit(solution)/shard_map/ppermute | solution.py:49
  85.8 2.0 %collective-permute-done.22.refs_10_ = bf16[192,2048]{1,0:T(8,128)(2,1)S(1)} collective-permute-done((bf16[192,2048]{1,0:T(8,128)(2,1)S(1)}, bf16[192,2048]{1,0:T(8,128)(2,1)S(1)}, u32[]{:S(2)}, u32[]{:S(2)}) %collective-permute-start.22) | collective-permute-done | bytes 786464 | tf_op jit(solution)/shard_map/ppermute | solution.py:49
  88.7 6.5 %logit_gradient.2 = (bf16[2,256,2048]{2,1,0:T(8,128)(2,1)}, f32[8,128]{1,0:T(8,128)S(1)}) custom-call(s32[19]{0:T(128)S(1)} %get-tuple-element.212.plan_ref, bf16[64,2048]{1,0:T(8,128)(2,1)} %get-tuple-element.146.refs_0_, bf16[64,2048]{1,0:T(8,128)(2,1)} %copy-done.15, bf16[64,2048]{1,0:T(8,128)(2,1)} %copy-done.16, bf16[64,2048]{1,0:T(8,128)(2,1)} %copy-done.17, ...), custom_call_target="tpu_custom_call" | custom-call | flops 4194304 | bytes 8388608 | tf_op jit(solution)/shard_map/logit_gradient/pallas_call | solution.py:426
  95.5 10.6 %hidden_share.1 = (f32[128,3072]{1,0:T(8,128)S(1)}, bf16[128,3072]{1,0:T(8,128)(2,1)S(1)}) custom-call(bf16[2,256,2048]{2,1,0:T(8,128)(2,1)} %get-tuple-element.197.given_ref.own_ref, bf16[2,3072,2048]{2,1,0:T(8,128)(2,1)} %copy-done), custom_call_target="tpu_custom_call" | custom-call | flops 6442450944 | bytes 25165824 | tf_op jit(solution)/shard_map/hidden_share/pallas_call | solution.py:504
  109.6 4.0 %collective-permute-start.27 = (bf16[16,3200]{1,0:T(8,128)(2,1)S(1)}, bf16[16,3200]{1,0:T(8,128)(2,1)S(1)}, u32[]{:S(2)}, u32[]{:S(2)}) collective-permute-start(bf16[16,3200]{1,0:T(8,128)(2,1)S(1)} %get-tuple-element.179), channel_id=1, source_target_pairs={{0,2},{1,3},{2,0},{3,1},{4,6},{5,7},{6,4},{7,5},{8,10},{9,11},{10,... | collective-permute-start | bytes 307208 | tf_op jit(solution)/shard_map/ppermute | solution.py:49
  113.5 3.0 %collective-permute-start.29 = (bf16[16,3200]{1,0:T(8,128)(2,1)S(1)}, bf16[16,3200]{1,0:T(8,128)(2,1)S(1)}, u32[]{:S(2)}, u32[]{:S(2)}) collective-permute-start(bf16[16,3200]{1,0:T(8,128)(2,1)S(1)} %get-tuple-element.181), channel_id=1, source_target_pairs={{0,4},{1,5},{2,6},{3,7},{4,0},{5,1},{6,2},{7,3},{8,12},{9,13},{10,... | collective-permute-start | bytes 307208 | tf_op jit(solution)/shard_map/ppermute | solution.py:49
  117.5 2.4 %collective-permute-start.31 = (bf16[16,3200]{1,0:T(8,128)(2,1)S(1)}, bf16[16,3200]{1,0:T(8,128)(2,1)S(1)}, u32[]{:S(2)}, u32[]{:S(2)}) collective-permute-start(bf16[16,3200]{1,0:T(8,128)(2,1)S(1)} %get-tuple-element.183), channel_id=1, source_target_pairs={{0,6},{1,7},{2,4},{3,5},{4,2},{5,3},{6,0},{7,1},{8,14},{9,15},{10,... | collective-permute-start | bytes 307208 | tf_op jit(solution)/shard_map/ppermute | solution.py:49
  121.3 6.8 %logit_gradient.3 = (bf16[2,256,2048]{2,1,0:T(8,128)(2,1)}, f32[8,128]{1,0:T(8,128)}) custom-call(s32[19]{0:T(128)S(1)} %get-tuple-element.211.plan_ref, bf16[64,2048]{1,0:T(8,128)(2,1)} %get-tuple-element.146.refs_0_, bf16[64,2048]{1,0:T(8,128)(2,1)} %copy-done.15, bf16[64,2048]{1,0:T(8,128)(2,1)} %copy-done.16, bf16[64,2048]{1,0:T(8,128)(2,1)} %copy-done.17, ...), custom_call_target="tpu_custom_call" | custom-call | flops 4194304 | bytes 8388608 | tf_op jit(solution)/shard_map/logit_gradient/pallas_call | solution.py:426
  128.1 3.9 %collective-permute-done.30 = bf16[16,3200]{1,0:T(8,128)(2,1)S(1)} collective-permute-done((bf16[16,3200]{1,0:T(8,128)(2,1)S(1)}, bf16[16,3200]{1,0:T(8,128)(2,1)S(1)}, u32[]{:S(2)}, u32[]{:S(2)}) %collective-permute-start.30) | collective-permute-done | bytes 102432 | tf_op jit(solution)/shard_map/ppermute | solution.py:49
  132.2 5.0 %collective-permute-start.34 = (bf16[16,3072]{1,0:T(8,128)(2,1)S(1)}, bf16[16,3072]{1,0:T(8,128)(2,1)S(1)}, u32[]{:S(2)}, u32[]{:S(2)}) collective-permute-start(bf16[16,3072]{1,0:T(8,128)(2,1)S(1)} %slice.13.refs_0_), channel_id=1, source_target_pairs={{0,4},{1,5},{2,6},{3,7},{4,0},{5,1},{6,2},{7,3},{8,12},{9,13},{10,... | collective-permute-start | bytes 294920 | tf_op jit(solution)/shard_map/ppermute | solution.py:49
  138.7 9.0 %head_pair.2.refs_0_ = bf16[768,1,4,2048]{3,2,1,0:T(4,128)(2,1)} custom-call(bf16[768,512]{1,0:T(8,128)(2,1)S(1)} %turn_features.1.left_ref, bf16[2,256,2048]{2,1,0:T(8,128)(2,1)} %get-tuple-element.197.given_ref.own_ref, bf16[2,256,2048]{2,1,0:T(8,128)(2,1)} %get-tuple-element.198.other_ref), custom_call_target="tpu_custom_call" | custom-call | flops 3221225472 | bytes 6291456 | tf_op jit(solution)/shard_map/head_pair/pallas_call | solution.py:694
  151.4 2.0 %collective-permute-start.39 = (f32[1]{0:T(128)}, f32[1]{0:T(128)}, u32[]{:S(2)}, u32[]{:S(2)}) collective-permute-start(f32[1]{0:T(128)} %bitcast.4), channel_id=1, source_target_pairs={{0,24},{8,16},{16,8},{24,0},{1,25},{9,17},{17,9},{25,1},{2,26},{10... | collective-permute-start | bytes 20 | tf_op jit(solution)/shard_map/ppermute | solution.py:49
  153.5 2.0 %collective-permute-start.38 = (f32[1]{0:T(128)}, f32[1]{0:T(128)}, u32[]{:S(2)}, u32[]{:S(2)}) collective-permute-start(f32[1]{0:T(128)} %bitcast.4), channel_id=1, source_target_pairs={{0,16},{8,24},{16,0},{24,8},{1,17},{9,25},{17,1},{25,9},{2,18},{10... | collective-permute-start | bytes 20 | tf_op jit(solution)/shard_map/ppermute | solution.py:49
  156.3 9.0 %head_pair.3 = bf16[768,1,4,2048]{3,2,1,0:T(4,128)(2,1)} custom-call(bf16[768,512]{1,0:T(8,128)(2,1)S(1)} %turn_features.1.left_ref, bf16[2,256,2048]{2,1,0:T(8,128)(2,1)} %copy-done.12, bf16[2,256,2048]{2,1,0:T(8,128)(2,1)} %copy-done.13, bf16[768,1,4,2048]{3,2,1,0:T(4,128)(2,1)} %head_pair.2.refs_0_), custom_call_target="tpu_custom_call", output_to_operand_aliasing={{}: (3, {})} | custom-call | flops 3221225472 | bytes 6291456 | tf_op jit(solution)/shard_map/head_pair/pallas_call | solution.py:694
  (125 shorter events, 36.7 us)
Async XLA Ops:
  1.1 23.7 %collective-permute-start.5 = (bf16[128,3072]{1,0:T(8,128)(2,1)}, bf16[128,3072]{1,0:T(8,128)(2,1)S(1)}, u32[]{:S(2)}, u32[]{:S(2)}) collective-permute-start(bf16[128,3072]{1,0:T(8,128)(2,1)} %refs_0_.3), channel_id=1, source_target_pairs={{0,16},{8,24},{16,0},{24,8},{1,17},{9,25},{17,1},{25,9},{2,18},{10... | collective-permute-start | bytes 2359304 | tf_op jit(solution)/shard_map/ppermute | solution.py:49
  8.3 17.2 %collective-permute-start.1 = (bf16[64,2048]{1,0:T(8,128)(2,1)}, bf16[64,2048]{1,0:T(8,128)(2,1)S(1)}, u32[]{:S(2)}, u32[]{:S(2)}) collective-permute-start(bf16[64,2048]{1,0:T(8,128)(2,1)} %get-tuple-element.115), channel_id=1, source_target_pairs={{0,1},{1,0},{2,3},{3,2},{4,5},{5,4},{6,7},{7,6},{8,9},{9,8},{10,11... | collective-permute-start | bytes 786440 | tf_op jit(solution)/shard_map/ppermute | solution.py:49
  9.8 15.6 %collective-permute-start.2 = (bf16[64,2048]{1,0:T(8,128)(2,1)}, bf16[64,2048]{1,0:T(8,128)(2,1)S(1)}, u32[]{:S(2)}, u32[]{:S(2)}) collective-permute-start(bf16[64,2048]{1,0:T(8,128)(2,1)} %get-tuple-element.116), channel_id=1, source_target_pairs={{0,2},{1,3},{2,0},{3,1},{4,6},{5,7},{6,4},{7,5},{8,10},{9,11},{10,... | collective-permute-start | bytes 786440 | tf_op jit(solution)/shard_map/ppermute | solution.py:49
  11.4 21.6 %collective-permute-start.3 = (bf16[64,2048]{1,0:T(8,128)(2,1)}, bf16[64,2048]{1,0:T(8,128)(2,1)S(1)}, u32[]{:S(2)}, u32[]{:S(2)}) collective-permute-start(bf16[64,2048]{1,0:T(8,128)(2,1)} %get-tuple-element.117), channel_id=1, source_target_pairs={{0,4},{1,5},{2,6},{3,7},{4,0},{5,1},{6,2},{7,3},{8,12},{9,13},{10,... | collective-permute-start | bytes 786440 | tf_op jit(solution)/shard_map/ppermute | solution.py:49
  14.0 23.2 %collective-permute-start.4 = (bf16[64,2048]{1,0:T(8,128)(2,1)}, bf16[64,2048]{1,0:T(8,128)(2,1)S(1)}, u32[]{:S(2)}, u32[]{:S(2)}) collective-permute-start(bf16[64,2048]{1,0:T(8,128)(2,1)} %get-tuple-element.118), channel_id=1, source_target_pairs={{0,5},{1,4},{2,7},{3,6},{4,1},{5,0},{6,3},{7,2},{8,13},{9,12},{10,... | collective-permute-start | bytes 786440 | tf_op jit(solution)/shard_map/ppermute | solution.py:49
  24.9 12.2 %collective-permute-start.6 = (bf16[64,2048]{1,0:T(8,128)(2,1)S(1)}, bf16[64,2048]{1,0:T(8,128)(2,1)S(1)}, u32[]{:S(2)}, u32[]{:S(2)}) collective-permute-start(bf16[64,2048]{1,0:T(8,128)(2,1)S(1)} %copy-done.14), channel_id=1, source_target_pairs={{0,16},{8,24},{16,0},{24,8},{1,17},{9,25},{17,1},{25,9},{2,18},{10... | collective-permute-start | bytes 786440 | tf_op jit(solution)/shard_map/ppermute | solution.py:49
  38.2 25.6 %collective-permute-start.9 = (bf16[256,2048]{1,0:T(8,128)(2,1)}, bf16[256,2048]{1,0:T(8,128)(2,1)S(1)}, u32[]{:S(2)}, u32[]{:S(2)}) collective-permute-start(bf16[256,2048]{1,0:T(8,128)(2,1)} %join.3.refs_4_), channel_id=1, source_target_pairs={{0,16},{8,24},{16,0},{24,8},{1,17},{9,25},{17,1},{25,9},{2,18},{10... | collective-permute-start | bytes 3145736 | tf_op jit(solution)/shard_map/ppermute | solution.py:49
  38.8 24.9 %collective-permute-start.10 = (bf16[64,2048]{1,0:T(8,128)(2,1)S(1)}, bf16[64,2048]{1,0:T(8,128)(2,1)S(1)}, u32[]{:S(2)}, u32[]{:S(2)}) collective-permute-start(bf16[64,2048]{1,0:T(8,128)(2,1)S(1)} %copy-done.21), channel_id=1, source_target_pairs={{0,3},{1,2},{2,1},{3,0},{4,7},{5,6},{6,5},{7,4},{8,11},{9,10},{10,... | collective-permute-start | bytes 786440 | tf_op jit(solution)/shard_map/ppermute | solution.py:49
  38.8 24.9 %collective-permute-start.11 = (bf16[64,2048]{1,0:T(8,128)(2,1)S(1)}, bf16[64,2048]{1,0:T(8,128)(2,1)S(1)}, u32[]{:S(2)}, u32[]{:S(2)}) collective-permute-start(bf16[64,2048]{1,0:T(8,128)(2,1)S(1)} %copy-done.20), channel_id=1, source_target_pairs={{0,6},{1,7},{2,4},{3,5},{4,2},{5,3},{6,0},{7,1},{8,14},{9,15},{10,... | collective-permute-start | bytes 786440 | tf_op jit(solution)/shard_map/ppermute | solution.py:49
  41.4 22.4 %collective-permute-start.12 = (bf16[64,2048]{1,0:T(8,128)(2,1)S(1)}, bf16[64,2048]{1,0:T(8,128)(2,1)S(1)}, u32[]{:S(2)}, u32[]{:S(2)}) collective-permute-start(bf16[64,2048]{1,0:T(8,128)(2,1)S(1)} %copy-done.19), channel_id=1, source_target_pairs={{0,7},{1,6},{2,5},{3,4},{4,3},{5,2},{6,1},{7,0},{8,15},{9,14},{10,... | collective-permute-start | bytes 786440 | tf_op jit(solution)/shard_map/ppermute | solution.py:49
  43.7 20.1 %collective-permute-start.14 = (f32[8,512]{1,0:T(8,128)S(1)}, f32[8,512]{1,0:T(8,128)S(1)}, u32[]{:S(2)}, u32[]{:S(2)}) collective-permute-start(f32[8,512]{1,0:T(8,128)S(1)} %get-tuple-element.141.refs_1_), channel_id=1, source_target_pairs={{0,16},{8,24},{16,0},{24,8},{1,17},{9,25},{17,1},{25,9},{2,18},{10... | collective-permute-start | bytes 49160 | tf_op jit(solution)/shard_map/ppermute | solution.py:49
  63.8 14.7 %collective-permute-start.15 = (bf16[256,2048]{1,0:T(8,128)(2,1)S(1)}, bf16[256,2048]{1,0:T(8,128)(2,1)S(1)}, u32[]{:S(2)}, u32[]{:S(2)}) collective-permute-start(bf16[256,2048]{1,0:T(8,128)(2,1)S(1)} %copy-done.2), channel_id=1, source_target_pairs={{0,8},{8,0},{16,24},{24,16},{1,9},{9,1},{17,25},{25,17},{2,10},{10... | collective-permute-start | bytes 3145736 | tf_op jit(solution)/shard_map/ppermute | solution.py:49
  63.9 14.6 %collective-permute-start.16 = (bf16[256,2048]{1,0:T(8,128)(2,1)S(1)}, bf16[256,2048]{1,0:T(8,128)(2,1)S(1)}, u32[]{:S(2)}, u32[]{:S(2)}) collective-permute-start(bf16[256,2048]{1,0:T(8,128)(2,1)S(1)} %collective-permute-done.9.refs_5_), channel_id=1, source_target_pairs={{0,8},{8,0},{16,24},{24,16},{1,9},{9,1},{17,25},{25,17},{2,10},{10... | collective-permute-start | bytes 3145736 | tf_op jit(solution)/shard_map/ppermute | solution.py:49
  65.4 19.8 %collective-permute-start.20 = (bf16[192,2048]{1,0:T(8,128)(2,1)}, bf16[192,2048]{1,0:T(8,128)(2,1)S(1)}, u32[]{:S(2)}, u32[]{:S(2)}) collective-permute-start(bf16[192,2048]{1,0:T(8,128)(2,1)} %join.4.refs_8_), channel_id=1, source_target_pairs={{0,16},{8,24},{16,0},{24,8},{1,17},{9,25},{17,1},{25,9},{2,18},{10... | collective-permute-start | bytes 2359304 | tf_op jit(solution)/shard_map/ppermute | solution.py:49
  95.3 13.4 %collective-permute-start.24 = (bf16[2,256,2048]{2,1,0:T(8,128)(2,1)}, bf16[2,256,2048]{2,1,0:T(8,128)(2,1)S(1)}, u32[]{:S(2)}, u32[]{:S(2)}) collective-permute-start(bf16[2,256,2048]{2,1,0:T(8,128)(2,1)} %get-tuple-element.197.given_ref.own_ref), channel_id=1, source_target_pairs={{0,8},{8,0},{16,24},{24,16},{1,9},{9,1},{17,25},{25,17},{2,10},{10... | collective-permute-start | bytes 6291464 | tf_op jit(solution)/shard_map/ppermute | solution.py:49
  113.5 14.6 %collective-permute-start.28 = (bf16[16,3200]{1,0:T(8,128)(2,1)S(1)}, bf16[16,3200]{1,0:T(8,128)(2,1)S(1)}, u32[]{:S(2)}, u32[]{:S(2)}) collective-permute-start(bf16[16,3200]{1,0:T(8,128)(2,1)S(1)} %get-tuple-element.180), channel_id=1, source_target_pairs={{0,3},{1,2},{2,1},{3,0},{4,7},{5,6},{6,5},{7,4},{8,11},{9,10},{10,... | collective-permute-start | bytes 307208 | tf_op jit(solution)/shard_map/ppermute | solution.py:49
  113.5 14.6 %collective-permute-start.29 = (bf16[16,3200]{1,0:T(8,128)(2,1)S(1)}, bf16[16,3200]{1,0:T(8,128)(2,1)S(1)}, u32[]{:S(2)}, u32[]{:S(2)}) collective-permute-start(bf16[16,3200]{1,0:T(8,128)(2,1)S(1)} %get-tuple-element.181), channel_id=1, source_target_pairs={{0,4},{1,5},{2,6},{3,7},{4,0},{5,1},{6,2},{7,3},{8,12},{9,13},{10,... | collective-permute-start | bytes 307208 | tf_op jit(solution)/shard_map/ppermute | solution.py:49
  116.5 15.5 %collective-permute-start.30 = (bf16[16,3200]{1,0:T(8,128)(2,1)S(1)}, bf16[16,3200]{1,0:T(8,128)(2,1)S(1)}, u32[]{:S(2)}, u32[]{:S(2)}) collective-permute-start(bf16[16,3200]{1,0:T(8,128)(2,1)S(1)} %get-tuple-element.182), channel_id=1, source_target_pairs={{0,5},{1,4},{2,7},{3,6},{4,1},{5,0},{6,3},{7,2},{8,13},{9,12},{10,... | collective-permute-start | bytes 307208 | tf_op jit(solution)/shard_map/ppermute | solution.py:49
  117.5 14.5 %collective-permute-start.31 = (bf16[16,3200]{1,0:T(8,128)(2,1)S(1)}, bf16[16,3200]{1,0:T(8,128)(2,1)S(1)}, u32[]{:S(2)}, u32[]{:S(2)}) collective-permute-start(bf16[16,3200]{1,0:T(8,128)(2,1)S(1)} %get-tuple-element.183), channel_id=1, source_target_pairs={{0,6},{1,7},{2,4},{3,5},{4,2},{5,3},{6,0},{7,1},{8,14},{9,15},{10,... | collective-permute-start | bytes 307208 | tf_op jit(solution)/shard_map/ppermute | solution.py:49
  132.0 17.0 %collective-permute-start.36 = (bf16[2,256,2048]{2,1,0:T(8,128)(2,1)}, bf16[2,256,2048]{2,1,0:T(8,128)(2,1)S(1)}, u32[]{:S(2)}, u32[]{:S(2)}) collective-permute-start(bf16[2,256,2048]{2,1,0:T(8,128)(2,1)} %get-tuple-element.198.other_ref), channel_id=1, source_target_pairs={{0,8},{8,0},{16,24},{24,16},{1,9},{9,1},{17,25},{25,17},{2,10},{10... | collective-permute-start | bytes 6291464 | tf_op jit(solution)/shard_map/ppermute | solution.py:49
  132.2 16.8 %collective-permute-start.34 = (bf16[16,3072]{1,0:T(8,128)(2,1)S(1)}, bf16[16,3072]{1,0:T(8,128)(2,1)S(1)}, u32[]{:S(2)}, u32[]{:S(2)}) collective-permute-start(bf16[16,3072]{1,0:T(8,128)(2,1)S(1)} %slice.13.refs_0_), channel_id=1, source_target_pairs={{0,4},{1,5},{2,6},{3,7},{4,0},{5,1},{6,2},{7,3},{8,12},{9,13},{10,... | collective-permute-start | bytes 294920 | tf_op jit(solution)/shard_map/ppermute | solution.py:49
  149.9 17.4 %collective-permute-start.40 = (bf16[64,3072]{1,0:T(8,128)(2,1)}, bf16[64,3072]{1,0:T(8,128)(2,1)S(1)}, u32[]{:S(2)}, u32[]{:S(2)}) collective-permute-start(bf16[64,3072]{1,0:T(8,128)(2,1)} %join.5.even_ref), channel_id=1, source_target_pairs={{0,1},{1,0},{2,3},{3,2},{4,5},{5,4},{6,7},{7,6},{8,9},{9,8},{10,11... | collective-permute-start | bytes 1179656 | tf_op jit(solution)/shard_map/ppermute | solution.py:49
  151.4 14.6 %collective-permute-start.39 = (f32[1]{0:T(128)}, f32[1]{0:T(128)}, u32[]{:S(2)}, u32[]{:S(2)}) collective-permute-start(f32[1]{0:T(128)} %bitcast.4), channel_id=1, source_target_pairs={{0,24},{8,16},{16,8},{24,0},{1,25},{9,17},{17,9},{25,1},{2,26},{10... | collective-permute-start | bytes 20 | tf_op jit(solution)/shard_map/ppermute | solution.py:49
  153.5 12.6 %collective-permute-start.38 = (f32[1]{0:T(128)}, f32[1]{0:T(128)}, u32[]{:S(2)}, u32[]{:S(2)}) collective-permute-start(f32[1]{0:T(128)} %bitcast.4), channel_id=1, source_target_pairs={{0,16},{8,24},{16,0},{24,8},{1,17},{9,25},{17,1},{25,9},{2,18},{10... | collective-permute-start | bytes 20 | tf_op jit(solution)/shard_map/ppermute | solution.py:49
  (39 other events, 433.2 us)
